TPU v7x, 32 devices: a whole 2x2x4 slice. The times are simulated.
32 devices in a mesh: grp: 2 (over x), ctx: 16 (over z, y, core).
Axes of the slice: x: 2, y: 2, z: 4, core: 2. Of those that a mesh axis runs over, the one named last changes fastest.
Arguments:
- queries: bfloat16 [4, 12, 64, 128], P(None, 'grp'), parts along dimension 1, may hold values from -150 to 150
- key_cache: bfloat16 [12, 8, 2048, 128], P('grp', None, 'ctx'), parts along dimension 0, may hold values from -6 to 6
- value_cache: bfloat16 [12, 8, 2048, 128], P('grp', None, 'ctx'), parts along dimension 0, may hold values from -6 to 6
- row_lengths: int32 [12], P('grp'), parts along dimension 0, may hold values from 128 to 2048, as said below
- kept_tiles: int32 [4, 12, 16], P(None, 'grp'), parts along dimension 1, may hold values from 0 to 1, as said below
- tile_dest: int32 [12, 8, 16], P('grp'), parts along dimension 0, may hold values from 0 to 15, as said below
Outputs:
- attn_out: bfloat16 [4, 12, 64, 128], P(None, 'grp'), parts along dimension 1
- tile_mass: float32 [12, 8, 16], P('grp', None, 'ctx'), parts along dimension 0
- moved_keys: bfloat16 [12, 8, 2048, 128], P('grp', None, 'ctx'), parts along dimension 0
- moved_values: bfloat16 [12, 8, 2048, 128], P('grp', None, 'ctx'), parts along dimension 0
There are 2 independent parts, one for each index of `grp`. A program takes and returns all parts, laid end to end along the dimension named above; each array names one. Nothing has to cross between parts.
Inputs may be any that keep to these rules, and one draw needn't show every extreme that they name: `row_lengths`: at least 128 positions of every row are filled; some row is filled to all 2048 positions. `kept_tiles`: A tile dropped at one step stays dropped at all later steps; tile 0 of every row is kept at every step. For each row and head, tile_dest is a permutation of the 16 tiles. The 1 tiles that one index of ctx holds for a row and head all go, in some order, to the index a per-row-and-head offset further along ctx, wrapping around; that offset is the same for every index. No offset is used by more than 3 row-head pairs, and some offset is used by exactly 3. The offsets 16 // 2 and 1 are used by some row-head pair in every draw.
All inputs are finite; a program needn't handle non-finite values.
Results may differ from a plain program's by a relative error of at most 0.0027.
Values may be sent and summed in bfloat16 or wider, within the bound.
No kernel may reach another device: no remote copies, remote signals or barrier semaphores. Data moves between devices by JAX's collectives and lax.ppermute only.
A program may use at most 64 MiB of HBM per device.

v0:
```python
import functools

import jax
import jax.numpy as jnp
from jax import lax
from jax.experimental import pallas as pl
from jax.experimental.pallas import tpu as pltpu
from jax.sharding import PartitionSpec as P

absent_score = -1e30
LANES = 128
F32 = jnp.float32
BF16 = jnp.bfloat16
VMEM = pl.BlockSpec(memory_space=pltpu.VMEM)
SMEM = pl.BlockSpec(memory_space=pltpu.SMEM)
HBM = pl.BlockSpec(memory_space=pltpu.HBM)
ANY = pl.BlockSpec(memory_space=pl.ANY)
PARAMS = pltpu.CompilerParams(vmem_limit_bytes=16 * 1024 * 1024)
WHOLE = pltpu.CompilerParams(vmem_limit_bytes=62 * 1024 * 1024)


COST = pl.CostEstimate(flops=1000, bytes_accessed=1000, transcendentals=0)


def stage_kernel(devices, group, me_ref, dest_hbm, k_ref, v_ref, buf, table, k_vm, v_vm, dest, counts, sem, load_sem):
    rows, heads = k_ref.shape[:2]
    small = pltpu.make_async_copy(dest_hbm, dest, sem.at[0])
    small.start()
    loads = []
    for row in range(rows):
        for which, (src, dst) in enumerate(((k_ref, k_vm), (v_ref, v_vm))):
            copy = pltpu.make_async_copy(src.at[row], dst.at[row], load_sem.at[which, row])
            copy.start()
            loads.append(copy)
    me = me_ref[0]

    def clear(i, carry):
        counts[i] = 0
        for k in range(group):
            table[i * group + k] = -1
        return carry

    lax.fori_loop(0, devices, clear, 0)
    small.wait()
    for row in range(rows):
        loads[2 * row].wait()
        loads[2 * row + 1].wait()

        def send(head, carry):
            offset = lax.rem(dest[row, head, 0], devices)
            rank = jnp.minimum(counts[offset], group - 1)
            counts[offset] = rank + 1
            table[offset * group + rank] = row * heads + head
            slot = lax.rem(me + offset, devices) * group + rank
            pltpu.make_async_copy(k_vm.at[row, head], buf.at[slot, 0], sem.at[1]).start()
            pltpu.make_async_copy(v_vm.at[row, head], buf.at[slot, 1], sem.at[2]).start()
            return carry

        lax.fori_loop(0, heads, send, 0)
    pltpu.make_async_copy(k_ref, k_vm, sem.at[1]).wait()
    pltpu.make_async_copy(v_ref, v_vm, sem.at[2]).wait()


def attend_kernel(
    levels,
    me_ref, table, len_hbm, kept_hbm, q_ref, k_ref, v_ref,
    stats_ref, *rest,
):
    chunks = rest[:levels // 2]
    len_ref, kept_ref, small_sem = rest[levels // 2:]
    rows, heads, tile, width = k_ref.shape
    steps, _, q_heads, _ = q_ref.shape
    per = q_heads // heads
    me = me_ref[0]

    small = [
        pltpu.make_async_copy(len_hbm, len_ref, small_sem.at[0]),
        pltpu.make_async_copy(kept_hbm, kept_ref, small_sem.at[1]),
    ]
    for copy in small:
        copy.start()
    for copy in small:
        copy.wait()

    lane = lax.broadcasted_iota(jnp.int32, (per, tile), 1)
    pair_lane = lax.broadcasted_iota(jnp.int32, (steps * per, LANES), 1)
    peaks = jnp.full((steps * per, LANES), absent_score, F32)
    totals = jnp.zeros((steps * per, LANES), F32)
    order = [jnp.bitwise_xor(place_of(me), level) for level in range(levels)]
    scale = width ** -0.5
    block = steps * per
    for row in range(rows):
        queries = [q_ref[step, row].astype(F32) for step in order]
        live = []
        for step in order:
            limit = jnp.where(kept_ref[row, step, me] > 0, len_ref[row] - me * tile, 0)
            live.append(lane < limit)
        live = jnp.concatenate(live * heads, axis=0)
        scores = []
        for head in range(heads):
            q = jnp.concatenate([x[head * per:(head + 1) * per] for x in queries], axis=0).astype(BF16)
            scores.append(lax.dot_general(
                q, k_ref[row, head], (((1,), (1,)), ((), ())), preferred_element_type=F32
            ))
        scores = jnp.concatenate(scores, axis=0) * scale
        peak = jnp.max(jnp.where(live, scores, absent_score), axis=1, keepdims=True)
        weights = jnp.where(live, jnp.exp(scores - peak), 0.0)
        total = jnp.sum(weights, axis=1, keepdims=True)
        rounded = weights.astype(BF16)
        for head in range(heads):
            out = jnp.dot(
                rounded[head * block:(head + 1) * block], v_ref[row, head], preferred_element_type=F32
            )
            pair = row * heads + head
            for i in range(levels):
                chunks[i // 2][i % 2, pair * per:(pair + 1) * per, :] = out[i * per:(i + 1) * per]
            here = pair_lane == pair
            peaks = jnp.where(here, peak[head * block:(head + 1) * block], peaks)
            totals = jnp.where(here, total[head * block:(head + 1) * block], totals)
    base = rows * q_heads
    for i in range(levels):
        chunks[i // 2][i % 2, base:base + per, :] = peaks[i * per:(i + 1) * per]
        chunks[i // 2][i % 2, base + per:base + 2 * per, :] = totals[i * per:(i + 1) * per]
    stats_ref[0] = peaks
    stats_ref[1] = totals


def place_of(me):
    return lax.rem(me, 2) * 2 + lax.rem(me // 2, 2)


def merge(swap, own, got, pairs, per, own_stats=None, got_stats=None):
    def both(rows, own=own, got=got):
        x, y = own[rows, :], got[rows, :]
        return jnp.where(swap, y, x), jnp.where(swap, x, y)

    scaled = own_stats is not None
    base = 0 if scaled else pairs * per
    stats = (own_stats, got_stats) if scaled else (own, got)
    peaks = both(slice(base, base + per), *stats)
    totals = both(slice(base + per, base + 2 * per), *stats)
    peak = jnp.maximum(*peaks)
    factors = [jnp.exp(x - peak) for x in peaks]
    total = factors[0] * totals[0] + factors[1] * totals[1]
    if scaled:
        scales = both(slice(2 * per, 3 * per), *stats)
        factors = [f * x for f, x in zip(factors, scales)]

    def summed(pair):
        first, second = [jnp.broadcast_to(f[:, pair:pair + 1], (per, LANES)) for f in factors]
        x, y = both(slice(pair * per, (pair + 1) * per))
        return first * x + second * y

    return peak, total, summed


def merge_kernel(bit, pairs, per, me_ref, own, got, *outs):
    swap = lax.rem(me_ref[0] // bit, 2) == 1
    base = pairs * per
    for i, out in enumerate(outs):
        x, y = (own, got) if len(outs) == 1 else (own.at[i], got.at[i])
        peak, total, summed = merge(swap, x, y, pairs, per)
        for pair in range(pairs):
            out[pair * per:(pair + 1) * per, :] = summed(pair)
        out[base:base + per, :] = peak
        out[base + per:base + 2 * per, :] = total


def scale_kernel(pairs, per, block, sums, stats):
    lane = lax.broadcasted_iota(jnp.int32, (per, LANES), 1)
    base = pairs * per
    scales = jnp.ones((per, LANES), F32)
    for pair in range(pairs):
        x = block[pair * per:(pair + 1) * per, :]
        largest = jnp.max(jnp.abs(x), axis=1, keepdims=True)
        largest = jnp.where(largest > 0.0, largest, 1.0)
        sums[pair * per:(pair + 1) * per, :] = x / largest
        scales = jnp.where(lane == pair, largest, scales)
    stats[:2 * per, :] = block[base:base + 2 * per, :]
    stats[2 * per:, :] = scales


def last_kernel(bit, pairs, per, me_ref, own, got, own_stats, got_stats, out):
    swap = lax.rem(me_ref[0] // bit, 2) == 1
    base = pairs * per
    peak, total, summed = merge(swap, own, got, pairs, per, own_stats, got_stats)
    lane = lax.broadcasted_iota(jnp.int32, peak.shape, 1)
    total = jnp.where(lane < pairs, total, 1.0)
    peak = jnp.where(lane < pairs, peak, 0.0)

    def result(pair):
        return summed(pair) / jnp.broadcast_to(total[:, pair:pair + 1], (per, LANES))

    for pair in range(0, pairs, 2):
        both = jnp.concatenate([result(pair), result(pair + 1)], axis=0)
        out[pair * per:(pair + 2) * per, :] = both.astype(BF16)
    rest = jnp.concatenate([peak, total], axis=0)
    lane = lax.broadcasted_iota(jnp.int32, rest.shape, 1)
    parts = []
    for i in range(3):
        parts.append(rest.astype(BF16).astype(F32))
        rest = rest - parts[i]
    half = LANES // 2
    packed = jnp.where(lane < half, parts[0], pltpu.roll(parts[1], half, 1))
    out[base:base + 2 * per, :] = packed.astype(BF16)
    out[base + 2 * per:base + 4 * per, :] = parts[2].astype(BF16)


def pass_kernel(me_ref, x, out):
    out[...] = x[...]


def finish_kernel(pairs, per, heads, levels, me_ref, stats_ref, *refs):
    ins, out, mass_ref = refs[:levels], refs[levels], refs[levels + 1]
    base = pairs * per
    lane = lax.broadcasted_iota(jnp.int32, (2 * per, LANES), 1)
    mass = jnp.zeros((per, LANES), F32)
    for level in range(levels):
        step = jnp.bitwise_xor(place_of(me_ref[0]), level)
        out[step] = ins[level][:base, :]
        packed = ins[level][base:base + 2 * per, :].astype(F32)
        third = ins[level][base + 2 * per:base + 4 * per, :].astype(F32)
        both = third + pltpu.roll(packed, LANES // 2, 1) + packed
        both = jnp.where(lane < pairs, both, 1.0)
        at = level * per
        coefficient = jnp.exp(jnp.minimum(stats_ref[0, at:at + per, :] - both[:per], 0.0)) / both[per:]
        mass = mass + stats_ref[1, at:at + per, :] * coefficient
    mass = jnp.sum(mass, axis=0, keepdims=True)
    for row in range(pairs // heads):
        mass_ref[row] = mass[:, row * heads:(row + 1) * heads]


def place_kernel(devices, group, me_ref, table, got_ref, k_ref, v_ref, me_out, sem):
    heads = k_ref.shape[1]
    me = me_ref[0]
    me_out[0] = me
    for offset in range(devices):
        source = lax.rem(me + devices - offset, devices)
        for k in range(group):
            pair = table[offset * group + k]

            @pl.when(pair >= 0)
            def _():
                row, head = pair // heads, lax.rem(pair, heads)
                for which, ref in enumerate((k_ref, v_ref)):
                    src = got_ref.at[source * group + k, which]
                    pltpu.make_async_copy(src, ref.at[row, head], sem.at[which]).start()
    pltpu.make_async_copy(k_ref, k_ref, sem.at[0]).wait()
    pltpu.make_async_copy(v_ref, v_ref, sem.at[1]).wait()


def local(queries, key_cache, value_cache, row_lengths, kept_tiles, tile_dest):
    devices = lax.axis_size("ctx")
    rows, heads, span, width = key_cache.shape
    steps, _, q_heads, _ = queries.shape
    per = q_heads // heads
    pairs = rows * heads
    group = -(-pairs // devices)
    levels = 4
    assert steps == levels and tile_dest.shape[2] == devices and pairs % 2 == 0 and pairs <= LANES // 2
    assert devices > levels and devices & (devices - 1) == 0 and width == LANES

    me = lax.axis_index("ctx").astype(jnp.int32).reshape(1)
    kept = jnp.transpose(kept_tiles, (1, 0, 2))
    block_rows = rows * q_heads + 2 * per
    block_type = jax.ShapeDtypeStruct((block_rows, width), F32)
    message_type = jax.ShapeDtypeStruct((rows * q_heads + 4 * per, width), BF16)
    tiles_type = jax.ShapeDtypeStruct((devices * group, 2, span, width), BF16)

    tiles_out, table = pl.pallas_call(
        functools.partial(stage_kernel, devices, group),
        out_shape=[tiles_type, jax.ShapeDtypeStruct((devices * group,), jnp.int32)],
        in_specs=[SMEM, HBM, HBM, HBM],
        out_specs=[HBM, SMEM],
        scratch_shapes=[
            pltpu.VMEM(key_cache.shape, BF16),
            pltpu.VMEM(value_cache.shape, BF16),
            pltpu.SMEM(tile_dest.shape, jnp.int32),
            pltpu.SMEM((devices,), jnp.int32),
            pltpu.SemaphoreType.DMA((3,)),
            pltpu.SemaphoreType.DMA((2, rows)),
        ],
        compiler_params=WHOLE,
        cost_estimate=COST,
        name="stage",
    )(me, tile_dest, key_cache, value_cache)
    tiles_in = lax.all_to_all(tiles_out, "ctx", split_axis=0, concat_axis=0, tiled=True)

    stats, *chunks = pl.pallas_call(
        functools.partial(attend_kernel, levels),
        out_shape=[
            jax.ShapeDtypeStruct((2, steps * per, LANES), F32),
        ] + [jax.ShapeDtypeStruct((2, block_rows, width), F32)] * 2,
        in_specs=[SMEM, SMEM, HBM, HBM, VMEM, VMEM, VMEM],
        out_specs=[VMEM] * 3,
        scratch_shapes=[
            pltpu.SMEM(row_lengths.shape, jnp.int32),
            pltpu.SMEM(kept.shape, jnp.int32),
            pltpu.SemaphoreType.DMA((2,)),
        ],
        compiler_params=PARAMS,
        cost_estimate=COST,
        name="attend",
    )(me, table, row_lengths, kept, queries, key_cache, value_cache)

    def flip(x, bit):
        return lax.ppermute(x, "ctx", [(i, i ^ bit) for i in range(devices)])

    def local_call(kernel, name, out_shape, *operands):
        return pl.pallas_call(
            kernel,
            out_shape=out_shape,
            in_specs=[SMEM if x is me or x.shape == (1,) else VMEM for x in operands],
            out_specs=[VMEM] * len(out_shape),
            compiler_params=PARAMS,
            cost_estimate=COST,
            name=name,
        )(*operands)

    def merged(name, bit, own, got, out_shape):
        return local_call(functools.partial(merge_kernel, bit, pairs, per), name, out_shape, me, own, got)

    block, sent = merged("core", 1, chunks[0], flip(chunks[1], 1), [block_type] * 2)
    block, = merged("near", 2, block, flip(sent, 2), [block_type])
    bit = levels
    while 2 * bit < devices:
        block, = merged("far", bit, block, flip(block, bit), [block_type])
        bit *= 2
    sums_type = jax.ShapeDtypeStruct((rows * q_heads, width), F32)
    stats_type = jax.ShapeDtypeStruct((3 * per, width), F32)
    sums, sum_stats = local_call(functools.partial(scale_kernel, pairs, per), "scale", [sums_type, stats_type], block)
    sums = lax.reduce_precision(sums, 5, 10)
    got = flip(sums.astype(jnp.float16), bit).astype(F32)
    message, = local_call(
        functools.partial(last_kernel, bit, pairs, per), "last", [message_type],
        me, sums, got, sum_stats, flip(sum_stats, bit),
    )
    other = flip(message, 2)

    moved_keys, moved_values, me_next = pl.pallas_call(
        functools.partial(place_kernel, devices, group),
        out_shape=[
            jax.ShapeDtypeStruct(key_cache.shape, BF16),
            jax.ShapeDtypeStruct(value_cache.shape, BF16),
            jax.ShapeDtypeStruct((1,), jnp.int32),
        ],
        in_specs=[SMEM, SMEM, ANY],
        out_specs=[HBM, HBM, SMEM],
        scratch_shapes=[pltpu.SemaphoreType.DMA((2,))],
        compiler_params=PARAMS,
        cost_estimate=COST,
        name="place",
    )(me, table, tiles_in)

    other_next, = local_call(pass_kernel, "pass", [message_type], me_next, other)
    arrived = [message, other, flip(message, 1), flip(other_next, 1)]

    attn_out, mass = pl.pallas_call(
        functools.partial(finish_kernel, pairs, per, heads, levels),
        out_shape=[
            jax.ShapeDtypeStruct((steps, rows * q_heads, width), BF16),
            jax.ShapeDtypeStruct((rows, 1, heads), F32),
        ],
        in_specs=[SMEM, VMEM] + [VMEM] * levels,
        out_specs=[VMEM, VMEM],
        compiler_params=PARAMS,
        cost_estimate=COST,
        name="finish",
    )(me_next, stats, *arrived)
    return attn_out.reshape(queries.shape), jnp.transpose(mass, (0, 2, 1)), moved_keys, moved_values


def solution(mesh):
    in_specs = (
        P(None, "grp", None, None),
        P("grp", None, "ctx", None),
        P("grp", None, "ctx", None),
        P("grp"),
        P(None, "grp", None),
        P("grp", None, None),
    )
    out_specs = (
        P(None, "grp", None, None),
        P("grp", None, "ctx"),
        P("grp", None, "ctx", None),
        P("grp", None, "ctx", None),
    )
    return jax.shard_map(local, mesh=mesh, in_specs=in_specs, out_specs=out_specs, check_vma=False)
```

profile of v0, /device:TPU:0, one launch (start us, length us, event | category | flops | bytes accessed | tf_op | source)
XLA Modules:
  0.0 96.6 jit_solution(9519567669335569920)
XLA Ops:
  0.6 3.5 %stage.1 = (bf16[48,2,128,128]{3,2,1,0:T(8,128)(2,1)}, s32[48]{0:T(128)}) custom-call(s32[1]{0:T(128)} %bitcast.me_ref, s32[6,8,16]{2,1,0:T(8,128)} %dest_hbm.1, bf16[6,8,128,128]{3,2,1,0:T(8,128)(2,1)} %k_ref.3, bf16[6,8,128,128]{3,2,1,0:T(8,128)(2,1)} %v_ref.3), custom_call_target="tpu_custom_call" | custom-call | flops 1000 | bytes 1000 | tf_op jit(solution)/shard_map/stage/pallas_call | solution.py:270
  4.1 0.0 copy-start.2
  4.1 0.0 copy-start.5
  4.2 0.0 copy-start.6
  4.2 7.5 %all-to-all-start = ((bf16[48,2,128,128]{3,2,1,0:T(8,128)(2,1)}), bf16[48,2,128,128]{3,2,1,0:T(8,128)(2,1)S(1)}, u32[]{:S(2)}, u32[]{:S(2)}) async-start(bf16[48,2,128,128]{3,2,1,0:T(8,128)(2,1)} %get-tuple-element.19), calls=%async_computation | async-start | bytes 6291456 | tf_op jit(solution)/shard_map/all_to_all | solution.py:287
  11.7 0.0 copy-done.2
  11.7 0.0 copy-done.5
  11.7 0.0 copy-done.6
  11.7 0.0 copy-start
  11.7 1.4 %copy-done = bf16[6,8,128,128]{3,2,1,0:T(8,128)(2,1)S(1)} copy-done((bf16[6,8,128,128]{3,2,1,0:T(8,128)(2,1)S(1)}, bf16[6,8,128,128]{3,2,1,0:T(8,128)(2,1)}, u32[]{:S(2)}) %copy-start) | copy-done | bytes 1572888
  13.1 0.0 copy-start.1
  13.1 1.4 %copy-done.1 = bf16[6,8,128,128]{3,2,1,0:T(8,128)(2,1)S(1)} copy-done((bf16[6,8,128,128]{3,2,1,0:T(8,128)(2,1)S(1)}, bf16[6,8,128,128]{3,2,1,0:T(8,128)(2,1)}, u32[]{:S(2)}) %copy-start.1) | copy-done | bytes 1572888
  14.6 0.0 copy-start.7
  14.6 0.7 copy-done.7
  15.2 3.5 %attend.1 = (f32[2,32,128]{2,1,0:T(8,128)S(1)}, f32[2,400,128]{2,1,0:T(8,128)S(1)}, f32[2,400,128]{2,1,0:T(8,128)S(1)}) custom-call(s32[1]{0:T(128)} %bitcast.me_ref, s32[48]{0:T(128)S(1)} %copy-done.6, s32[6]{0:T(128)S(1)} %copy-done.7, s32[6,4,16]{2,1,0:T(4,128)S(1)} %bitcast.4, bf16[4,6,64,128]{3,2,1,0:T(8,128)(2,1)S(1)} %copy-done.2, ...), custom_call_target="tpu_custom_call" | custom-call | flops 1000 | bytes 1000 | tf_op jit(solution)/shard_map/attend/pallas_call | solution.py:289
  18.7 0.0 copy-start.3
  18.7 0.5 collective-permute-start
  19.2 1.4 %collective-permute-done.got = f32[2,400,128]{2,1,0:T(8,128)S(1)} collective-permute-done((f32[2,400,128]{2,1,0:T(8,128)S(1)}, f32[2,400,128]{2,1,0:T(8,128)S(1)}, u32[]{:S(2)}, u32[]{:S(2)}) %collective-permute-start) | collective-permute-done | bytes 409632 | tf_op jit(solution)/shard_map/ppermute | solution.py:307
  20.5 0.4 core.1
  20.9 2.0 %collective-permute-start.1 = (f32[400,128]{1,0:T(8,128)S(1)}, f32[400,128]{1,0:T(8,128)S(1)}, u32[]{:S(2)}, u32[]{:S(2)}) collective-permute-start(f32[400,128]{1,0:T(8,128)S(1)} %get-tuple-element.25), channel_id=1, source_target_pairs={{0,2},{1,3},{2,0},{3,1},{4,6},{5,7},{6,4},{7,5},{8,10},{9,11},{10,... | collective-permute-start | bytes 614408 | tf_op jit(solution)/shard_map/ppermute | solution.py:307
  22.9 14.2 %collective-permute-done.1.got = f32[400,128]{1,0:T(8,128)S(1)} collective-permute-done((f32[400,128]{1,0:T(8,128)S(1)}, f32[400,128]{1,0:T(8,128)S(1)}, u32[]{:S(2)}, u32[]{:S(2)}) %collective-permute-start.1) | collective-permute-done | bytes 204832 | tf_op jit(solution)/shard_map/ppermute | solution.py:307
  37.1 0.2 near.1.own
  37.3 0.1 collective-permute-start.2
  37.4 30.5 %collective-permute-done.2.got = f32[400,128]{1,0:T(8,128)S(1)} collective-permute-done((f32[400,128]{1,0:T(8,128)S(1)}, f32[400,128]{1,0:T(8,128)S(1)}, u32[]{:S(2)}, u32[]{:S(2)}) %collective-permute-start.2) | collective-permute-done | bytes 204832 | tf_op jit(solution)/shard_map/ppermute | solution.py:307
  67.9 0.2 far.1.block
  68.1 0.1 scale.1
  68.3 0.1 reduce-precision_convert_fusion
  68.4 4.6 %collective-permute-start.3 = (f16[384,128]{1,0:T(8,128)(2,1)S(1)}, f16[384,128]{1,0:T(8,128)(2,1)S(1)}, u32[]{:S(2)}, u32[]{:S(2)}) collective-permute-start(f16[384,128]{1,0:T(8,128)(2,1)S(1)} %get-tuple-element.32), channel_id=1, source_target_pairs={{0,8},{1,9},{2,10},{3,11},{4,12},{5,13},{6,14},{7,15},{8,0},{9,1},... | collective-permute-start | bytes 294920 | tf_op jit(solution)/shard_map/ppermute | solution.py:307
  72.9 0.1 collective-permute-start.4
  73.0 14.9 %collective-permute-done.3 = f16[384,128]{1,0:T(8,128)(2,1)S(1)} collective-permute-done((f16[384,128]{1,0:T(8,128)(2,1)S(1)}, f16[384,128]{1,0:T(8,128)(2,1)S(1)}, u32[]{:S(2)}, u32[]{:S(2)}) %collective-permute-start.3) | collective-permute-done | bytes 98336 | tf_op jit(solution)/shard_map/ppermute | solution.py:307
  87.9 0.1 collective-permute-done.4.got_stats
  88.0 0.3 last.1.refs_0_
  88.3 0.0 copy-done.3
  88.4 1.6 %collective-permute-start.5 = (bf16[416,128]{1,0:T(8,128)(2,1)S(1)}, bf16[416,128]{1,0:T(8,128)(2,1)S(1)}, u32[]{:S(2)}, u32[]{:S(2)}) collective-permute-start(bf16[416,128]{1,0:T(8,128)(2,1)S(1)} %last.1.refs_0_), channel_id=1, source_target_pairs={{0,2},{1,3},{2,0},{3,1},{4,6},{5,7},{6,4},{7,5},{8,10},{9,11},{10,... | collective-permute-start | bytes 319496 | tf_op jit(solution)/shard_map/ppermute | solution.py:307
  89.9 0.0 copy-start.4
  89.9 0.0 collective-permute-start.6
  89.9 0.0 all-to-all-done.got_ref
  89.9 2.7 %place.1 = (bf16[6,8,128,128]{3,2,1,0:T(8,128)(2,1)}, bf16[6,8,128,128]{3,2,1,0:T(8,128)(2,1)}, s32[1]{0:T(128)}) custom-call(s32[1]{0:T(128)} %bitcast.me_ref, s32[48]{0:T(128)S(1)} %copy-done.6, bf16[48,2,128,128]{3,2,1,0:T(8,128)(2,1)S(1)} %all-to-all-done.got_ref), custom_call_target="tpu_custom_call" | custom-call | flops 1000 | bytes 1000 | tf_op jit(solution)/shard_map/place/pallas_call | solution.py:340
  92.6 0.5 collective-permute-done.5.x.refs_1_
  93.1 0.6 pass.1
  93.8 0.1 collective-permute-start.7
  93.9 0.0 collective-permute-done.6.refs_2_
  93.9 1.3 %collective-permute-done.7.refs_3_ = bf16[416,128]{1,0:T(8,128)(2,1)S(1)} collective-permute-done((bf16[416,128]{1,0:T(8,128)(2,1)S(1)}, bf16[416,128]{1,0:T(8,128)(2,1)S(1)}, u32[]{:S(2)}, u32[]{:S(2)}) %collective-permute-start.7) | collective-permute-done | bytes 106528 | tf_op jit(solution)/shard_map/ppermute | solution.py:307
  95.1 0.0 copy-done.4
  95.1 1.5 %finish.1 = (bf16[4,384,128]{2,1,0:T(8,128)(2,1)}, f32[6,1,8]{2,1,0:T(1,128)}) custom-call(s32[1]{0:T(128)} %get-tuple-element.20.me_ref, f32[2,32,128]{2,1,0:T(8,128)S(1)} %copy-done.4, bf16[416,128]{1,0:T(8,128)(2,1)S(1)} %last.1.refs_0_, bf16[416,128]{1,0:T(8,128)(2,1)S(1)} %collective-permute-done.5.x.refs_1_, ...), custom_call_target="tpu_custom_call" | custom-call | flops 1000 | bytes 1000 | tf_op jit(solution)/shard_map/finish/pallas_call | solution.py:358
  (1 shorter events, 0.0 us)
Async XLA Ops:
  4.1 7.6 %copy-start.2 = (bf16[4,6,64,128]{3,2,1,0:T(8,128)(2,1)S(1)}, bf16[4,6,64,128]{3,2,1,0:T(8,128)(2,1)}, u32[]{:S(2)}) copy-start(bf16[4,6,64,128]{3,2,1,0:T(8,128)(2,1)} %q_ref.1) | copy-start | bytes 1179652
  4.1 7.6 %copy-start.5 = (s32[4,6,16]{2,0,1:T(4,128)S(1)}, s32[4,6,16]{2,0,1:T(4,128)}, u32[]{:S(2)}) copy-start(s32[4,6,16]{2,0,1:T(4,128)} %param.10) | copy-start | bytes 4612
  4.2 7.6 %copy-start.6 = (s32[48]{0:T(128)S(1)}, s32[48]{0:T(128)}, u32[]{:S(2)}) copy-start(s32[48]{0:T(128)} %get-tuple-element.18.table) | copy-start | bytes 580
  4.2 85.8 %all-to-all-start = ((bf16[48,2,128,128]{3,2,1,0:T(8,128)(2,1)}), bf16[48,2,128,128]{3,2,1,0:T(8,128)(2,1)S(1)}, u32[]{:S(2)}, u32[]{:S(2)}) async-start(bf16[48,2,128,128]{3,2,1,0:T(8,128)(2,1)} %get-tuple-element.19), calls=%async_computation | async-start | bytes 6291456 | tf_op jit(solution)/shard_map/all_to_all | solution.py:287
  11.7 1.4 %copy-start = (bf16[6,8,128,128]{3,2,1,0:T(8,128)(2,1)S(1)}, bf16[6,8,128,128]{3,2,1,0:T(8,128)(2,1)}, u32[]{:S(2)}) copy-start(bf16[6,8,128,128]{3,2,1,0:T(8,128)(2,1)} %k_ref.3) | copy-start | bytes 4718596
  13.1 1.4 %copy-start.1 = (bf16[6,8,128,128]{3,2,1,0:T(8,128)(2,1)S(1)}, bf16[6,8,128,128]{3,2,1,0:T(8,128)(2,1)}, u32[]{:S(2)}) copy-start(bf16[6,8,128,128]{3,2,1,0:T(8,128)(2,1)} %v_ref.3) | copy-start | bytes 4718596
  14.6 0.7 copy-start.7
  18.7 69.7 %copy-start.3 = (f32[2,32,128]{2,1,0:T(8,128)}, f32[2,32,128]{2,1,0:T(8,128)S(1)}, u32[]{:S(2)}) copy-start(f32[2,32,128]{2,1,0:T(8,128)S(1)} %get-tuple-element.21.stats_ref) | copy-start | bytes 98308
  18.7 1.8 %collective-permute-start = (f32[2,400,128]{2,1,0:T(8,128)S(1)}, f32[2,400,128]{2,1,0:T(8,128)S(1)}, u32[]{:S(2)}, u32[]{:S(2)}) collective-permute-start(f32[2,400,128]{2,1,0:T(8,128)S(1)} %get-tuple-element.23), channel_id=1, source_target_pairs={{0,1},{1,0},{2,3},{3,2},{4,5},{5,4},{6,7},{7,6},{8,9},{9,8},{10,11... | collective-permute-start | bytes 1228808 | tf_op jit(solution)/shard_map/ppermute | solution.py:307
  20.9 16.1 %collective-permute-start.1 = (f32[400,128]{1,0:T(8,128)S(1)}, f32[400,128]{1,0:T(8,128)S(1)}, u32[]{:S(2)}, u32[]{:S(2)}) collective-permute-start(f32[400,128]{1,0:T(8,128)S(1)} %get-tuple-element.25), channel_id=1, source_target_pairs={{0,2},{1,3},{2,0},{3,1},{4,6},{5,7},{6,4},{7,5},{8,10},{9,11},{10,... | collective-permute-start | bytes 614408 | tf_op jit(solution)/shard_map/ppermute | solution.py:307
  37.3 30.6 %collective-permute-start.2 = (f32[400,128]{1,0:T(8,128)S(1)}, f32[400,128]{1,0:T(8,128)S(1)}, u32[]{:S(2)}, u32[]{:S(2)}) collective-permute-start(f32[400,128]{1,0:T(8,128)S(1)} %near.1.own), channel_id=1, source_target_pairs={{0,4},{1,5},{2,6},{3,7},{4,0},{5,1},{6,2},{7,3},{8,12},{9,13},{10,... | collective-permute-start | bytes 614408 | tf_op jit(solution)/shard_map/ppermute | solution.py:307
  68.4 19.5 %collective-permute-start.3 = (f16[384,128]{1,0:T(8,128)(2,1)S(1)}, f16[384,128]{1,0:T(8,128)(2,1)S(1)}, u32[]{:S(2)}, u32[]{:S(2)}) collective-permute-start(f16[384,128]{1,0:T(8,128)(2,1)S(1)} %get-tuple-element.32), channel_id=1, source_target_pairs={{0,8},{1,9},{2,10},{3,11},{4,12},{5,13},{6,14},{7,15},{8,0},{9,1},... | collective-permute-start | bytes 294920 | tf_op jit(solution)/shard_map/ppermute | solution.py:307
  72.9 15.1 %collective-permute-start.4 = (f32[24,128]{1,0:T(8,128)S(1)}, f32[24,128]{1,0:T(8,128)S(1)}, u32[]{:S(2)}, u32[]{:S(2)}) collective-permute-start(f32[24,128]{1,0:T(8,128)S(1)} %get-tuple-element.27.own_stats), channel_id=1, source_target_pairs={{0,8},{1,9},{2,10},{3,11},{4,12},{5,13},{6,14},{7,15},{8,0},{9,1},... | collective-permute-start | bytes 36872 | tf_op jit(solution)/shard_map/ppermute | solution.py:307
  88.4 4.8 %collective-permute-start.5 = (bf16[416,128]{1,0:T(8,128)(2,1)S(1)}, bf16[416,128]{1,0:T(8,128)(2,1)S(1)}, u32[]{:S(2)}, u32[]{:S(2)}) collective-permute-start(bf16[416,128]{1,0:T(8,128)(2,1)S(1)} %last.1.refs_0_), channel_id=1, source_target_pairs={{0,2},{1,3},{2,0},{3,1},{4,6},{5,7},{6,4},{7,5},{8,10},{9,11},{10,... | collective-permute-start | bytes 319496 | tf_op jit(solution)/shard_map/ppermute | solution.py:307
  89.9 5.2 %copy-start.4 = (f32[2,32,128]{2,1,0:T(8,128)S(1)}, f32[2,32,128]{2,1,0:T(8,128)}, u32[]{:S(2)}) copy-start(f32[2,32,128]{2,1,0:T(8,128)} %copy-done.3) | copy-start | bytes 98308
  89.9 3.9 %collective-permute-start.6 = (bf16[416,128]{1,0:T(8,128)(2,1)S(1)}, bf16[416,128]{1,0:T(8,128)(2,1)S(1)}, u32[]{:S(2)}, u32[]{:S(2)}) collective-permute-start(bf16[416,128]{1,0:T(8,128)(2,1)S(1)} %last.1.refs_0_), channel_id=1, source_target_pairs={{0,1},{1,0},{2,3},{3,2},{4,5},{5,4},{6,7},{7,6},{8,9},{9,8},{10,11... | collective-permute-start | bytes 319496 | tf_op jit(solution)/shard_map/ppermute | solution.py:307
  93.8 1.4 %collective-permute-start.7 = (bf16[416,128]{1,0:T(8,128)(2,1)S(1)}, bf16[416,128]{1,0:T(8,128)(2,1)S(1)}, u32[]{:S(2)}, u32[]{:S(2)}) collective-permute-start(bf16[416,128]{1,0:T(8,128)(2,1)S(1)} %pass.1), channel_id=1, source_target_pairs={{0,1},{1,0},{2,3},{3,2},{4,5},{5,4},{6,7},{7,6},{8,9},{9,8},{10,11... | collective-permute-start | bytes 319496 | tf_op jit(solution)/shard_map/ppermute | solution.py:307
where the time goes:
time: 96.9 us; the launch traced here: 96.6 us
  waiting for transfers between devices  62.8 us (65%)
  starting transfers between devices  16.3 us (17%)
  Pallas kernels  13.1 us (14%)
  local copies, waits for them, and re-layouts  3.49 us (4%)
    ppermute x8, waiting for transfers between devices, flip(): return lax.ppermute(x, 'ctx', [(i, i ^ bit) for i in range(devices)])  62.8 us
    ppermute x8, starting transfers between devices, flip(): return lax.ppermute(x, 'ctx', [(i, i ^ bit) for i in range(devices)])  8.82 us
    all_to_all x1, starting transfers between devices, local(): lax.all_to_all(tiles_out, 'ctx', split_axis=0, concat_axis=0, tiled=True)  7.53 us
    unnamed x16, local copies, waits for them, and re-layouts  3.49 us
    pallas_call x1, Pallas kernels, local(): pl.pallas_call(functools.partial(stage_kernel, devices, group), out_shape...  3.49 us
    pallas_call x1, Pallas kernels, local(): pl.pallas_call(functools.partial(attend_kernel, levels), out_shape=[jax.S...  3.47 us
    pallas_call x1, Pallas kernels, local(): pl.pallas_call(functools.partial(place_kernel, devices, group), out_shape...  2.7 us
    pallas_call x6, Pallas kernels, local_call(): pl.pallas_call(kernel, out_shape=out_shape, in_specs=[SMEM if x is me or...  1.94 us
  transfers between devices with their start and end apart: 9, of which 7 were waited for; matrix products, arithmetic and copies ran while one was open for 0% of the time, Pallas kernels for 8%

commit v1 on v0

--- a/solution.py
+++ b/solution.py
@@ -22,17 +22,17 @@
 COST = pl.CostEstimate(flops=1000, bytes_accessed=1000, transcendentals=0)
 
 
-def stage_kernel(devices, group, me_ref, dest_hbm, k_ref, v_ref, buf, table, k_vm, v_vm, dest, counts, sem, load_sem):
-    rows, heads = k_ref.shape[:2]
+def stage_kernel(devices, group, me_ref, dest_hbm, x_ref, buf, table, me_out, x_vm, dest, counts, sem, load_sem):
+    rows, heads = x_ref.shape[:2]
     small = pltpu.make_async_copy(dest_hbm, dest, sem.at[0])
     small.start()
     loads = []
     for row in range(rows):
-        for which, (src, dst) in enumerate(((k_ref, k_vm), (v_ref, v_vm))):
-            copy = pltpu.make_async_copy(src.at[row], dst.at[row], load_sem.at[which, row])
-            copy.start()
-            loads.append(copy)
+        copy = pltpu.make_async_copy(x_ref.at[row], x_vm.at[row], load_sem.at[row])
+        copy.start()
+        loads.append(copy)
     me = me_ref[0]
+    me_out[0] = me
 
     def clear(i, carry):
         counts[i] = 0
@@ -43,22 +43,15 @@
     lax.fori_loop(0, devices, clear, 0)
     small.wait()
     for row in range(rows):
-        loads[2 * row].wait()
-        loads[2 * row + 1].wait()
-
-        def send(head, carry):
-            offset = lax.rem(dest[row, head, 0], devices)
-            rank = jnp.minimum(counts[offset], group - 1)
+        loads[row].wait()
+        for head in range(heads):
+            offset = dest[row, head, 0]
+            rank = counts[offset]
             counts[offset] = rank + 1
             table[offset * group + rank] = row * heads + head
-            slot = lax.rem(me + offset, devices) * group + rank
-            pltpu.make_async_copy(k_vm.at[row, head], buf.at[slot, 0], sem.at[1]).start()
-            pltpu.make_async_copy(v_vm.at[row, head], buf.at[slot, 1], sem.at[2]).start()
-            return carry
-
-        lax.fori_loop(0, heads, send, 0)
-    pltpu.make_async_copy(k_ref, k_vm, sem.at[1]).wait()
-    pltpu.make_async_copy(v_ref, v_vm, sem.at[2]).wait()
+            slot = jnp.bitwise_and(me + offset, devices - 1) * group + rank
+            pltpu.make_async_copy(x_vm.at[row, head], buf.at[slot], sem.at[1]).start()
+    pltpu.make_async_copy(x_ref, x_vm, sem.at[1]).wait()
 
 
 def attend_kernel(
@@ -206,10 +199,6 @@
     out[base + 2 * per:base + 4 * per, :] = parts[2].astype(BF16)
 
 
-def pass_kernel(me_ref, x, out):
-    out[...] = x[...]
-
-
 def finish_kernel(pairs, per, heads, levels, me_ref, stats_ref, *refs):
     ins, out, mass_ref = refs[:levels], refs[levels], refs[levels + 1]
     base = pairs * per
@@ -230,23 +219,19 @@
         mass_ref[row] = mass[:, row * heads:(row + 1) * heads]
 
 
-def place_kernel(devices, group, me_ref, table, got_ref, k_ref, v_ref, me_out, sem):
-    heads = k_ref.shape[1]
+def place_kernel(devices, group, me_ref, table, got_ref, out_ref, sem):
+    heads = out_ref.shape[1]
     me = me_ref[0]
-    me_out[0] = me
     for offset in range(devices):
-        source = lax.rem(me + devices - offset, devices)
+        source = jnp.bitwise_and(me + devices - offset, devices - 1)
         for k in range(group):
             pair = table[offset * group + k]
 
             @pl.when(pair >= 0)
             def _():
-                row, head = pair // heads, lax.rem(pair, heads)
-                for which, ref in enumerate((k_ref, v_ref)):
-                    src = got_ref.at[source * group + k, which]
-                    pltpu.make_async_copy(src, ref.at[row, head], sem.at[which]).start()
-    pltpu.make_async_copy(k_ref, k_ref, sem.at[0]).wait()
-    pltpu.make_async_copy(v_ref, v_ref, sem.at[1]).wait()
+                dst = out_ref.at[pair // heads, lax.rem(pair, heads)]
+                pltpu.make_async_copy(got_ref.at[source * group + k], dst, sem).start()
+    pltpu.make_async_copy(out_ref, out_ref, sem).wait()
 
 
 def local(queries, key_cache, value_cache, row_lengths, kept_tiles, tile_dest):
@@ -265,26 +250,35 @@
     block_rows = rows * q_heads + 2 * per
     block_type = jax.ShapeDtypeStruct((block_rows, width), F32)
     message_type = jax.ShapeDtypeStruct((rows * q_heads + 4 * per, width), BF16)
-    tiles_type = jax.ShapeDtypeStruct((devices * group, 2, span, width), BF16)
-
-    tiles_out, table = pl.pallas_call(
-        functools.partial(stage_kernel, devices, group),
-        out_shape=[tiles_type, jax.ShapeDtypeStruct((devices * group,), jnp.int32)],
-        in_specs=[SMEM, HBM, HBM, HBM],
-        out_specs=[HBM, SMEM],
-        scratch_shapes=[
-            pltpu.VMEM(key_cache.shape, BF16),
-            pltpu.VMEM(value_cache.shape, BF16),
-            pltpu.SMEM(tile_dest.shape, jnp.int32),
-            pltpu.SMEM((devices,), jnp.int32),
-            pltpu.SemaphoreType.DMA((3,)),
-            pltpu.SemaphoreType.DMA((2, rows)),
-        ],
-        compiler_params=WHOLE,
-        cost_estimate=COST,
-        name="stage",
-    )(me, tile_dest, key_cache, value_cache)
-    tiles_in = lax.all_to_all(tiles_out, "ctx", split_axis=0, concat_axis=0, tiled=True)
+    tiles_type = jax.ShapeDtypeStruct((devices * group, span, width), BF16)
+
+    def stage(name, params, me, dest, x):
+        return pl.pallas_call(
+            functools.partial(stage_kernel, devices, group),
+            out_shape=[
+                tiles_type,
+                jax.ShapeDtypeStruct((devices * group,), jnp.int32),
+                jax.ShapeDtypeStruct((1,), jnp.int32),
+            ],
+            in_specs=[SMEM, HBM, HBM],
+            out_specs=[HBM, SMEM, SMEM],
+            scratch_shapes=[
+                pltpu.VMEM(x.shape, BF16),
+                pltpu.SMEM(dest.shape, jnp.int32),
+                pltpu.SMEM((devices,), jnp.int32),
+                pltpu.SemaphoreType.DMA((2,)),
+                pltpu.SemaphoreType.DMA((rows,)),
+            ],
+            compiler_params=params,
+            cost_estimate=COST,
+            name=name,
+        )(me, dest, x)
+
+    def exchange(x):
+        return lax.all_to_all(x, "ctx", split_axis=0, concat_axis=0, tiled=True)
+
+    keys_out, table, me_next = stage("stage_keys", WHOLE, me, tile_dest, key_cache)
+    keys_in = exchange(keys_out)
 
     stats, *chunks = pl.pallas_call(
         functools.partial(attend_kernel, levels),
@@ -303,6 +297,9 @@
         name="attend",
     )(me, table, row_lengths, kept, queries, key_cache, value_cache)
 
+    values_out, _, _ = stage("stage_values", PARAMS, me_next, tile_dest, value_cache)
+    values_in = exchange(values_out)
+
     def flip(x, bit):
         return lax.ppermute(x, "ctx", [(i, i ^ bit) for i in range(devices)])
 
@@ -337,24 +334,21 @@
     )
     other = flip(message, 2)
 
-    moved_keys, moved_values, me_next = pl.pallas_call(
-        functools.partial(place_kernel, devices, group),
-        out_shape=[
-            jax.ShapeDtypeStruct(key_cache.shape, BF16),
-            jax.ShapeDtypeStruct(value_cache.shape, BF16),
-            jax.ShapeDtypeStruct((1,), jnp.int32),
-        ],
-        in_specs=[SMEM, SMEM, ANY],
-        out_specs=[HBM, HBM, SMEM],
-        scratch_shapes=[pltpu.SemaphoreType.DMA((2,))],
-        compiler_params=PARAMS,
-        cost_estimate=COST,
-        name="place",
-    )(me, table, tiles_in)
-
-    other_next, = local_call(pass_kernel, "pass", [message_type], me_next, other)
-    arrived = [message, other, flip(message, 1), flip(other_next, 1)]
-
+    def place(name, got):
+        return pl.pallas_call(
+            functools.partial(place_kernel, devices, group),
+            out_shape=jax.ShapeDtypeStruct(key_cache.shape, BF16),
+            in_specs=[SMEM, SMEM, ANY],
+            out_specs=HBM,
+            scratch_shapes=[pltpu.SemaphoreType.DMA],
+            compiler_params=PARAMS,
+            cost_estimate=COST,
+            name=name,
+        )(me, table, got)
+
+    moved_keys = place("place_keys", keys_in)
+    moved_values = place("place_values", values_in)
+    arrived = [message, other, flip(message, 1), flip(other, 1)]
     attn_out, mass = pl.pallas_call(
         functools.partial(finish_kernel, pairs, per, heads, levels),
         out_shape=[
@@ -366,7 +360,7 @@
         compiler_params=PARAMS,
         cost_estimate=COST,
         name="finish",
-    )(me_next, stats, *arrived)
+    )(me, stats, *arrived)
     return attn_out.reshape(queries.shape), jnp.transpose(mass, (0, 2, 1)), moved_keys, moved_values
 
 

time: 96.9 us -> 155 us (1.60)
  Pallas kernels: 13.1 us -> 64.1 us
  starting transfers between devices: 16.3 us -> 25.4 us
  waiting for transfers between devices: 62.8 us -> 60.8 us
    pallas_call x2 -> x4, Pallas kernels: 6.19 us -> 58.5 us  [the longest x2 51 us: place(): pl.pallas_call(functools.partial(place_kernel, devices, group), out_shape...]
    ppermute x8, waiting for transfers between devices: 62.8 us -> 34.7 us  [flip(): return lax.ppermute(x, 'ctx', [(i, i ^ bit) for i in range(devices)])]
    all_to_all x1 -> x2, waiting for transfers between devices: 0.01 us -> 26.2 us  [exchange(): return lax.all_to_all(x, 'ctx', split_axis=0, concat_axis=0, tiled=True)]
    all_to_all x1 -> x2, starting transfers between devices: 7.53 us -> 16.8 us  [exchange(): return lax.all_to_all(x, 'ctx', split_axis=0, concat_axis=0, tiled=True)]
    unnamed x16 -> x20, local copies, waits for them, and re-layouts: 3.49 us -> 2.96 us
  transfers between devices with their start and end apart: 9 -> 10, of which waited for: 7 -> 8; matrix products, arithmetic and copies ran while one was open for 0% -> 0% of each run, Pallas kernels for 8% -> 8%
where the time goes in v1:
time: 155 us; the launch traced here: 154 us
  Pallas kernels  64.1 us (41%)
  waiting for transfers between devices  60.8 us (39%)
  starting transfers between devices  25.4 us (16%)
  local copies, waits for them, and re-layouts  2.96 us (2%)
    pallas_call x2, Pallas kernels, place(): pl.pallas_call(functools.partial(place_kernel, devices, group), out_shape...  51 us
    ppermute x8, waiting for transfers between devices, flip(): return lax.ppermute(x, 'ctx', [(i, i ^ bit) for i in range(devices)])  34.7 us
    all_to_all x2, waiting for transfers between devices, exchange(): return lax.all_to_all(x, 'ctx', split_axis=0, concat_axis=0, tiled=True)  26.2 us
    all_to_all x2, starting transfers between devices, exchange(): return lax.all_to_all(x, 'ctx', split_axis=0, concat_axis=0, tiled=True)  16.8 us
    ppermute x8, starting transfers between devices, flip(): return lax.ppermute(x, 'ctx', [(i, i ^ bit) for i in range(devices)])  8.57 us
    pallas_call x2, Pallas kernels, stage(): pl.pallas_call(functools.partial(stage_kernel, devices, group), out_shape...  7.53 us
    pallas_call x1, Pallas kernels, local(): pl.pallas_call(functools.partial(attend_kernel, levels), out_shape=[jax.S...  3.46 us
  transfers between devices with their start and end apart: 10, of which 8 were waited for; matrix products, arithmetic and copies ran while one was open for 0% of the time, Pallas kernels for 8%

profile of v1, /device:TPU:0, one launch (start us, length us, event | category | flops | bytes accessed | tf_op | source)
XLA Modules:
  0.0 154.3 jit_solution(3373155024866615217)
XLA Ops:
  0.6 2.9 %stage_keys.1 = (bf16[48,128,128]{2,1,0:T(8,128)(2,1)}, s32[48]{0:T(128)}, s32[1]{0:T(128)}) custom-call(s32[1]{0:T(128)} %bitcast.me_ref, s32[6,8,16]{2,1,0:T(8,128)} %dest_hbm.3, bf16[6,8,128,128]{3,2,1,0:T(8,128)(2,1)} %k_ref.1), custom_call_target="tpu_custom_call" | custom-call | flops 1000 | bytes 1000 | tf_op jit(solution)/shard_map/stage_keys/pallas_call | solution.py:256
  3.6 0.0 copy-start.1
  3.6 0.0 copy-start.6
  3.6 7.5 %all-to-all-start = ((bf16[48,128,128]{2,1,0:T(8,128)(2,1)}), bf16[48,128,128]{2,1,0:T(8,128)(2,1)S(1)}, u32[]{:S(2)}, u32[]{:S(2)}) async-start(bf16[48,128,128]{2,1,0:T(8,128)(2,1)} %get-tuple-element.27), calls=%async_computation | async-start | bytes 3145728 | tf_op jit(solution)/shard_map/all_to_all | solution.py:278
  11.1 0.0 copy-done.1
  11.1 0.0 copy-done.6
  11.1 4.6 %stage_values.1 = (bf16[48,128,128]{2,1,0:T(8,128)(2,1)S(1)}, s32[48]{0:T(128)}, s32[1]{0:T(128)}) custom-call(s32[1]{0:T(128)} %get-tuple-element.28.me_ref, s32[6,8,16]{2,1,0:T(8,128)S(1)} %copy-done.6, bf16[6,8,128,128]{3,2,1,0:T(8,128)(2,1)S(1)} %copy-done.1), custom_call_target="tpu_custom_call" | custom-call | flops 1000 | bytes 1000 | tf_op jit(solution)/shard_map/stage_values/pallas_call | solution.py:256
  15.8 0.0 copy-start.4
  15.8 1.1 copy-done.4
  16.9 26.2 %all-to-all-done.got_ref = bf16[48,128,128]{2,1,0:T(8,128)(2,1)S(1)} async-done(((bf16[48,128,128]{2,1,0:T(8,128)(2,1)}), bf16[48,128,128]{2,1,0:T(8,128)(2,1)S(1)}, u32[]{:S(2)}, u32[]{:S(2)}) %all-to-all-start) | async-done | bytes 1572896 | tf_op jit(solution)/shard_map/all_to_all | solution.py:278
  43.1 0.0 copy-start.2
  43.1 1.1 copy-done.2
  44.2 0.0 copy-start
  44.2 9.3 %all-to-all-start.1 = ((bf16[48,128,128]{2,1,0:T(8,128)(2,1)}), bf16[48,128,128]{2,1,0:T(8,128)(2,1)}, u32[]{:S(2)}, u32[]{:S(2)}) async-start(bf16[48,128,128]{2,1,0:T(8,128)(2,1)} %copy-done.4), calls=%async_computation.1 | async-start | bytes 3145728 | tf_op jit(solution)/shard_map/all_to_all | solution.py:278
  53.6 0.0 copy-done
  53.6 0.0 copy-done.5
  53.6 0.0 copy-done.7
  53.6 0.0 copy-done.8
  53.6 0.0 copy-start.9
  53.6 0.6 copy-done.9
  54.2 3.5 %attend.1 = (f32[2,32,128]{2,1,0:T(8,128)S(1)}, f32[2,400,128]{2,1,0:T(8,128)S(1)}, f32[2,400,128]{2,1,0:T(8,128)S(1)}) custom-call(s32[1]{0:T(128)} %bitcast.me_ref, s32[48]{0:T(128)S(1)} %copy-done.8, s32[6]{0:T(128)S(1)} %copy-done.9, s32[6,4,16]{2,1,0:T(4,128)S(1)} %bitcast.4, bf16[4,6,64,128]{3,2,1,0:T(8,128)(2,1)S(1)} %copy-done.5, ...), custom_call_target="tpu_custom_call" | custom-call | flops 1000 | bytes 1000 | tf_op jit(solution)/shard_map/attend/pallas_call | solution.py:283
  57.7 0.4 collective-permute-start
  58.1 1.4 collective-permute-done.got
  59.5 0.4 core.1
  59.9 1.9 %collective-permute-start.1 = (f32[400,128]{1,0:T(8,128)S(1)}, f32[400,128]{1,0:T(8,128)S(1)}, u32[]{:S(2)}, u32[]{:S(2)}) collective-permute-start(f32[400,128]{1,0:T(8,128)S(1)} %get-tuple-element.22), channel_id=1, source_target_pairs={{0,2},{1,3},{2,0},{3,1},{4,6},{5,7},{6,4},{7,5},{8,10},{9,11},{10,... | collective-permute-start | bytes 614408 | tf_op jit(solution)/shard_map/ppermute | solution.py:304
  61.9 11.5 %collective-permute-done.1.got = f32[400,128]{1,0:T(8,128)S(1)} collective-permute-done((f32[400,128]{1,0:T(8,128)S(1)}, f32[400,128]{1,0:T(8,128)S(1)}, u32[]{:S(2)}, u32[]{:S(2)}) %collective-permute-start.1) | collective-permute-done | bytes 204832 | tf_op jit(solution)/shard_map/ppermute | solution.py:304
  73.4 0.2 near.1.own
  73.6 0.1 collective-permute-start.2
  73.7 10.7 %collective-permute-done.2.got = f32[400,128]{1,0:T(8,128)S(1)} collective-permute-done((f32[400,128]{1,0:T(8,128)S(1)}, f32[400,128]{1,0:T(8,128)S(1)}, u32[]{:S(2)}, u32[]{:S(2)}) %collective-permute-start.2) | collective-permute-done | bytes 204832 | tf_op jit(solution)/shard_map/ppermute | solution.py:304
  84.4 0.2 far.1.block
  84.6 0.1 scale.1
  84.8 0.1 reduce-precision_convert_fusion
  84.9 4.5 %collective-permute-start.3 = (f16[384,128]{1,0:T(8,128)(2,1)S(1)}, f16[384,128]{1,0:T(8,128)(2,1)S(1)}, u32[]{:S(2)}, u32[]{:S(2)}) collective-permute-start(f16[384,128]{1,0:T(8,128)(2,1)S(1)} %get-tuple-element.30), channel_id=1, source_target_pairs={{0,8},{1,9},{2,10},{3,11},{4,12},{5,13},{6,14},{7,15},{8,0},{9,1},... | collective-permute-start | bytes 294920 | tf_op jit(solution)/shard_map/ppermute | solution.py:304
  89.4 0.1 collective-permute-start.4
  89.5 6.4 %collective-permute-done.3 = f16[384,128]{1,0:T(8,128)(2,1)S(1)} collective-permute-done((f16[384,128]{1,0:T(8,128)(2,1)S(1)}, f16[384,128]{1,0:T(8,128)(2,1)S(1)}, u32[]{:S(2)}, u32[]{:S(2)}) %collective-permute-start.3) | collective-permute-done | bytes 98336 | tf_op jit(solution)/shard_map/ppermute | solution.py:304
  95.9 0.1 collective-permute-done.4.got_stats
  96.0 0.3 last.1.refs_0_
  96.3 1.5 collective-permute-start.5
  97.9 0.0 collective-permute-start.6
  97.9 3.2 %collective-permute-done.5.refs_1_ = bf16[416,128]{1,0:T(8,128)(2,1)S(1)} collective-permute-done((bf16[416,128]{1,0:T(8,128)(2,1)S(1)}, bf16[416,128]{1,0:T(8,128)(2,1)S(1)}, u32[]{:S(2)}, u32[]{:S(2)}) %collective-permute-start.5) | collective-permute-done | bytes 106528 | tf_op jit(solution)/shard_map/ppermute | solution.py:304
  101.1 0.0 collective-permute-start.7
  101.1 0.0 collective-permute-done.6.refs_2_
  101.1 1.3 collective-permute-done.7.refs_3_
  102.4 0.9 finish.1
  103.3 0.0 copy-done.3
  103.3 1.7 %place_keys.1 = bf16[6,8,128,128]{3,2,1,0:T(8,128)(2,1)} custom-call(s32[1]{0:T(128)} %bitcast.me_ref, s32[48]{0:T(128)S(1)} %copy-done.8, bf16[48,128,128]{2,1,0:T(8,128)(2,1)S(1)} %copy-done.3), custom_call_target="tpu_custom_call" | custom-call | flops 1000 | bytes 1000 | tf_op jit(solution)/shard_map/place_keys/pallas_call | solution.py:338
  105.0 0.0 all-to-all-done.1.got_ref
  105.0 49.3 %place_values.1 = bf16[6,8,128,128]{3,2,1,0:T(8,128)(2,1)} custom-call(s32[1]{0:T(128)} %bitcast.me_ref, s32[48]{0:T(128)S(1)} %copy-done.8, bf16[48,128,128]{2,1,0:T(8,128)(2,1)} %all-to-all-done.1.got_ref), custom_call_target="tpu_custom_call" | custom-call | flops 1000 | bytes 1000 | tf_op jit(solution)/shard_map/place_values/pallas_call | solution.py:338
  (5 shorter events, 0.0 us)
Async XLA Ops:
  3.6 7.6 %copy-start.1 = (bf16[6,8,128,128]{3,2,1,0:T(8,128)(2,1)S(1)}, bf16[6,8,128,128]{3,2,1,0:T(8,128)(2,1)}, u32[]{:S(2)}) copy-start(bf16[6,8,128,128]{3,2,1,0:T(8,128)(2,1)} %x_ref.3) | copy-start | bytes 4718596
  3.6 7.6 %copy-start.6 = (s32[6,8,16]{2,1,0:T(8,128)S(1)}, s32[6,8,16]{2,1,0:T(8,128)}, u32[]{:S(2)}) copy-start(s32[6,8,16]{2,1,0:T(8,128)} %dest_hbm.3) | copy-start | bytes 9220
  3.6 39.5 %all-to-all-start = ((bf16[48,128,128]{2,1,0:T(8,128)(2,1)}), bf16[48,128,128]{2,1,0:T(8,128)(2,1)S(1)}, u32[]{:S(2)}, u32[]{:S(2)}) async-start(bf16[48,128,128]{2,1,0:T(8,128)(2,1)} %get-tuple-element.27), calls=%async_computation | async-start | bytes 3145728 | tf_op jit(solution)/shard_map/all_to_all | solution.py:278
  15.8 1.1 copy-start.4
  43.1 1.1 copy-start.2
  44.2 9.3 %copy-start = (bf16[6,8,128,128]{3,2,1,0:T(8,128)(2,1)S(1)}, bf16[6,8,128,128]{3,2,1,0:T(8,128)(2,1)}, u32[]{:S(2)}) copy-start(bf16[6,8,128,128]{3,2,1,0:T(8,128)(2,1)} %k_ref.1) | copy-start | bytes 4718596
  44.2 9.3 %copy-start.5 = (bf16[4,6,64,128]{3,2,1,0:T(8,128)(2,1)S(1)}, bf16[4,6,64,128]{3,2,1,0:T(8,128)(2,1)}, u32[]{:S(2)}) copy-start(bf16[4,6,64,128]{3,2,1,0:T(8,128)(2,1)} %q_ref.1) | copy-start | bytes 1179652
  44.2 9.3 %copy-start.7 = (s32[4,6,16]{2,0,1:T(4,128)S(1)}, s32[4,6,16]{2,0,1:T(4,128)}, u32[]{:S(2)}) copy-start(s32[4,6,16]{2,0,1:T(4,128)} %param.10) | copy-start | bytes 4612
  44.2 9.3 %copy-start.8 = (s32[48]{0:T(128)S(1)}, s32[48]{0:T(128)}, u32[]{:S(2)}) copy-start(s32[48]{0:T(128)} %get-tuple-element.17.table) | copy-start | bytes 580
  44.2 60.7 %all-to-all-start.1 = ((bf16[48,128,128]{2,1,0:T(8,128)(2,1)}), bf16[48,128,128]{2,1,0:T(8,128)(2,1)}, u32[]{:S(2)}, u32[]{:S(2)}) async-start(bf16[48,128,128]{2,1,0:T(8,128)(2,1)} %copy-done.4), calls=%async_computation.1 | async-start | bytes 3145728 | tf_op jit(solution)/shard_map/all_to_all | solution.py:278
  53.6 0.7 copy-start.9
  57.7 1.8 %collective-permute-start = (f32[2,400,128]{2,1,0:T(8,128)S(1)}, f32[2,400,128]{2,1,0:T(8,128)S(1)}, u32[]{:S(2)}, u32[]{:S(2)}) collective-permute-start(f32[2,400,128]{2,1,0:T(8,128)S(1)} %get-tuple-element.20), channel_id=1, source_target_pairs={{0,1},{1,0},{2,3},{3,2},{4,5},{5,4},{6,7},{7,6},{8,9},{9,8},{10,11... | collective-permute-start | bytes 1228808 | tf_op jit(solution)/shard_map/ppermute | solution.py:304
  59.9 13.5 %collective-permute-start.1 = (f32[400,128]{1,0:T(8,128)S(1)}, f32[400,128]{1,0:T(8,128)S(1)}, u32[]{:S(2)}, u32[]{:S(2)}) collective-permute-start(f32[400,128]{1,0:T(8,128)S(1)} %get-tuple-element.22), channel_id=1, source_target_pairs={{0,2},{1,3},{2,0},{3,1},{4,6},{5,7},{6,4},{7,5},{8,10},{9,11},{10,... | collective-permute-start | bytes 614408 | tf_op jit(solution)/shard_map/ppermute | solution.py:304
  73.4 29.9 %copy-start.3 = (bf16[48,128,128]{2,1,0:T(8,128)(2,1)S(1)}, bf16[48,128,128]{2,1,0:T(8,128)(2,1)}, u32[]{:S(2)}) copy-start(bf16[48,128,128]{2,1,0:T(8,128)(2,1)} %copy-done.2) | copy-start | bytes 4718596
  73.6 10.8 %collective-permute-start.2 = (f32[400,128]{1,0:T(8,128)S(1)}, f32[400,128]{1,0:T(8,128)S(1)}, u32[]{:S(2)}, u32[]{:S(2)}) collective-permute-start(f32[400,128]{1,0:T(8,128)S(1)} %near.1.own), channel_id=1, source_target_pairs={{0,4},{1,5},{2,6},{3,7},{4,0},{5,1},{6,2},{7,3},{8,12},{9,13},{10,... | collective-permute-start | bytes 614408 | tf_op jit(solution)/shard_map/ppermute | solution.py:304
  84.9 11.0 %collective-permute-start.3 = (f16[384,128]{1,0:T(8,128)(2,1)S(1)}, f16[384,128]{1,0:T(8,128)(2,1)S(1)}, u32[]{:S(2)}, u32[]{:S(2)}) collective-permute-start(f16[384,128]{1,0:T(8,128)(2,1)S(1)} %get-tuple-element.30), channel_id=1, source_target_pairs={{0,8},{1,9},{2,10},{3,11},{4,12},{5,13},{6,14},{7,15},{8,0},{9,1},... | collective-permute-start | bytes 294920 | tf_op jit(solution)/shard_map/ppermute | solution.py:304
  89.4 6.6 %collective-permute-start.4 = (f32[24,128]{1,0:T(8,128)S(1)}, f32[24,128]{1,0:T(8,128)S(1)}, u32[]{:S(2)}, u32[]{:S(2)}) collective-permute-start(f32[24,128]{1,0:T(8,128)S(1)} %get-tuple-element.24.own_stats), channel_id=1, source_target_pairs={{0,8},{1,9},{2,10},{3,11},{4,12},{5,13},{6,14},{7,15},{8,0},{9,1},... | collective-permute-start | bytes 36872 | tf_op jit(solution)/shard_map/ppermute | solution.py:304
  96.3 4.8 %collective-permute-start.5 = (bf16[416,128]{1,0:T(8,128)(2,1)S(1)}, bf16[416,128]{1,0:T(8,128)(2,1)S(1)}, u32[]{:S(2)}, u32[]{:S(2)}) collective-permute-start(bf16[416,128]{1,0:T(8,128)(2,1)S(1)} %last.1.refs_0_), channel_id=1, source_target_pairs={{0,2},{1,3},{2,0},{3,1},{4,6},{5,7},{6,4},{7,5},{8,10},{9,11},{10,... | collective-permute-start | bytes 319496 | tf_op jit(solution)/shard_map/ppermute | solution.py:304
  97.9 3.2 %collective-permute-start.6 = (bf16[416,128]{1,0:T(8,128)(2,1)S(1)}, bf16[416,128]{1,0:T(8,128)(2,1)S(1)}, u32[]{:S(2)}, u32[]{:S(2)}) collective-permute-start(bf16[416,128]{1,0:T(8,128)(2,1)S(1)} %last.1.refs_0_), channel_id=1, source_target_pairs={{0,1},{1,0},{2,3},{3,2},{4,5},{5,4},{6,7},{7,6},{8,9},{9,8},{10,11... | collective-permute-start | bytes 319496 | tf_op jit(solution)/shard_map/ppermute | solution.py:304
  101.1 1.3 collective-permute-start.7

commit v2 on v0

--- a/solution.py
+++ b/solution.py
@@ -46,17 +46,14 @@
         loads[2 * row].wait()
         loads[2 * row + 1].wait()
 
-        def send(head, carry):
-            offset = lax.rem(dest[row, head, 0], devices)
-            rank = jnp.minimum(counts[offset], group - 1)
+        for head in range(heads):
+            offset = dest[row, head, 0]
+            rank = counts[offset]
             counts[offset] = rank + 1
             table[offset * group + rank] = row * heads + head
-            slot = lax.rem(me + offset, devices) * group + rank
+            slot = jnp.bitwise_and(me + offset, devices - 1) * group + rank
             pltpu.make_async_copy(k_vm.at[row, head], buf.at[slot, 0], sem.at[1]).start()
             pltpu.make_async_copy(v_vm.at[row, head], buf.at[slot, 1], sem.at[2]).start()
-            return carry
-
-        lax.fori_loop(0, heads, send, 0)
     pltpu.make_async_copy(k_ref, k_vm, sem.at[1]).wait()
     pltpu.make_async_copy(v_ref, v_vm, sem.at[2]).wait()
 
@@ -206,18 +203,20 @@
     out[base + 2 * per:base + 4 * per, :] = parts[2].astype(BF16)
 
 
-def pass_kernel(me_ref, x, out):
-    out[...] = x[...]
-
-
 def finish_kernel(pairs, per, heads, levels, me_ref, stats_ref, *refs):
-    ins, out, mass_ref = refs[:levels], refs[levels], refs[levels + 1]
+    ins, (out, mass_ref, sem) = refs[:levels], refs[levels:]
     base = pairs * per
+    copies = [
+        pltpu.make_async_copy(
+            ins[level].at[:base], out.at[jnp.bitwise_xor(place_of(me_ref[0]), level)], sem.at[level]
+        )
+        for level in range(levels)
+    ]
+    for copy in copies:
+        copy.start()
     lane = lax.broadcasted_iota(jnp.int32, (2 * per, LANES), 1)
     mass = jnp.zeros((per, LANES), F32)
     for level in range(levels):
-        step = jnp.bitwise_xor(place_of(me_ref[0]), level)
-        out[step] = ins[level][:base, :]
         packed = ins[level][base:base + 2 * per, :].astype(F32)
         third = ins[level][base + 2 * per:base + 4 * per, :].astype(F32)
         both = third + pltpu.roll(packed, LANES // 2, 1) + packed
@@ -228,6 +227,8 @@
     mass = jnp.sum(mass, axis=0, keepdims=True)
     for row in range(pairs // heads):
         mass_ref[row] = mass[:, row * heads:(row + 1) * heads]
+    for copy in copies:
+        copy.wait()
 
 
 def place_kernel(devices, group, me_ref, table, got_ref, k_ref, v_ref, me_out, sem):
@@ -235,7 +236,7 @@
     me = me_ref[0]
     me_out[0] = me
     for offset in range(devices):
-        source = lax.rem(me + devices - offset, devices)
+        source = jnp.bitwise_and(me + devices - offset, devices - 1)
         for k in range(group):
             pair = table[offset * group + k]
 
@@ -331,12 +332,6 @@
     sums, sum_stats = local_call(functools.partial(scale_kernel, pairs, per), "scale", [sums_type, stats_type], block)
     sums = lax.reduce_precision(sums, 5, 10)
     got = flip(sums.astype(jnp.float16), bit).astype(F32)
-    message, = local_call(
-        functools.partial(last_kernel, bit, pairs, per), "last", [message_type],
-        me, sums, got, sum_stats, flip(sum_stats, bit),
-    )
-    other = flip(message, 2)
-
     moved_keys, moved_values, me_next = pl.pallas_call(
         functools.partial(place_kernel, devices, group),
         out_shape=[
@@ -352,8 +347,13 @@
         name="place",
     )(me, table, tiles_in)
 
-    other_next, = local_call(pass_kernel, "pass", [message_type], me_next, other)
-    arrived = [message, other, flip(message, 1), flip(other_next, 1)]
+
+    message, = local_call(
+        functools.partial(last_kernel, bit, pairs, per), "last", [message_type],
+        me_next, sums, got, sum_stats, flip(sum_stats, bit),
+    )
+    other = flip(message, 2)
+    arrived = [message, other, flip(message, 1), flip(other, 1)]
 
     attn_out, mass = pl.pallas_call(
         functools.partial(finish_kernel, pairs, per, heads, levels),
@@ -362,11 +362,12 @@
             jax.ShapeDtypeStruct((rows, 1, heads), F32),
         ],
         in_specs=[SMEM, VMEM] + [VMEM] * levels,
-        out_specs=[VMEM, VMEM],
+        out_specs=[HBM, VMEM],
+        scratch_shapes=[pltpu.SemaphoreType.DMA((levels,))],
         compiler_params=PARAMS,
         cost_estimate=COST,
         name="finish",
-    )(me_next, stats, *arrived)
+    )(me, stats, *arrived)
     return attn_out.reshape(queries.shape), jnp.transpose(mass, (0, 2, 1)), moved_keys, moved_values
 
 

time: 96.9 us -> 100 us (1.032)
  waiting for transfers between devices: 62.8 us -> 65.4 us
    ppermute x8, waiting for transfers between devices: 62.8 us -> 65.4 us  [flip(): return lax.ppermute(x, 'ctx', [(i, i ^ bit) for i in range(devices)])]
    pallas_call x6 -> x5, Pallas kernels: 1.94 us -> 2.67 us  [local_call(): pl.pallas_call(kernel, out_shape=out_shape, in_specs=[SMEM if x is me or...]
  transfers between devices with their start and end apart: 9 -> 9, of which waited for: 7 -> 6; matrix products, arithmetic and copies ran while one was open for 0% -> 0% of each run, Pallas kernels for 8% -> 7%
where the time goes in v2:
time: 100 us; the launch traced here: 99.9 us
  waiting for transfers between devices  65.4 us (65%)
  starting transfers between devices  16.3 us (16%)
  Pallas kernels  13.8 us (14%)
  local copies, waits for them, and re-layouts  3.5 us (4%)
    ppermute x8, waiting for transfers between devices, flip(): return lax.ppermute(x, 'ctx', [(i, i ^ bit) for i in range(devices)])  65.4 us
    ppermute x8, starting transfers between devices, flip(): return lax.ppermute(x, 'ctx', [(i, i ^ bit) for i in range(devices)])  8.72 us
    all_to_all x1, starting transfers between devices, local(): lax.all_to_all(tiles_out, 'ctx', split_axis=0, concat_axis=0, tiled=True)  7.53 us
    pallas_call x1, Pallas kernels, local(): pl.pallas_call(functools.partial(stage_kernel, devices, group), out_shape...  3.51 us
    unnamed x16, local copies, waits for them, and re-layouts  3.5 us
    pallas_call x1, Pallas kernels, local(): pl.pallas_call(functools.partial(attend_kernel, levels), out_shape=[jax.S...  3.47 us
    pallas_call x1, Pallas kernels, local(): pl.pallas_call(functools.partial(place_kernel, devices, group), out_shape...  2.7 us
    pallas_call x5, Pallas kernels, local_call(): pl.pallas_call(kernel, out_shape=out_shape, in_specs=[SMEM if x is me or...  2.67 us
  transfers between devices with their start and end apart: 9, of which 6 were waited for; matrix products, arithmetic and copies ran while one was open for 0% of the time, Pallas kernels for 7%

profile of v2, /device:TPU:0, one launch (start us, length us, event | category | flops | bytes accessed | tf_op | source)
XLA Modules:
  0.0 99.9 jit_solution(16062048711507147497)
XLA Ops:
  0.6 3.5 %stage.1 = (bf16[48,2,128,128]{3,2,1,0:T(8,128)(2,1)}, s32[48]{0:T(128)}) custom-call(s32[1]{0:T(128)} %bitcast.me_ref, s32[6,8,16]{2,1,0:T(8,128)} %dest_hbm.1, bf16[6,8,128,128]{3,2,1,0:T(8,128)(2,1)} %k_ref.3, bf16[6,8,128,128]{3,2,1,0:T(8,128)(2,1)} %v_ref.3), custom_call_target="tpu_custom_call" | custom-call | flops 1000 | bytes 1000 | tf_op jit(solution)/shard_map/stage/pallas_call | solution.py:271
  4.1 0.0 copy-start.2
  4.2 0.0 copy-start.5
  4.2 0.0 copy-start.6
  4.2 7.5 %all-to-all-start = ((bf16[48,2,128,128]{3,2,1,0:T(8,128)(2,1)}), bf16[48,2,128,128]{3,2,1,0:T(8,128)(2,1)S(1)}, u32[]{:S(2)}, u32[]{:S(2)}) async-start(bf16[48,2,128,128]{3,2,1,0:T(8,128)(2,1)} %get-tuple-element.20), calls=%async_computation | async-start | bytes 6291456 | tf_op jit(solution)/shard_map/all_to_all | solution.py:288
  11.7 0.0 copy-done.2
  11.7 0.0 copy-done.5
  11.7 0.0 copy-done.6
  11.8 0.0 copy-start
  11.8 1.4 %copy-done = bf16[6,8,128,128]{3,2,1,0:T(8,128)(2,1)S(1)} copy-done((bf16[6,8,128,128]{3,2,1,0:T(8,128)(2,1)S(1)}, bf16[6,8,128,128]{3,2,1,0:T(8,128)(2,1)}, u32[]{:S(2)}) %copy-start) | copy-done | bytes 1572888
  13.2 0.0 copy-start.1
  13.2 1.4 %copy-done.1 = bf16[6,8,128,128]{3,2,1,0:T(8,128)(2,1)S(1)} copy-done((bf16[6,8,128,128]{3,2,1,0:T(8,128)(2,1)S(1)}, bf16[6,8,128,128]{3,2,1,0:T(8,128)(2,1)}, u32[]{:S(2)}) %copy-start.1) | copy-done | bytes 1572888
  14.6 0.0 copy-start.7
  14.6 0.7 copy-done.7
  15.2 3.5 %attend.1 = (f32[2,32,128]{2,1,0:T(8,128)S(1)}, f32[2,400,128]{2,1,0:T(8,128)S(1)}, f32[2,400,128]{2,1,0:T(8,128)S(1)}) custom-call(s32[1]{0:T(128)} %bitcast.me_ref, s32[48]{0:T(128)S(1)} %copy-done.6, s32[6]{0:T(128)S(1)} %copy-done.7, s32[6,4,16]{2,1,0:T(4,128)S(1)} %bitcast.4, bf16[4,6,64,128]{3,2,1,0:T(8,128)(2,1)S(1)} %copy-done.2, ...), custom_call_target="tpu_custom_call" | custom-call | flops 1000 | bytes 1000 | tf_op jit(solution)/shard_map/attend/pallas_call | solution.py:290
  18.7 0.0 copy-start.3
  18.7 0.5 collective-permute-start
  19.2 1.4 %collective-permute-done.got = f32[2,400,128]{2,1,0:T(8,128)S(1)} collective-permute-done((f32[2,400,128]{2,1,0:T(8,128)S(1)}, f32[2,400,128]{2,1,0:T(8,128)S(1)}, u32[]{:S(2)}, u32[]{:S(2)}) %collective-permute-start) | collective-permute-done | bytes 409632 | tf_op jit(solution)/shard_map/ppermute | solution.py:308
  20.6 0.4 core.1
  21.0 2.0 %collective-permute-start.1 = (f32[400,128]{1,0:T(8,128)S(1)}, f32[400,128]{1,0:T(8,128)S(1)}, u32[]{:S(2)}, u32[]{:S(2)}) collective-permute-start(f32[400,128]{1,0:T(8,128)S(1)} %get-tuple-element.25), channel_id=1, source_target_pairs={{0,2},{1,3},{2,0},{3,1},{4,6},{5,7},{6,4},{7,5},{8,10},{9,11},{10,... | collective-permute-start | bytes 614408 | tf_op jit(solution)/shard_map/ppermute | solution.py:308
  22.9 14.2 %collective-permute-done.1.got = f32[400,128]{1,0:T(8,128)S(1)} collective-permute-done((f32[400,128]{1,0:T(8,128)S(1)}, f32[400,128]{1,0:T(8,128)S(1)}, u32[]{:S(2)}, u32[]{:S(2)}) %collective-permute-start.1) | collective-permute-done | bytes 204832 | tf_op jit(solution)/shard_map/ppermute | solution.py:308
  37.1 0.2 near.1.own
  37.3 0.1 collective-permute-start.2
  37.4 30.5 %collective-permute-done.2.got = f32[400,128]{1,0:T(8,128)S(1)} collective-permute-done((f32[400,128]{1,0:T(8,128)S(1)}, f32[400,128]{1,0:T(8,128)S(1)}, u32[]{:S(2)}, u32[]{:S(2)}) %collective-permute-start.2) | collective-permute-done | bytes 204832 | tf_op jit(solution)/shard_map/ppermute | solution.py:308
  67.9 0.2 far.1.block
  68.1 0.1 scale.1
  68.3 0.1 reduce-precision_convert_fusion
  68.4 4.6 %collective-permute-start.3 = (f16[384,128]{1,0:T(8,128)(2,1)S(1)}, f16[384,128]{1,0:T(8,128)(2,1)S(1)}, u32[]{:S(2)}, u32[]{:S(2)}) collective-permute-start(f16[384,128]{1,0:T(8,128)(2,1)S(1)} %get-tuple-element.32), channel_id=1, source_target_pairs={{0,8},{1,9},{2,10},{3,11},{4,12},{5,13},{6,14},{7,15},{8,0},{9,1},... | collective-permute-start | bytes 294920 | tf_op jit(solution)/shard_map/ppermute | solution.py:308
  73.0 0.1 collective-permute-start.4
  73.0 14.9 %collective-permute-done.3 = f16[384,128]{1,0:T(8,128)(2,1)S(1)} collective-permute-done((f16[384,128]{1,0:T(8,128)(2,1)S(1)}, f16[384,128]{1,0:T(8,128)(2,1)S(1)}, u32[]{:S(2)}, u32[]{:S(2)}) %collective-permute-start.3) | collective-permute-done | bytes 98336 | tf_op jit(solution)/shard_map/ppermute | solution.py:308
  87.9 0.0 copy-done.3
  87.9 0.0 all-to-all-done.got_ref
  87.9 0.0 copy-start.4
  88.0 2.7 %place.1 = (bf16[6,8,128,128]{3,2,1,0:T(8,128)(2,1)}, bf16[6,8,128,128]{3,2,1,0:T(8,128)(2,1)}, s32[1]{0:T(128)}) custom-call(s32[1]{0:T(128)} %bitcast.me_ref, s32[48]{0:T(128)S(1)} %copy-done.6, bf16[48,2,128,128]{3,2,1,0:T(8,128)(2,1)S(1)} %all-to-all-done.got_ref), custom_call_target="tpu_custom_call" | custom-call | flops 1000 | bytes 1000 | tf_op jit(solution)/shard_map/place/pallas_call | solution.py:335
  90.7 0.0 collective-permute-done.4.got_stats
  90.7 1.7 %last.1.refs_0_ = bf16[416,128]{1,0:T(8,128)(2,1)S(1)} custom-call(s32[1]{0:T(128)} %get-tuple-element.21.me_ref, f32[384,128]{1,0:T(8,128)S(1)} %get-tuple-element.33.own, f32[384,128]{1,0:T(8,128)S(1)} %convert_element_type.7.got, f32[24,128]{1,0:T(8,128)S(1)} %get-tuple-element.27.own_stats, f32[24,128]{1,0:T(8,128)} %collective-permute-done.4.got_stats), custom_call_target="tpu_custom_call" | custom-call | flops 1000 | bytes 1000 | tf_op jit(solution)/shard_map/last/pallas_call | solution.py:311
  92.4 1.6 %collective-permute-start.5 = (bf16[416,128]{1,0:T(8,128)(2,1)S(1)}, bf16[416,128]{1,0:T(8,128)(2,1)S(1)}, u32[]{:S(2)}, u32[]{:S(2)}) collective-permute-start(bf16[416,128]{1,0:T(8,128)(2,1)S(1)} %last.1.refs_0_), channel_id=1, source_target_pairs={{0,2},{1,3},{2,0},{3,1},{4,6},{5,7},{6,4},{7,5},{8,10},{9,11},{10,... | collective-permute-start | bytes 319496 | tf_op jit(solution)/shard_map/ppermute | solution.py:308
  93.9 0.0 collective-permute-start.6
  93.9 3.2 %collective-permute-done.5.refs_1_ = bf16[416,128]{1,0:T(8,128)(2,1)S(1)} collective-permute-done((bf16[416,128]{1,0:T(8,128)(2,1)S(1)}, bf16[416,128]{1,0:T(8,128)(2,1)S(1)}, u32[]{:S(2)}, u32[]{:S(2)}) %collective-permute-start.5) | collective-permute-done | bytes 106528 | tf_op jit(solution)/shard_map/ppermute | solution.py:308
  97.1 0.0 collective-permute-start.7
  97.1 0.0 collective-permute-done.6.refs_2_
  97.1 1.3 %collective-permute-done.7.refs_3_ = bf16[416,128]{1,0:T(8,128)(2,1)S(1)} collective-permute-done((bf16[416,128]{1,0:T(8,128)(2,1)S(1)}, bf16[416,128]{1,0:T(8,128)(2,1)S(1)}, u32[]{:S(2)}, u32[]{:S(2)}) %collective-permute-start.7) | collective-permute-done | bytes 106528 | tf_op jit(solution)/shard_map/ppermute | solution.py:308
  98.4 0.0 copy-done.4
  98.4 1.4 %finish.1 = (bf16[4,384,128]{2,1,0:T(8,128)(2,1)}, f32[6,1,8]{2,1,0:T(1,128)}) custom-call(s32[1]{0:T(128)} %bitcast.me_ref, f32[2,32,128]{2,1,0:T(8,128)S(1)} %copy-done.4, bf16[416,128]{1,0:T(8,128)(2,1)S(1)} %last.1.refs_0_, bf16[416,128]{1,0:T(8,128)(2,1)S(1)} %collective-permute-done.5.refs_1_, bf16[416,128]{1,0:T(8,128)(2,1)S(1)} %collective-permute-done.6.refs_2_, ...), custom_call_target="tpu_custom_call" | custom-call | flops 1000 | bytes 1000 | tf_op jit(solution)/shard_map/finish/pallas_call | solution.py:358
  (1 shorter events, 0.0 us)
Async XLA Ops:
  4.1 7.6 %copy-start.2 = (bf16[4,6,64,128]{3,2,1,0:T(8,128)(2,1)S(1)}, bf16[4,6,64,128]{3,2,1,0:T(8,128)(2,1)}, u32[]{:S(2)}) copy-start(bf16[4,6,64,128]{3,2,1,0:T(8,128)(2,1)} %q_ref.1) | copy-start | bytes 1179652
  4.2 7.6 %copy-start.5 = (s32[4,6,16]{2,0,1:T(4,128)S(1)}, s32[4,6,16]{2,0,1:T(4,128)}, u32[]{:S(2)}) copy-start(s32[4,6,16]{2,0,1:T(4,128)} %param.10) | copy-start | bytes 4612
  4.2 7.6 %copy-start.6 = (s32[48]{0:T(128)S(1)}, s32[48]{0:T(128)}, u32[]{:S(2)}) copy-start(s32[48]{0:T(128)} %get-tuple-element.18.table) | copy-start | bytes 580
  4.2 83.8 %all-to-all-start = ((bf16[48,2,128,128]{3,2,1,0:T(8,128)(2,1)}), bf16[48,2,128,128]{3,2,1,0:T(8,128)(2,1)S(1)}, u32[]{:S(2)}, u32[]{:S(2)}) async-start(bf16[48,2,128,128]{3,2,1,0:T(8,128)(2,1)} %get-tuple-element.20), calls=%async_computation | async-start | bytes 6291456 | tf_op jit(solution)/shard_map/all_to_all | solution.py:288
  11.8 1.4 %copy-start = (bf16[6,8,128,128]{3,2,1,0:T(8,128)(2,1)S(1)}, bf16[6,8,128,128]{3,2,1,0:T(8,128)(2,1)}, u32[]{:S(2)}) copy-start(bf16[6,8,128,128]{3,2,1,0:T(8,128)(2,1)} %k_ref.3) | copy-start | bytes 4718596
  13.2 1.4 %copy-start.1 = (bf16[6,8,128,128]{3,2,1,0:T(8,128)(2,1)S(1)}, bf16[6,8,128,128]{3,2,1,0:T(8,128)(2,1)}, u32[]{:S(2)}) copy-start(bf16[6,8,128,128]{3,2,1,0:T(8,128)(2,1)} %v_ref.3) | copy-start | bytes 4718596
  14.6 0.7 copy-start.7
  18.7 69.2 %copy-start.3 = (f32[2,32,128]{2,1,0:T(8,128)}, f32[2,32,128]{2,1,0:T(8,128)S(1)}, u32[]{:S(2)}) copy-start(f32[2,32,128]{2,1,0:T(8,128)S(1)} %get-tuple-element.19.stats_ref) | copy-start | bytes 98308
  18.7 1.8 %collective-permute-start = (f32[2,400,128]{2,1,0:T(8,128)S(1)}, f32[2,400,128]{2,1,0:T(8,128)S(1)}, u32[]{:S(2)}, u32[]{:S(2)}) collective-permute-start(f32[2,400,128]{2,1,0:T(8,128)S(1)} %get-tuple-element.23), channel_id=1, source_target_pairs={{0,1},{1,0},{2,3},{3,2},{4,5},{5,4},{6,7},{7,6},{8,9},{9,8},{10,11... | collective-permute-start | bytes 1228808 | tf_op jit(solution)/shard_map/ppermute | solution.py:308
  21.0 16.1 %collective-permute-start.1 = (f32[400,128]{1,0:T(8,128)S(1)}, f32[400,128]{1,0:T(8,128)S(1)}, u32[]{:S(2)}, u32[]{:S(2)}) collective-permute-start(f32[400,128]{1,0:T(8,128)S(1)} %get-tuple-element.25), channel_id=1, source_target_pairs={{0,2},{1,3},{2,0},{3,1},{4,6},{5,7},{6,4},{7,5},{8,10},{9,11},{10,... | collective-permute-start | bytes 614408 | tf_op jit(solution)/shard_map/ppermute | solution.py:308
  37.3 30.6 %collective-permute-start.2 = (f32[400,128]{1,0:T(8,128)S(1)}, f32[400,128]{1,0:T(8,128)S(1)}, u32[]{:S(2)}, u32[]{:S(2)}) collective-permute-start(f32[400,128]{1,0:T(8,128)S(1)} %near.1.own), channel_id=1, source_target_pairs={{0,4},{1,5},{2,6},{3,7},{4,0},{5,1},{6,2},{7,3},{8,12},{9,13},{10,... | collective-permute-start | bytes 614408 | tf_op jit(solution)/shard_map/ppermute | solution.py:308
  68.4 19.5 %collective-permute-start.3 = (f16[384,128]{1,0:T(8,128)(2,1)S(1)}, f16[384,128]{1,0:T(8,128)(2,1)S(1)}, u32[]{:S(2)}, u32[]{:S(2)}) collective-permute-start(f16[384,128]{1,0:T(8,128)(2,1)S(1)} %get-tuple-element.32), channel_id=1, source_target_pairs={{0,8},{1,9},{2,10},{3,11},{4,12},{5,13},{6,14},{7,15},{8,0},{9,1},... | collective-permute-start | bytes 294920 | tf_op jit(solution)/shard_map/ppermute | solution.py:308
  73.0 17.7 %collective-permute-start.4 = (f32[24,128]{1,0:T(8,128)S(1)}, f32[24,128]{1,0:T(8,128)}, u32[]{:S(2)}, u32[]{:S(2)}) collective-permute-start(f32[24,128]{1,0:T(8,128)S(1)} %get-tuple-element.27.own_stats), channel_id=1, source_target_pairs={{0,8},{1,9},{2,10},{3,11},{4,12},{5,13},{6,14},{7,15},{8,0},{9,1},... | collective-permute-start | bytes 36872 | tf_op jit(solution)/shard_map/ppermute | solution.py:308
  87.9 10.5 %copy-start.4 = (f32[2,32,128]{2,1,0:T(8,128)S(1)}, f32[2,32,128]{2,1,0:T(8,128)}, u32[]{:S(2)}) copy-start(f32[2,32,128]{2,1,0:T(8,128)} %copy-done.3) | copy-start | bytes 98308
  92.4 4.8 %collective-permute-start.5 = (bf16[416,128]{1,0:T(8,128)(2,1)S(1)}, bf16[416,128]{1,0:T(8,128)(2,1)S(1)}, u32[]{:S(2)}, u32[]{:S(2)}) collective-permute-start(bf16[416,128]{1,0:T(8,128)(2,1)S(1)} %last.1.refs_0_), channel_id=1, source_target_pairs={{0,2},{1,3},{2,0},{3,1},{4,6},{5,7},{6,4},{7,5},{8,10},{9,11},{10,... | collective-permute-start | bytes 319496 | tf_op jit(solution)/shard_map/ppermute | solution.py:308
  93.9 3.2 %collective-permute-start.6 = (bf16[416,128]{1,0:T(8,128)(2,1)S(1)}, bf16[416,128]{1,0:T(8,128)(2,1)S(1)}, u32[]{:S(2)}, u32[]{:S(2)}) collective-permute-start(bf16[416,128]{1,0:T(8,128)(2,1)S(1)} %last.1.refs_0_), channel_id=1, source_target_pairs={{0,1},{1,0},{2,3},{3,2},{4,5},{5,4},{6,7},{7,6},{8,9},{9,8},{10,11... | collective-permute-start | bytes 319496 | tf_op jit(solution)/shard_map/ppermute | solution.py:308
  97.1 1.3 %collective-permute-start.7 = (bf16[416,128]{1,0:T(8,128)(2,1)S(1)}, bf16[416,128]{1,0:T(8,128)(2,1)S(1)}, u32[]{:S(2)}, u32[]{:S(2)}) collective-permute-start(bf16[416,128]{1,0:T(8,128)(2,1)S(1)} %collective-permute-done.5.refs_1_), channel_id=1, source_target_pairs={{0,1},{1,0},{2,3},{3,2},{4,5},{5,4},{6,7},{7,6},{8,9},{9,8},{10,11... | collective-permute-start | bytes 319496 | tf_op jit(solution)/shard_map/ppermute | solution.py:308

commit v3 on v2

--- a/solution.py
+++ b/solution.py
@@ -126,61 +126,59 @@
     return lax.rem(me, 2) * 2 + lax.rem(me // 2, 2)
 
 
-def merge(swap, own, got, pairs, per, own_stats=None, got_stats=None):
-    def both(rows, own=own, got=got):
-        x, y = own[rows, :], got[rows, :]
+def merge(swap, own, got, own_stats, got_stats, pairs, per, scaled):
+    def both(x, y, rows):
+        x, y = x[rows, :], y[rows, :]
         return jnp.where(swap, y, x), jnp.where(swap, x, y)
 
-    scaled = own_stats is not None
-    base = 0 if scaled else pairs * per
-    stats = (own_stats, got_stats) if scaled else (own, got)
-    peaks = both(slice(base, base + per), *stats)
-    totals = both(slice(base + per, base + 2 * per), *stats)
+    peaks = both(own_stats, got_stats, slice(0, per))
+    totals = both(own_stats, got_stats, slice(per, 2 * per))
     peak = jnp.maximum(*peaks)
     factors = [jnp.exp(x - peak) for x in peaks]
     total = factors[0] * totals[0] + factors[1] * totals[1]
     if scaled:
-        scales = both(slice(2 * per, 3 * per), *stats)
-        factors = [f * x for f, x in zip(factors, scales)]
+        factors = [f * x for f, x in zip(factors, both(own_stats, got_stats, slice(2 * per, 3 * per)))]
 
     def summed(pair):
         first, second = [jnp.broadcast_to(f[:, pair:pair + 1], (per, LANES)) for f in factors]
-        x, y = both(slice(pair * per, (pair + 1) * per))
+        x, y = both(own, got, slice(pair * per, (pair + 1) * per))
         return first * x + second * y
 
     return peak, total, summed
 
 
-def merge_kernel(bit, pairs, per, me_ref, own, got, *outs):
-    swap = lax.rem(me_ref[0] // bit, 2) == 1
-    base = pairs * per
-    for i, out in enumerate(outs):
-        x, y = (own, got) if len(outs) == 1 else (own.at[i], got.at[i])
-        peak, total, summed = merge(swap, x, y, pairs, per)
-        for pair in range(pairs):
-            out[pair * per:(pair + 1) * per, :] = summed(pair)
-        out[base:base + per, :] = peak
-        out[base + per:base + 2 * per, :] = total
-
-
-def scale_kernel(pairs, per, block, sums, stats):
+def put_scaled(peak, total, summed, pairs, per, sums, stats):
     lane = lax.broadcasted_iota(jnp.int32, (per, LANES), 1)
-    base = pairs * per
     scales = jnp.ones((per, LANES), F32)
     for pair in range(pairs):
-        x = block[pair * per:(pair + 1) * per, :]
+        x = summed(pair)
         largest = jnp.max(jnp.abs(x), axis=1, keepdims=True)
         largest = jnp.where(largest > 0.0, largest, 1.0)
         sums[pair * per:(pair + 1) * per, :] = x / largest
         scales = jnp.where(lane == pair, largest, scales)
-    stats[:2 * per, :] = block[base:base + 2 * per, :]
+    stats[:per, :] = peak
+    stats[per:2 * per, :] = total
     stats[2 * per:, :] = scales
 
 
-def last_kernel(bit, pairs, per, me_ref, own, got, own_stats, got_stats, out):
+def core_kernel(pairs, per, me_ref, own, got, *outs):
+    base = pairs * per
+    swap = lax.rem(me_ref[0], 2) == 1
+    for i in range(2):
+        x, y = own.at[i], got.at[i]
+        merged = merge(swap, x, y, x.at[pl.ds(base, 2 * per)], y.at[pl.ds(base, 2 * per)], pairs, per, False)
+        put_scaled(*merged, pairs, per, outs[2 * i], outs[2 * i + 1])
+
+
+def merge_kernel(bit, pairs, per, me_ref, own, own_stats, got, got_stats, sums, stats):
+    swap = lax.rem(me_ref[0] // bit, 2) == 1
+    put_scaled(*merge(swap, own, got, own_stats, got_stats, pairs, per, True), pairs, per, sums, stats)
+
+
+def last_kernel(bit, pairs, per, me_ref, own, own_stats, got, got_stats, out):
     swap = lax.rem(me_ref[0] // bit, 2) == 1
     base = pairs * per
-    peak, total, summed = merge(swap, own, got, pairs, per, own_stats, got_stats)
+    peak, total, summed = merge(swap, own, got, own_stats, got_stats, pairs, per, True)
     lane = lax.broadcasted_iota(jnp.int32, peak.shape, 1)
     total = jnp.where(lane < pairs, total, 1.0)
     peak = jnp.where(lane < pairs, peak, 0.0)
@@ -201,6 +199,10 @@
     packed = jnp.where(lane < half, parts[0], pltpu.roll(parts[1], half, 1))
     out[base:base + 2 * per, :] = packed.astype(BF16)
     out[base + 2 * per:base + 4 * per, :] = parts[2].astype(BF16)
+
+
+def pass_kernel(me_ref, x, out):
+    out[...] = x[...]
 
 
 def finish_kernel(pairs, per, heads, levels, me_ref, stats_ref, *refs):
@@ -318,20 +320,32 @@
             name=name,
         )(*operands)
 
-    def merged(name, bit, own, got, out_shape):
-        return local_call(functools.partial(merge_kernel, bit, pairs, per), name, out_shape, me, own, got)
-
-    block, sent = merged("core", 1, chunks[0], flip(chunks[1], 1), [block_type] * 2)
-    block, = merged("near", 2, block, flip(sent, 2), [block_type])
-    bit = levels
-    while 2 * bit < devices:
-        block, = merged("far", bit, block, flip(block, bit), [block_type])
-        bit *= 2
     sums_type = jax.ShapeDtypeStruct((rows * q_heads, width), F32)
     stats_type = jax.ShapeDtypeStruct((3 * per, width), F32)
-    sums, sum_stats = local_call(functools.partial(scale_kernel, pairs, per), "scale", [sums_type, stats_type], block)
-    sums = lax.reduce_precision(sums, 5, 10)
-    got = flip(sums.astype(jnp.float16), bit).astype(F32)
+
+    def flip_sums(sums, stats, bit):
+        return flip(sums.astype(jnp.float16), bit).astype(F32), flip(stats, bit)
+
+    def rounded(x):
+        return lax.reduce_precision(x, 5, 10)
+
+    sums, stats_own, sent, sent_stats = local_call(
+        functools.partial(core_kernel, pairs, per), "core", [sums_type, stats_type] * 2,
+        me, chunks[0], flip(chunks[1], 1),
+    )
+    bit, other = 2, flip_sums(rounded(sent), sent_stats, 2)
+    while 2 * bit < devices:
+        sums, stats_own = local_call(
+            functools.partial(merge_kernel, bit, pairs, per), "merge", [sums_type, stats_type],
+            me, sums, stats_own, *other,
+        )
+        sums, bit = rounded(sums), 2 * bit
+        other = flip_sums(sums, stats_own, bit)
+    message, = local_call(
+        functools.partial(last_kernel, bit, pairs, per), "last", [message_type], me, sums, stats_own, *other,
+    )
+    other = flip(message, 2)
+
     moved_keys, moved_values, me_next = pl.pallas_call(
         functools.partial(place_kernel, devices, group),
         out_shape=[
@@ -348,12 +362,8 @@
     )(me, table, tiles_in)
 
 
-    message, = local_call(
-        functools.partial(last_kernel, bit, pairs, per), "last", [message_type],
-        me_next, sums, got, sum_stats, flip(sum_stats, bit),
-    )
-    other = flip(message, 2)
-    arrived = [message, other, flip(message, 1), flip(other, 1)]
+    other_next, = local_call(pass_kernel, "pass", [message_type], me_next, other)
+    arrived = [message, other, flip(message, 1), flip(other_next, 1)]
 
     attn_out, mass = pl.pallas_call(
         functools.partial(finish_kernel, pairs, per, heads, levels),

time: 100 us -> 96.9 us (0.969)
  waiting for transfers between devices: 65.4 us -> 51.7 us
  Pallas kernels: 13.8 us -> 21.7 us
  starting transfers between devices: 16.3 us -> 18.5 us
    ppermute x8 -> x10, waiting for transfers between devices: 65.4 us -> 51.7 us  [flip(): return lax.ppermute(x, 'ctx', [(i, i ^ bit) for i in range(devices)])]
    pallas_call x5, Pallas kernels: 2.67 us -> 10.6 us  [local_call(): pl.pallas_call(kernel, out_shape=out_shape, in_specs=[SMEM if x is me or...]
    ppermute x8 -> x10, starting transfers between devices: 8.72 us -> 11 us  [flip(): return lax.ppermute(x, 'ctx', [(i, i ^ bit) for i in range(devices)])]
  transfers between devices with their start and end apart: 9 -> 11, of which waited for: 6 -> 9; matrix products, arithmetic and copies ran while one was open for 0% -> 0% of each run, Pallas kernels for 7% -> 17%
where the time goes in v3:
time: 96.9 us; the launch traced here: 96.6 us
  waiting for transfers between devices  51.7 us (53%)
  Pallas kernels  21.7 us (22%)
  starting transfers between devices  18.5 us (19%)
  local copies, waits for them, and re-layouts  3.5 us (4%)
    ppermute x10, waiting for transfers between devices, flip(): return lax.ppermute(x, 'ctx', [(i, i ^ bit) for i in range(devices)])  51.7 us
    ppermute x10, starting transfers between devices, flip(): return lax.ppermute(x, 'ctx', [(i, i ^ bit) for i in range(devices)])  11 us
    pallas_call x5, Pallas kernels, local_call(): pl.pallas_call(kernel, out_shape=out_shape, in_specs=[SMEM if x is me or...  10.6 us
    all_to_all x1, starting transfers between devices, local(): lax.all_to_all(tiles_out, 'ctx', split_axis=0, concat_axis=0, tiled=True)  7.52 us
    pallas_call x1, Pallas kernels, local(): pl.pallas_call(functools.partial(stage_kernel, devices, group), out_shape...  3.51 us
    unnamed x16, local copies, waits for them, and re-layouts  3.5 us
    pallas_call x1, Pallas kernels, local(): pl.pallas_call(functools.partial(attend_kernel, levels), out_shape=[jax.S...  3.47 us
    pallas_call x1, Pallas kernels, local(): pl.pallas_call(functools.partial(place_kernel, devices, group), out_shape...  2.7 us
  transfers between devices with their start and end apart: 11, of which 9 were waited for; matrix products, arithmetic and copies ran while one was open for 0% of the time, Pallas kernels for 17%

profile of v3, /device:TPU:0, one launch (start us, length us, event | category | flops | bytes accessed | tf_op | source)
XLA Modules:
  0.0 96.6 jit_solution(6020165626762651199)
XLA Ops:
  0.6 3.5 %stage.1 = (bf16[48,2,128,128]{3,2,1,0:T(8,128)(2,1)}, s32[48]{0:T(128)}) custom-call(s32[1]{0:T(128)} %bitcast.me_ref, s32[6,8,16]{2,1,0:T(8,128)} %dest_hbm.1, bf16[6,8,128,128]{3,2,1,0:T(8,128)(2,1)} %k_ref.3, bf16[6,8,128,128]{3,2,1,0:T(8,128)(2,1)} %v_ref.3), custom_call_target="tpu_custom_call" | custom-call | flops 1000 | bytes 1000 | tf_op jit(solution)/shard_map/stage/pallas_call | solution.py:273
  4.2 0.0 copy-start.2
  4.2 0.0 copy-start.5
  4.2 0.0 copy-start.6
  4.2 7.5 %all-to-all-start = ((bf16[48,2,128,128]{3,2,1,0:T(8,128)(2,1)}), bf16[48,2,128,128]{3,2,1,0:T(8,128)(2,1)S(1)}, u32[]{:S(2)}, u32[]{:S(2)}) async-start(bf16[48,2,128,128]{3,2,1,0:T(8,128)(2,1)} %get-tuple-element.34), calls=%async_computation | async-start | bytes 6291456 | tf_op jit(solution)/shard_map/all_to_all | solution.py:290
  11.7 0.0 copy-done.2
  11.7 0.0 copy-done.5
  11.7 0.0 copy-done.6
  11.8 0.0 copy-start
  11.8 1.4 %copy-done = bf16[6,8,128,128]{3,2,1,0:T(8,128)(2,1)S(1)} copy-done((bf16[6,8,128,128]{3,2,1,0:T(8,128)(2,1)S(1)}, bf16[6,8,128,128]{3,2,1,0:T(8,128)(2,1)}, u32[]{:S(2)}) %copy-start) | copy-done | bytes 1572888
  13.2 1.4 %copy-done.1 = bf16[6,8,128,128]{3,2,1,0:T(8,128)(2,1)S(1)} copy-done((bf16[6,8,128,128]{3,2,1,0:T(8,128)(2,1)S(1)}, bf16[6,8,128,128]{3,2,1,0:T(8,128)(2,1)}, u32[]{:S(2)}) %copy-start.1) | copy-done | bytes 1572888
  14.6 0.7 copy-done.7
  15.2 3.5 %attend.1 = (f32[2,32,128]{2,1,0:T(8,128)S(1)}, f32[2,400,128]{2,1,0:T(8,128)S(1)}, f32[2,400,128]{2,1,0:T(8,128)S(1)}) custom-call(s32[1]{0:T(128)} %bitcast.me_ref, s32[48]{0:T(128)S(1)} %copy-done.6, s32[6]{0:T(128)S(1)} %copy-done.7, s32[6,4,16]{2,1,0:T(4,128)S(1)} %bitcast.4, bf16[4,6,64,128]{3,2,1,0:T(8,128)(2,1)S(1)} %copy-done.2, ...), custom_call_target="tpu_custom_call" | custom-call | flops 1000 | bytes 1000 | tf_op jit(solution)/shard_map/attend/pallas_call | solution.py:292
  18.7 0.0 copy-start.3
  18.7 0.5 collective-permute-start
  19.2 1.4 %collective-permute-done.got = f32[2,400,128]{2,1,0:T(8,128)S(1)} collective-permute-done((f32[2,400,128]{2,1,0:T(8,128)S(1)}, f32[2,400,128]{2,1,0:T(8,128)S(1)}, u32[]{:S(2)}, u32[]{:S(2)}) %collective-permute-start) | collective-permute-done | bytes 409632 | tf_op jit(solution)/shard_map/ppermute | solution.py:310
  20.6 5.0 %core.1 = (f32[384,128]{1,0:T(8,128)S(1)}, f32[24,128]{1,0:T(8,128)S(1)}, f32[384,128]{1,0:T(8,128)S(1)}, f32[24,128]{1,0:T(8,128)S(1)}) custom-call(s32[1]{0:T(128)} %bitcast.me_ref, f32[2,400,128]{2,1,0:T(8,128)S(1)} %get-tuple-element.24.own, f32[2,400,128]{2,1,0:T(8,128)S(1)} %collective-permute-done.got), custom_call_target="tpu_custom_call" | custom-call | flops 1000 | bytes 1000 | tf_op jit(solution)/shard_map/core/pallas_call | solution.py:313
  25.6 0.1 reduce-precision_convert_fusion
  25.7 2.0 %collective-permute-start.1 = (f16[384,128]{1,0:T(8,128)(2,1)S(1)}, f16[384,128]{1,0:T(8,128)(2,1)S(1)}, u32[]{:S(2)}, u32[]{:S(2)}) collective-permute-start(f16[384,128]{1,0:T(8,128)(2,1)S(1)} %reduce-precision_convert_fusion), channel_id=1, source_target_pairs={{0,2},{1,3},{2,0},{3,1},{4,6},{5,7},{6,4},{7,5},{8,10},{9,11},{10,... | collective-permute-start | bytes 294920 | tf_op jit(solution)/shard_map/ppermute | solution.py:310
  27.6 0.1 collective-permute-start.2
  27.8 7.3 %collective-permute-done.1 = f16[384,128]{1,0:T(8,128)(2,1)S(1)} collective-permute-done((f16[384,128]{1,0:T(8,128)(2,1)S(1)}, f16[384,128]{1,0:T(8,128)(2,1)S(1)}, u32[]{:S(2)}, u32[]{:S(2)}) %collective-permute-start.1) | collective-permute-done | bytes 98336 | tf_op jit(solution)/shard_map/ppermute | solution.py:310
  35.1 0.1 collective-permute-done.2.got_stats
  35.2 2.3 %merge.2 = (f32[384,128]{1,0:T(8,128)S(1)}, f32[24,128]{1,0:T(8,128)S(1)}) custom-call(s32[1]{0:T(128)} %bitcast.me_ref, f32[384,128]{1,0:T(8,128)S(1)} %get-tuple-element.26.own, f32[24,128]{1,0:T(8,128)S(1)} %get-tuple-element.27.own_stats, f32[384,128]{1,0:T(8,128)S(1)} %convert_element_type.19.got, f32[24,128]{1,0:T(8,128)S(1)} %collective-permute-done.2.got_stats), custom_call_target="tpu_custom_call" | custom-call | flops 1000 | bytes 1000 | tf_op jit(solution)/shard_map/merge/pallas_call | solution.py:313
  37.5 0.1 reduce-precision_convert_fusion.2
  37.7 0.4 collective-permute-start.3
  38.1 1.7 %collective-permute-start.4 = (f32[24,128]{1,0:T(8,128)S(1)}, f32[24,128]{1,0:T(8,128)S(1)}, u32[]{:S(2)}, u32[]{:S(2)}) collective-permute-start(f32[24,128]{1,0:T(8,128)S(1)} %get-tuple-element.31.own_stats), channel_id=1, source_target_pairs={{0,4},{1,5},{2,6},{3,7},{4,0},{5,1},{6,2},{7,3},{8,12},{9,13},{10,... | collective-permute-start | bytes 36872 | tf_op jit(solution)/shard_map/ppermute | solution.py:310
  39.8 26.0 %collective-permute-done.3 = f16[384,128]{1,0:T(8,128)(2,1)S(1)} collective-permute-done((f16[384,128]{1,0:T(8,128)(2,1)S(1)}, f16[384,128]{1,0:T(8,128)(2,1)S(1)}, u32[]{:S(2)}, u32[]{:S(2)}) %collective-permute-start.3) | collective-permute-done | bytes 98336 | tf_op jit(solution)/shard_map/ppermute | solution.py:310
  65.8 0.1 collective-permute-done.4.got_stats
  65.9 2.3 %merge.3 = (f32[384,128]{1,0:T(8,128)S(1)}, f32[24,128]{1,0:T(8,128)S(1)}) custom-call(s32[1]{0:T(128)} %bitcast.me_ref, f32[384,128]{1,0:T(8,128)S(1)} %get-tuple-element.43.own, f32[24,128]{1,0:T(8,128)S(1)} %get-tuple-element.31.own_stats, f32[384,128]{1,0:T(8,128)S(1)} %convert_element_type.21.got, f32[24,128]{1,0:T(8,128)S(1)} %collective-permute-done.4.got_stats), custom_call_target="tpu_custom_call" | custom-call | flops 1000 | bytes 1000 | tf_op jit(solution)/shard_map/merge/pallas_call | solution.py:313
  68.1 0.1 reduce-precision_convert_fusion.1
  68.3 0.0 copy-done.3
  68.3 4.6 %collective-permute-start.5 = (f16[384,128]{1,0:T(8,128)(2,1)S(1)}, f16[384,128]{1,0:T(8,128)(2,1)S(1)}, u32[]{:S(2)}, u32[]{:S(2)}) collective-permute-start(f16[384,128]{1,0:T(8,128)(2,1)S(1)} %get-tuple-element.40), channel_id=1, source_target_pairs={{0,8},{1,9},{2,10},{3,11},{4,12},{5,13},{6,14},{7,15},{8,0},{9,1},... | collective-permute-start | bytes 294920 | tf_op jit(solution)/shard_map/ppermute | solution.py:310
  72.9 0.1 collective-permute-start.6
  73.0 14.9 %collective-permute-done.5 = f16[384,128]{1,0:T(8,128)(2,1)S(1)} collective-permute-done((f16[384,128]{1,0:T(8,128)(2,1)S(1)}, f16[384,128]{1,0:T(8,128)(2,1)S(1)}, u32[]{:S(2)}, u32[]{:S(2)}) %collective-permute-start.5) | collective-permute-done | bytes 98336 | tf_op jit(solution)/shard_map/ppermute | solution.py:310
  87.9 0.1 collective-permute-done.6.got_stats
  88.0 0.3 last.1.refs_0_
  88.4 0.0 copy-start.4
  88.4 1.6 %collective-permute-start.7 = (bf16[416,128]{1,0:T(8,128)(2,1)S(1)}, bf16[416,128]{1,0:T(8,128)(2,1)S(1)}, u32[]{:S(2)}, u32[]{:S(2)}) collective-permute-start(bf16[416,128]{1,0:T(8,128)(2,1)S(1)} %last.1.refs_0_), channel_id=1, source_target_pairs={{0,2},{1,3},{2,0},{3,1},{4,6},{5,7},{6,4},{7,5},{8,10},{9,11},{10,... | collective-permute-start | bytes 319496 | tf_op jit(solution)/shard_map/ppermute | solution.py:310
  89.9 0.0 collective-permute-start.8
  90.0 0.0 all-to-all-done.got_ref
  90.0 2.7 %place.1 = (bf16[6,8,128,128]{3,2,1,0:T(8,128)(2,1)}, bf16[6,8,128,128]{3,2,1,0:T(8,128)(2,1)}, s32[1]{0:T(128)}) custom-call(s32[1]{0:T(128)} %bitcast.me_ref, s32[48]{0:T(128)S(1)} %copy-done.6, bf16[48,2,128,128]{3,2,1,0:T(8,128)(2,1)S(1)} %all-to-all-done.got_ref), custom_call_target="tpu_custom_call" | custom-call | flops 1000 | bytes 1000 | tf_op jit(solution)/shard_map/place/pallas_call | solution.py:349
  92.7 0.5 collective-permute-done.7.x.refs_1_
  93.1 0.7 pass.1
  93.8 0.1 collective-permute-start.9
  93.9 0.0 collective-permute-done.8.refs_2_
  93.9 1.3 %collective-permute-done.9.refs_3_ = bf16[416,128]{1,0:T(8,128)(2,1)S(1)} collective-permute-done((bf16[416,128]{1,0:T(8,128)(2,1)S(1)}, bf16[416,128]{1,0:T(8,128)(2,1)S(1)}, u32[]{:S(2)}, u32[]{:S(2)}) %collective-permute-start.9) | collective-permute-done | bytes 106528 | tf_op jit(solution)/shard_map/ppermute | solution.py:310
  95.2 0.0 copy-done.4
  95.2 1.4 %finish.1 = (bf16[4,384,128]{2,1,0:T(8,128)(2,1)}, f32[6,1,8]{2,1,0:T(1,128)}) custom-call(s32[1]{0:T(128)} %bitcast.me_ref, f32[2,32,128]{2,1,0:T(8,128)S(1)} %copy-done.4, bf16[416,128]{1,0:T(8,128)(2,1)S(1)} %last.1.refs_0_, bf16[416,128]{1,0:T(8,128)(2,1)S(1)} %collective-permute-done.7.x.refs_1_, bf16[416,128]{1,0:T(8,128)(2,1)S(1)} %collective-permute-done.8.refs_2_, ...), custom_call_target="tpu_custom_call" | custom-call | flops 1000 | bytes 1000 | tf_op jit(solution)/shard_map/finish/pallas_call | solution.py:368
  (5 shorter events, 0.0 us)
Async XLA Ops:
  4.2 7.6 %copy-start.2 = (bf16[4,6,64,128]{3,2,1,0:T(8,128)(2,1)S(1)}, bf16[4,6,64,128]{3,2,1,0:T(8,128)(2,1)}, u32[]{:S(2)}) copy-start(bf16[4,6,64,128]{3,2,1,0:T(8,128)(2,1)} %q_ref.1) | copy-start | bytes 1179652
  4.2 7.6 %copy-start.5 = (s32[4,6,16]{2,0,1:T(4,128)S(1)}, s32[4,6,16]{2,0,1:T(4,128)}, u32[]{:S(2)}) copy-start(s32[4,6,16]{2,0,1:T(4,128)} %param.10) | copy-start | bytes 4612
  4.2 7.6 %copy-start.6 = (s32[48]{0:T(128)S(1)}, s32[48]{0:T(128)}, u32[]{:S(2)}) copy-start(s32[48]{0:T(128)} %get-tuple-element.22.table) | copy-start | bytes 580
  4.2 85.8 %all-to-all-start = ((bf16[48,2,128,128]{3,2,1,0:T(8,128)(2,1)}), bf16[48,2,128,128]{3,2,1,0:T(8,128)(2,1)S(1)}, u32[]{:S(2)}, u32[]{:S(2)}) async-start(bf16[48,2,128,128]{3,2,1,0:T(8,128)(2,1)} %get-tuple-element.34), calls=%async_computation | async-start | bytes 6291456 | tf_op jit(solution)/shard_map/all_to_all | solution.py:290
  11.8 1.4 %copy-start = (bf16[6,8,128,128]{3,2,1,0:T(8,128)(2,1)S(1)}, bf16[6,8,128,128]{3,2,1,0:T(8,128)(2,1)}, u32[]{:S(2)}) copy-start(bf16[6,8,128,128]{3,2,1,0:T(8,128)(2,1)} %k_ref.3) | copy-start | bytes 4718596
  13.2 1.4 %copy-start.1 = (bf16[6,8,128,128]{3,2,1,0:T(8,128)(2,1)S(1)}, bf16[6,8,128,128]{3,2,1,0:T(8,128)(2,1)}, u32[]{:S(2)}) copy-start(bf16[6,8,128,128]{3,2,1,0:T(8,128)(2,1)} %v_ref.3) | copy-start | bytes 4718596
  14.6 0.7 copy-start.7
  18.7 49.6 %copy-start.3 = (f32[2,32,128]{2,1,0:T(8,128)}, f32[2,32,128]{2,1,0:T(8,128)S(1)}, u32[]{:S(2)}) copy-start(f32[2,32,128]{2,1,0:T(8,128)S(1)} %get-tuple-element.23.stats_ref) | copy-start | bytes 98308
  18.7 1.8 %collective-permute-start = (f32[2,400,128]{2,1,0:T(8,128)S(1)}, f32[2,400,128]{2,1,0:T(8,128)S(1)}, u32[]{:S(2)}, u32[]{:S(2)}) collective-permute-start(f32[2,400,128]{2,1,0:T(8,128)S(1)} %get-tuple-element.25), channel_id=1, source_target_pairs={{0,1},{1,0},{2,3},{3,2},{4,5},{5,4},{6,7},{7,6},{8,9},{9,8},{10,11... | collective-permute-start | bytes 1228808 | tf_op jit(solution)/shard_map/ppermute | solution.py:310
  25.7 9.4 %collective-permute-start.1 = (f16[384,128]{1,0:T(8,128)(2,1)S(1)}, f16[384,128]{1,0:T(8,128)(2,1)S(1)}, u32[]{:S(2)}, u32[]{:S(2)}) collective-permute-start(f16[384,128]{1,0:T(8,128)(2,1)S(1)} %reduce-precision_convert_fusion), channel_id=1, source_target_pairs={{0,2},{1,3},{2,0},{3,1},{4,6},{5,7},{6,4},{7,5},{8,10},{9,11},{10,... | collective-permute-start | bytes 294920 | tf_op jit(solution)/shard_map/ppermute | solution.py:310
  27.6 7.6 %collective-permute-start.2 = (f32[24,128]{1,0:T(8,128)S(1)}, f32[24,128]{1,0:T(8,128)S(1)}, u32[]{:S(2)}, u32[]{:S(2)}) collective-permute-start(f32[24,128]{1,0:T(8,128)S(1)} %get-tuple-element.29), channel_id=1, source_target_pairs={{0,2},{1,3},{2,0},{3,1},{4,6},{5,7},{6,4},{7,5},{8,10},{9,11},{10,... | collective-permute-start | bytes 36872 | tf_op jit(solution)/shard_map/ppermute | solution.py:310
  37.7 28.1 %collective-permute-start.3 = (f16[384,128]{1,0:T(8,128)(2,1)S(1)}, f16[384,128]{1,0:T(8,128)(2,1)S(1)}, u32[]{:S(2)}, u32[]{:S(2)}) collective-permute-start(f16[384,128]{1,0:T(8,128)(2,1)S(1)} %get-tuple-element.42), channel_id=1, source_target_pairs={{0,4},{1,5},{2,6},{3,7},{4,0},{5,1},{6,2},{7,3},{8,12},{9,13},{10,... | collective-permute-start | bytes 294920 | tf_op jit(solution)/shard_map/ppermute | solution.py:310
  38.1 27.8 %collective-permute-start.4 = (f32[24,128]{1,0:T(8,128)S(1)}, f32[24,128]{1,0:T(8,128)S(1)}, u32[]{:S(2)}, u32[]{:S(2)}) collective-permute-start(f32[24,128]{1,0:T(8,128)S(1)} %get-tuple-element.31.own_stats), channel_id=1, source_target_pairs={{0,4},{1,5},{2,6},{3,7},{4,0},{5,1},{6,2},{7,3},{8,12},{9,13},{10,... | collective-permute-start | bytes 36872 | tf_op jit(solution)/shard_map/ppermute | solution.py:310
  68.3 19.6 %collective-permute-start.5 = (f16[384,128]{1,0:T(8,128)(2,1)S(1)}, f16[384,128]{1,0:T(8,128)(2,1)S(1)}, u32[]{:S(2)}, u32[]{:S(2)}) collective-permute-start(f16[384,128]{1,0:T(8,128)(2,1)S(1)} %get-tuple-element.40), channel_id=1, source_target_pairs={{0,8},{1,9},{2,10},{3,11},{4,12},{5,13},{6,14},{7,15},{8,0},{9,1},... | collective-permute-start | bytes 294920 | tf_op jit(solution)/shard_map/ppermute | solution.py:310
  72.9 15.2 %collective-permute-start.6 = (f32[24,128]{1,0:T(8,128)S(1)}, f32[24,128]{1,0:T(8,128)S(1)}, u32[]{:S(2)}, u32[]{:S(2)}) collective-permute-start(f32[24,128]{1,0:T(8,128)S(1)} %get-tuple-element.33.own_stats), channel_id=1, source_target_pairs={{0,8},{1,9},{2,10},{3,11},{4,12},{5,13},{6,14},{7,15},{8,0},{9,1},... | collective-permute-start | bytes 36872 | tf_op jit(solution)/shard_map/ppermute | solution.py:310
  88.4 6.8 %copy-start.4 = (f32[2,32,128]{2,1,0:T(8,128)S(1)}, f32[2,32,128]{2,1,0:T(8,128)}, u32[]{:S(2)}) copy-start(f32[2,32,128]{2,1,0:T(8,128)} %copy-done.3) | copy-start | bytes 98308
  88.4 4.8 %collective-permute-start.7 = (bf16[416,128]{1,0:T(8,128)(2,1)S(1)}, bf16[416,128]{1,0:T(8,128)(2,1)S(1)}, u32[]{:S(2)}, u32[]{:S(2)}) collective-permute-start(bf16[416,128]{1,0:T(8,128)(2,1)S(1)} %last.1.refs_0_), channel_id=1, source_target_pairs={{0,2},{1,3},{2,0},{3,1},{4,6},{5,7},{6,4},{7,5},{8,10},{9,11},{10,... | collective-permute-start | bytes 319496 | tf_op jit(solution)/shard_map/ppermute | solution.py:310
  89.9 4.0 %collective-permute-start.8 = (bf16[416,128]{1,0:T(8,128)(2,1)S(1)}, bf16[416,128]{1,0:T(8,128)(2,1)S(1)}, u32[]{:S(2)}, u32[]{:S(2)}) collective-permute-start(bf16[416,128]{1,0:T(8,128)(2,1)S(1)} %last.1.refs_0_), channel_id=1, source_target_pairs={{0,1},{1,0},{2,3},{3,2},{4,5},{5,4},{6,7},{7,6},{8,9},{9,8},{10,11... | collective-permute-start | bytes 319496 | tf_op jit(solution)/shard_map/ppermute | solution.py:310
  93.8 1.4 %collective-permute-start.9 = (bf16[416,128]{1,0:T(8,128)(2,1)S(1)}, bf16[416,128]{1,0:T(8,128)(2,1)S(1)}, u32[]{:S(2)}, u32[]{:S(2)}) collective-permute-start(bf16[416,128]{1,0:T(8,128)(2,1)S(1)} %pass.1), channel_id=1, source_target_pairs={{0,1},{1,0},{2,3},{3,2},{4,5},{5,4},{6,7},{7,6},{8,9},{9,8},{10,11... | collective-permute-start | bytes 319496 | tf_op jit(solution)/shard_map/ppermute | solution.py:310

commit v4 on v2

--- a/solution.py
+++ b/solution.py
@@ -22,7 +22,9 @@
 COST = pl.CostEstimate(flops=1000, bytes_accessed=1000, transcendentals=0)
 
 
-def stage_kernel(devices, group, me_ref, dest_hbm, k_ref, v_ref, buf, table, k_vm, v_vm, dest, counts, sem, load_sem):
+def stage_kernel(
+    devices, group, first, me_ref, dest_hbm, k_ref, v_ref, buf, buf_rest, table, k_vm, v_vm, dest, counts, sem, load_sem
+):
     rows, heads = k_ref.shape[:2]
     small = pltpu.make_async_copy(dest_hbm, dest, sem.at[0])
     small.start()
@@ -46,14 +48,26 @@
         loads[2 * row].wait()
         loads[2 * row + 1].wait()
 
-        for head in range(heads):
+        def send(head, carry):
             offset = dest[row, head, 0]
             rank = counts[offset]
             counts[offset] = rank + 1
             table[offset * group + rank] = row * heads + head
-            slot = jnp.bitwise_and(me + offset, devices - 1) * group + rank
-            pltpu.make_async_copy(k_vm.at[row, head], buf.at[slot, 0], sem.at[1]).start()
-            pltpu.make_async_copy(v_vm.at[row, head], buf.at[slot, 1], sem.at[2]).start()
+            target = jnp.bitwise_and(me + offset, devices - 1)
+            pltpu.make_async_copy(k_vm.at[row, head], buf.at[target * first + rank], sem.at[1]).start()
+
+            @pl.when(rank < first - group)
+            def _():
+                at = target * first + group + rank
+                pltpu.make_async_copy(v_vm.at[row, head], buf.at[at], sem.at[2]).start()
+
+            @pl.when(rank >= first - group)
+            def _():
+                at = target * (2 * group - first) + rank + group - first
+                pltpu.make_async_copy(v_vm.at[row, head], buf_rest.at[at], sem.at[2]).start()
+            return carry
+
+        lax.fori_loop(0, heads, send, 0)
     pltpu.make_async_copy(k_ref, k_vm, sem.at[1]).wait()
     pltpu.make_async_copy(v_ref, v_vm, sem.at[2]).wait()
 
@@ -231,23 +245,33 @@
         copy.wait()
 
 
-def place_kernel(devices, group, me_ref, table, got_ref, k_ref, v_ref, me_out, sem):
-    heads = k_ref.shape[1]
+def place_keys_kernel(devices, group, first, me_ref, table, got, out, sem):
+    heads = out.shape[1]
     me = me_ref[0]
-    me_out[0] = me
     for offset in range(devices):
         source = jnp.bitwise_and(me + devices - offset, devices - 1)
         for k in range(group):
-            pair = table[offset * group + k]
-
-            @pl.when(pair >= 0)
-            def _():
-                row, head = pair // heads, lax.rem(pair, heads)
-                for which, ref in enumerate((k_ref, v_ref)):
-                    src = got_ref.at[source * group + k, which]
-                    pltpu.make_async_copy(src, ref.at[row, head], sem.at[which]).start()
-    pltpu.make_async_copy(k_ref, k_ref, sem.at[0]).wait()
-    pltpu.make_async_copy(v_ref, v_ref, sem.at[1]).wait()
+            put(got.at[source * first + k], table[offset * group + k], heads, out, sem)
+    pltpu.make_async_copy(out, out, sem).wait()
+
+
+def place_values_kernel(devices, group, first, me_ref, table, got, got_rest, out, sem):
+    heads = out.shape[1]
+    me = me_ref[0]
+    rest = 2 * group - first
+    for offset in range(devices):
+        source = jnp.bitwise_and(me + devices - offset, devices - 1)
+        for k in range(group):
+            at = group + k
+            src = got.at[source * first + at] if at < first else got_rest.at[source * rest + at - first]
+            put(src, table[offset * group + k], heads, out, sem)
+    pltpu.make_async_copy(out, out, sem).wait()
+
+
+def put(src, pair, heads, out, sem):
+    @pl.when(pair >= 0)
+    def _():
+        pltpu.make_async_copy(src, out.at[pair // heads, lax.rem(pair, heads)], sem).start()
 
 
 def local(queries, key_cache, value_cache, row_lengths, kept_tiles, tile_dest):
@@ -266,13 +290,23 @@
     block_rows = rows * q_heads + 2 * per
     block_type = jax.ShapeDtypeStruct((block_rows, width), F32)
     message_type = jax.ShapeDtypeStruct((rows * q_heads + 4 * per, width), BF16)
-    tiles_type = jax.ShapeDtypeStruct((devices * group, 2, span, width), BF16)
-
-    tiles_out, table = pl.pallas_call(
-        functools.partial(stage_kernel, devices, group),
-        out_shape=[tiles_type, jax.ShapeDtypeStruct((devices * group,), jnp.int32)],
+    first = 2 * group - max(1, 2 * group // 3)
+
+    def tiles_type(count):
+        return jax.ShapeDtypeStruct((devices * count, span, width), BF16)
+
+    def exchange(x):
+        return lax.all_to_all(x, "ctx", split_axis=0, concat_axis=0, tiled=True)
+
+
+    tiles_out, rest_out, table = pl.pallas_call(
+        functools.partial(stage_kernel, devices, group, first),
+        out_shape=[
+            tiles_type(first), tiles_type(2 * group - first),
+            jax.ShapeDtypeStruct((devices * group,), jnp.int32),
+        ],
         in_specs=[SMEM, HBM, HBM, HBM],
-        out_specs=[HBM, SMEM],
+        out_specs=[HBM, HBM, SMEM],
         scratch_shapes=[
             pltpu.VMEM(key_cache.shape, BF16),
             pltpu.VMEM(value_cache.shape, BF16),
@@ -285,7 +319,7 @@
         cost_estimate=COST,
         name="stage",
     )(me, tile_dest, key_cache, value_cache)
-    tiles_in = lax.all_to_all(tiles_out, "ctx", split_axis=0, concat_axis=0, tiled=True)
+    tiles_in = exchange(tiles_out)
 
     stats, *chunks = pl.pallas_call(
         functools.partial(attend_kernel, levels),
@@ -332,27 +366,28 @@
     sums, sum_stats = local_call(functools.partial(scale_kernel, pairs, per), "scale", [sums_type, stats_type], block)
     sums = lax.reduce_precision(sums, 5, 10)
     got = flip(sums.astype(jnp.float16), bit).astype(F32)
-    moved_keys, moved_values, me_next = pl.pallas_call(
-        functools.partial(place_kernel, devices, group),
-        out_shape=[
-            jax.ShapeDtypeStruct(key_cache.shape, BF16),
-            jax.ShapeDtypeStruct(value_cache.shape, BF16),
-            jax.ShapeDtypeStruct((1,), jnp.int32),
-        ],
-        in_specs=[SMEM, SMEM, ANY],
-        out_specs=[HBM, HBM, SMEM],
-        scratch_shapes=[pltpu.SemaphoreType.DMA((2,))],
-        compiler_params=PARAMS,
-        cost_estimate=COST,
-        name="place",
-    )(me, table, tiles_in)
-
-
+    got, rest_out = lax.optimization_barrier((got, rest_out))
+    rest_in = exchange(rest_out)
     message, = local_call(
         functools.partial(last_kernel, bit, pairs, per), "last", [message_type],
-        me_next, sums, got, sum_stats, flip(sum_stats, bit),
+        me, sums, got, sum_stats, flip(sum_stats, bit),
     )
     other = flip(message, 2)
+
+    def place(kernel, name, *got):
+        return pl.pallas_call(
+            functools.partial(kernel, devices, group, first),
+            out_shape=jax.ShapeDtypeStruct(key_cache.shape, BF16),
+            in_specs=[SMEM, SMEM] + [ANY] * len(got),
+            out_specs=HBM,
+            scratch_shapes=[pltpu.SemaphoreType.DMA],
+            compiler_params=PARAMS,
+            cost_estimate=COST,
+            name=name,
+        )(me, table, *got)
+
+    moved_keys = place(place_keys_kernel, "place_keys", tiles_in)
+    moved_values = place(place_values_kernel, "place_values", tiles_in, rest_in)
     arrived = [message, other, flip(message, 1), flip(other, 1)]
 
     attn_out, mass = pl.pallas_call(

time: 100 us -> 108 us (1.080)
  starting transfers between devices: 16.3 us -> 22.7 us
  waiting for transfers between devices: 65.4 us -> 67.5 us
    all_to_all x1 -> x2, starting transfers between devices: 7.53 us -> 11.2 us  [exchange(): return lax.all_to_all(x, 'ctx', split_axis=0, concat_axis=0, tiled=True)]
    ppermute x8, starting transfers between devices: 8.72 us -> 11.4 us  [flip(): return lax.ppermute(x, 'ctx', [(i, i ^ bit) for i in range(devices)])]
    ppermute x8, waiting for transfers between devices: 65.4 us -> 67.5 us  [flip(): return lax.ppermute(x, 'ctx', [(i, i ^ bit) for i in range(devices)])]
    pallas_call x5, Pallas kernels: 2.67 us -> 1.31 us  [local_call(): pl.pallas_call(kernel, out_shape=out_shape, in_specs=[SMEM if x is me or...]
    pallas_call x2 -> x3, Pallas kernels: 6.21 us -> 6.82 us  [the longest x1 3.48 us: local(): pl.pallas_call(functools.partial(stage_kernel, devices, group, first), ou...]
  transfers between devices with their start and end apart: 9 -> 10, of which waited for: 6 -> 7; matrix products, arithmetic and copies ran while one was open for 0% -> 0% of each run, Pallas kernels for 7% -> 7%
where the time goes in v4:
time: 108 us
  waiting for transfers between devices  67.5 us (62%)
  starting transfers between devices  22.7 us (21%)
  Pallas kernels  13 us (12%)
  local copies, waits for them, and re-layouts  3.6 us (3%)
    ppermute x8, waiting for transfers between devices, flip(): return lax.ppermute(x, 'ctx', [(i, i ^ bit) for i in range(devices)])  67.5 us
    ppermute x8, starting transfers between devices, flip(): return lax.ppermute(x, 'ctx', [(i, i ^ bit) for i in range(devices)])  11.4 us
    all_to_all x2, starting transfers between devices, exchange(): return lax.all_to_all(x, 'ctx', split_axis=0, concat_axis=0, tiled=True)  11.2 us
    unnamed x16, local copies, waits for them, and re-layouts  3.6 us
    pallas_call x1, Pallas kernels, local(): pl.pallas_call(functools.partial(stage_kernel, devices, group, first), ou...  3.48 us
    pallas_call x1, Pallas kernels, local(): pl.pallas_call(functools.partial(attend_kernel, levels), out_shape=[jax.S...  3.47 us
    pallas_call x2, Pallas kernels, place(): pl.pallas_call(functools.partial(kernel, devices, group, first), out_shap...  3.34 us
  transfers between devices with their start and end apart: 10, of which 7 were waited for; matrix products, arithmetic and copies ran while one was open for 0% of the time, Pallas kernels for 7%

profile of v4, /device:TPU:0, one launch (start us, length us, event | category | flops | bytes accessed | tf_op | source)
XLA Modules:
  0.0 107.8 jit_solution(6748200668534608378)
XLA Ops:
  0.6 3.5 %stage.1 = (bf16[64,128,128]{2,1,0:T(8,128)(2,1)}, bf16[32,128,128]{2,1,0:T(8,128)(2,1)}, s32[48]{0:T(128)}) custom-call(s32[1]{0:T(128)} %bitcast.me_ref, s32[6,8,16]{2,1,0:T(8,128)} %dest_hbm.1, bf16[6,8,128,128]{3,2,1,0:T(8,128)(2,1)} %k_ref.3, bf16[6,8,128,128]{3,2,1,0:T(8,128)(2,1)} %v_ref.3), custom_call_target="tpu_custom_call" | custom-call | flops 1000 | bytes 1000 | tf_op jit(solution)/shard_map/stage/pallas_call | solution.py:302
  4.1 0.0 copy-start.2
  4.1 0.0 copy-start.5
  4.1 0.0 copy-start.6
  4.2 0.0 copy-start.7
  4.2 7.5 %all-to-all-start = ((bf16[64,128,128]{2,1,0:T(8,128)(2,1)}), bf16[64,128,128]{2,1,0:T(8,128)(2,1)S(1)}, u32[]{:S(2)}, u32[]{:S(2)}) async-start(bf16[64,128,128]{2,1,0:T(8,128)(2,1)} %get-tuple-element.30), calls=%async_computation | async-start | bytes 4194304 | tf_op jit(solution)/shard_map/all_to_all | solution.py:299
  11.7 0.0 copy-done.2
  11.7 0.0 copy-done.5
  11.7 0.0 copy-done.6
  11.7 0.0 copy-done.7
  11.7 0.0 copy-start
  11.8 1.4 %copy-done = bf16[6,8,128,128]{3,2,1,0:T(8,128)(2,1)S(1)} copy-done((bf16[6,8,128,128]{3,2,1,0:T(8,128)(2,1)S(1)}, bf16[6,8,128,128]{3,2,1,0:T(8,128)(2,1)}, u32[]{:S(2)}) %copy-start) | copy-done | bytes 1572888
  13.2 0.0 copy-start.1
  13.2 1.4 %copy-done.1 = bf16[6,8,128,128]{3,2,1,0:T(8,128)(2,1)S(1)} copy-done((bf16[6,8,128,128]{3,2,1,0:T(8,128)(2,1)S(1)}, bf16[6,8,128,128]{3,2,1,0:T(8,128)(2,1)}, u32[]{:S(2)}) %copy-start.1) | copy-done | bytes 1572888
  14.6 3.5 %attend.1 = (f32[2,32,128]{2,1,0:T(8,128)S(1)}, f32[2,400,128]{2,1,0:T(8,128)S(1)}, f32[2,400,128]{2,1,0:T(8,128)S(1)}) custom-call(s32[1]{0:T(128)} %bitcast.me_ref, s32[48]{0:T(128)S(1)} %copy-done.6, s32[6]{0:T(128)S(1)} %copy-done.7, s32[6,4,16]{2,1,0:T(4,128)S(1)} %bitcast.4, bf16[4,6,64,128]{3,2,1,0:T(8,128)(2,1)S(1)} %copy-done.2, ...), custom_call_target="tpu_custom_call" | custom-call | flops 1000 | bytes 1000 | tf_op jit(solution)/shard_map/attend/pallas_call | solution.py:324
  18.0 0.0 copy-start.3
  18.1 0.5 collective-permute-start
  18.5 1.4 %collective-permute-done.got = f32[2,400,128]{2,1,0:T(8,128)S(1)} collective-permute-done((f32[2,400,128]{2,1,0:T(8,128)S(1)}, f32[2,400,128]{2,1,0:T(8,128)S(1)}, u32[]{:S(2)}, u32[]{:S(2)}) %collective-permute-start) | collective-permute-done | bytes 409632 | tf_op jit(solution)/shard_map/ppermute | solution.py:342
  19.9 0.4 core.1
  20.3 2.0 %collective-permute-start.1 = (f32[400,128]{1,0:T(8,128)S(1)}, f32[400,128]{1,0:T(8,128)S(1)}, u32[]{:S(2)}, u32[]{:S(2)}) collective-permute-start(f32[400,128]{1,0:T(8,128)S(1)} %get-tuple-element.23), channel_id=1, source_target_pairs={{0,2},{1,3},{2,0},{3,1},{4,6},{5,7},{6,4},{7,5},{8,10},{9,11},{10,... | collective-permute-start | bytes 614408 | tf_op jit(solution)/shard_map/ppermute | solution.py:342
  22.3 13.0 %collective-permute-done.1.got = f32[400,128]{1,0:T(8,128)S(1)} collective-permute-done((f32[400,128]{1,0:T(8,128)S(1)}, f32[400,128]{1,0:T(8,128)S(1)}, u32[]{:S(2)}, u32[]{:S(2)}) %collective-permute-start.1) | collective-permute-done | bytes 204832 | tf_op jit(solution)/shard_map/ppermute | solution.py:342
  35.3 0.2 near.1.own
  35.5 0.1 collective-permute-start.2
  35.6 15.4 %collective-permute-done.2.got = f32[400,128]{1,0:T(8,128)S(1)} collective-permute-done((f32[400,128]{1,0:T(8,128)S(1)}, f32[400,128]{1,0:T(8,128)S(1)}, u32[]{:S(2)}, u32[]{:S(2)}) %collective-permute-start.2) | collective-permute-done | bytes 204832 | tf_op jit(solution)/shard_map/ppermute | solution.py:342
  51.0 0.2 far.1.block
  51.2 0.1 scale.1
  51.4 0.1 reduce-precision_convert_fusion
  51.5 4.6 %collective-permute-start.3 = (f16[384,128]{1,0:T(8,128)(2,1)S(1)}, f16[384,128]{1,0:T(8,128)(2,1)S(1)}, u32[]{:S(2)}, u32[]{:S(2)}) collective-permute-start(f16[384,128]{1,0:T(8,128)(2,1)S(1)} %get-tuple-element.32), channel_id=1, source_target_pairs={{0,8},{1,9},{2,10},{3,11},{4,12},{5,13},{6,14},{7,15},{8,0},{9,1},... | collective-permute-start | bytes 294920 | tf_op jit(solution)/shard_map/ppermute | solution.py:342
  56.0 8.9 %collective-permute-done.3 = f16[384,128]{1,0:T(8,128)(2,1)S(1)} collective-permute-done((f16[384,128]{1,0:T(8,128)(2,1)S(1)}, f16[384,128]{1,0:T(8,128)(2,1)S(1)}, u32[]{:S(2)}, u32[]{:S(2)}) %collective-permute-start.3) | collective-permute-done | bytes 98336 | tf_op jit(solution)/shard_map/ppermute | solution.py:342
  65.0 0.0 copy-done.3
  65.0 0.0 all-to-all-done.got
  65.0 3.7 %all-to-all-start.1 = ((bf16[32,128,128]{2,1,0:T(8,128)(2,1)}), bf16[32,128,128]{2,1,0:T(8,128)(2,1)S(1)}, u32[]{:S(2)}, u32[]{:S(2)}) async-start(bf16[32,128,128]{2,1,0:T(8,128)(2,1)} %get-tuple-element.31), calls=%async_computation.1 | async-start | bytes 2097152 | tf_op jit(solution)/shard_map/all_to_all | solution.py:299
  68.7 2.8 %collective-permute-start.4 = (f32[24,128]{1,0:T(8,128)S(1)}, f32[24,128]{1,0:T(8,128)S(1)}, u32[]{:S(2)}, u32[]{:S(2)}) collective-permute-start(f32[24,128]{1,0:T(8,128)S(1)} %get-tuple-element.27.own_stats), channel_id=1, source_target_pairs={{0,8},{1,9},{2,10},{3,11},{4,12},{5,13},{6,14},{7,15},{8,0},{9,1},... | collective-permute-start | bytes 36872 | tf_op jit(solution)/shard_map/ppermute | solution.py:342
  71.6 24.2 %collective-permute-done.4.got_stats = f32[24,128]{1,0:T(8,128)S(1)} collective-permute-done((f32[24,128]{1,0:T(8,128)S(1)}, f32[24,128]{1,0:T(8,128)S(1)}, u32[]{:S(2)}, u32[]{:S(2)}) %collective-permute-start.4) | collective-permute-done | bytes 12320 | tf_op jit(solution)/shard_map/ppermute | solution.py:342
  95.8 0.3 last.1.refs_0_
  96.1 1.5 %collective-permute-start.5 = (bf16[416,128]{1,0:T(8,128)(2,1)S(1)}, bf16[416,128]{1,0:T(8,128)(2,1)S(1)}, u32[]{:S(2)}, u32[]{:S(2)}) collective-permute-start(bf16[416,128]{1,0:T(8,128)(2,1)S(1)} %last.1.refs_0_), channel_id=1, source_target_pairs={{0,2},{1,3},{2,0},{3,1},{4,6},{5,7},{6,4},{7,5},{8,10},{9,11},{10,... | collective-permute-start | bytes 319496 | tf_op jit(solution)/shard_map/ppermute | solution.py:342
  97.7 0.0 collective-permute-start.6
  97.7 3.2 %collective-permute-done.5.refs_1_ = bf16[416,128]{1,0:T(8,128)(2,1)S(1)} collective-permute-done((bf16[416,128]{1,0:T(8,128)(2,1)S(1)}, bf16[416,128]{1,0:T(8,128)(2,1)S(1)}, u32[]{:S(2)}, u32[]{:S(2)}) %collective-permute-start.5) | collective-permute-done | bytes 106528 | tf_op jit(solution)/shard_map/ppermute | solution.py:342
  100.9 0.0 collective-permute-start.7
  100.9 0.0 collective-permute-done.6.refs_2_
  100.9 1.3 %collective-permute-done.7.refs_3_ = bf16[416,128]{1,0:T(8,128)(2,1)S(1)} collective-permute-done((bf16[416,128]{1,0:T(8,128)(2,1)S(1)}, bf16[416,128]{1,0:T(8,128)(2,1)S(1)}, u32[]{:S(2)}, u32[]{:S(2)}) %collective-permute-start.7) | collective-permute-done | bytes 106528 | tf_op jit(solution)/shard_map/ppermute | solution.py:342
  102.2 0.0 copy-start.4
  102.2 0.8 copy-done.4
  103.0 1.4 %finish.1 = (bf16[4,384,128]{2,1,0:T(8,128)(2,1)}, f32[6,1,8]{2,1,0:T(1,128)}) custom-call(s32[1]{0:T(128)} %bitcast.me_ref, f32[2,32,128]{2,1,0:T(8,128)S(1)} %copy-done.4, bf16[416,128]{1,0:T(8,128)(2,1)S(1)} %last.1.refs_0_, bf16[416,128]{1,0:T(8,128)(2,1)S(1)} %collective-permute-done.5.refs_1_, bf16[416,128]{1,0:T(8,128)(2,1)S(1)} %collective-permute-done.6.refs_2_, ...), custom_call_target="tpu_custom_call" | custom-call | flops 1000 | bytes 1000 | tf_op jit(solution)/shard_map/finish/pallas_call | solution.py:393
  104.4 1.7 %place_keys.1 = bf16[6,8,128,128]{3,2,1,0:T(8,128)(2,1)} custom-call(s32[1]{0:T(128)} %bitcast.me_ref, s32[48]{0:T(128)S(1)} %copy-done.6, bf16[64,128,128]{2,1,0:T(8,128)(2,1)S(1)} %all-to-all-done.got), custom_call_target="tpu_custom_call" | custom-call | flops 1000 | bytes 1000 | tf_op jit(solution)/shard_map/place_keys/pallas_call | solution.py:378
  106.1 0.0 all-to-all-done.1.got_rest
  106.1 1.7 %place_values.1 = bf16[6,8,128,128]{3,2,1,0:T(8,128)(2,1)} custom-call(s32[1]{0:T(128)} %bitcast.me_ref, s32[48]{0:T(128)S(1)} %copy-done.6, bf16[64,128,128]{2,1,0:T(8,128)(2,1)S(1)} %all-to-all-done.got, bf16[32,128,128]{2,1,0:T(8,128)(2,1)S(1)} %all-to-all-done.1.got_rest), custom_call_target="tpu_custom_call" | custom-call | flops 1000 | bytes 1000 | tf_op jit(solution)/shard_map/place_values/pallas_call | solution.py:378
  (1 shorter events, 0.0 us)
Async XLA Ops:
  4.1 7.6 %copy-start.2 = (bf16[4,6,64,128]{3,2,1,0:T(8,128)(2,1)S(1)}, bf16[4,6,64,128]{3,2,1,0:T(8,128)(2,1)}, u32[]{:S(2)}) copy-start(bf16[4,6,64,128]{3,2,1,0:T(8,128)(2,1)} %q_ref.1) | copy-start | bytes 1179652
  4.1 7.6 %copy-start.5 = (s32[4,6,16]{2,0,1:T(4,128)S(1)}, s32[4,6,16]{2,0,1:T(4,128)}, u32[]{:S(2)}) copy-start(s32[4,6,16]{2,0,1:T(4,128)} %param.10) | copy-start | bytes 4612
  4.1 7.6 %copy-start.6 = (s32[48]{0:T(128)S(1)}, s32[48]{0:T(128)}, u32[]{:S(2)}) copy-start(s32[48]{0:T(128)} %get-tuple-element.18.table) | copy-start | bytes 580
  4.2 7.6 %copy-start.7 = (s32[6]{0:T(128)S(1)}, s32[6]{0:T(128)}, u32[]{:S(2)}) copy-start(s32[6]{0:T(128)} %len_hbm.1) | copy-start | bytes 76
  4.2 60.8 %all-to-all-start = ((bf16[64,128,128]{2,1,0:T(8,128)(2,1)}), bf16[64,128,128]{2,1,0:T(8,128)(2,1)S(1)}, u32[]{:S(2)}, u32[]{:S(2)}) async-start(bf16[64,128,128]{2,1,0:T(8,128)(2,1)} %get-tuple-element.30), calls=%async_computation | async-start | bytes 4194304 | tf_op jit(solution)/shard_map/all_to_all | solution.py:299
  11.7 1.4 %copy-start = (bf16[6,8,128,128]{3,2,1,0:T(8,128)(2,1)S(1)}, bf16[6,8,128,128]{3,2,1,0:T(8,128)(2,1)}, u32[]{:S(2)}) copy-start(bf16[6,8,128,128]{3,2,1,0:T(8,128)(2,1)} %k_ref.3) | copy-start | bytes 4718596
  13.2 1.4 %copy-start.1 = (bf16[6,8,128,128]{3,2,1,0:T(8,128)(2,1)S(1)}, bf16[6,8,128,128]{3,2,1,0:T(8,128)(2,1)}, u32[]{:S(2)}) copy-start(bf16[6,8,128,128]{3,2,1,0:T(8,128)(2,1)} %v_ref.3) | copy-start | bytes 4718596
  18.0 47.0 %copy-start.3 = (f32[2,32,128]{2,1,0:T(8,128)}, f32[2,32,128]{2,1,0:T(8,128)S(1)}, u32[]{:S(2)}) copy-start(f32[2,32,128]{2,1,0:T(8,128)S(1)} %get-tuple-element.19.stats_ref) | copy-start | bytes 98308
  18.1 1.8 %collective-permute-start = (f32[2,400,128]{2,1,0:T(8,128)S(1)}, f32[2,400,128]{2,1,0:T(8,128)S(1)}, u32[]{:S(2)}, u32[]{:S(2)}) collective-permute-start(f32[2,400,128]{2,1,0:T(8,128)S(1)} %get-tuple-element.21), channel_id=1, source_target_pairs={{0,1},{1,0},{2,3},{3,2},{4,5},{5,4},{6,7},{7,6},{8,9},{9,8},{10,11... | collective-permute-start | bytes 1228808 | tf_op jit(solution)/shard_map/ppermute | solution.py:342
  20.3 15.0 %collective-permute-start.1 = (f32[400,128]{1,0:T(8,128)S(1)}, f32[400,128]{1,0:T(8,128)S(1)}, u32[]{:S(2)}, u32[]{:S(2)}) collective-permute-start(f32[400,128]{1,0:T(8,128)S(1)} %get-tuple-element.23), channel_id=1, source_target_pairs={{0,2},{1,3},{2,0},{3,1},{4,6},{5,7},{6,4},{7,5},{8,10},{9,11},{10,... | collective-permute-start | bytes 614408 | tf_op jit(solution)/shard_map/ppermute | solution.py:342
  35.5 15.5 %collective-permute-start.2 = (f32[400,128]{1,0:T(8,128)S(1)}, f32[400,128]{1,0:T(8,128)S(1)}, u32[]{:S(2)}, u32[]{:S(2)}) collective-permute-start(f32[400,128]{1,0:T(8,128)S(1)} %near.1.own), channel_id=1, source_target_pairs={{0,4},{1,5},{2,6},{3,7},{4,0},{5,1},{6,2},{7,3},{8,12},{9,13},{10,... | collective-permute-start | bytes 614408 | tf_op jit(solution)/shard_map/ppermute | solution.py:342
  51.5 13.5 %collective-permute-start.3 = (f16[384,128]{1,0:T(8,128)(2,1)S(1)}, f16[384,128]{1,0:T(8,128)(2,1)S(1)}, u32[]{:S(2)}, u32[]{:S(2)}) collective-permute-start(f16[384,128]{1,0:T(8,128)(2,1)S(1)} %get-tuple-element.32), channel_id=1, source_target_pairs={{0,8},{1,9},{2,10},{3,11},{4,12},{5,13},{6,14},{7,15},{8,0},{9,1},... | collective-permute-start | bytes 294920 | tf_op jit(solution)/shard_map/ppermute | solution.py:342
  65.0 41.1 %all-to-all-start.1 = ((bf16[32,128,128]{2,1,0:T(8,128)(2,1)}), bf16[32,128,128]{2,1,0:T(8,128)(2,1)S(1)}, u32[]{:S(2)}, u32[]{:S(2)}) async-start(bf16[32,128,128]{2,1,0:T(8,128)(2,1)} %get-tuple-element.31), calls=%async_computation.1 | async-start | bytes 2097152 | tf_op jit(solution)/shard_map/all_to_all | solution.py:299
  68.7 27.1 %collective-permute-start.4 = (f32[24,128]{1,0:T(8,128)S(1)}, f32[24,128]{1,0:T(8,128)S(1)}, u32[]{:S(2)}, u32[]{:S(2)}) collective-permute-start(f32[24,128]{1,0:T(8,128)S(1)} %get-tuple-element.27.own_stats), channel_id=1, source_target_pairs={{0,8},{1,9},{2,10},{3,11},{4,12},{5,13},{6,14},{7,15},{8,0},{9,1},... | collective-permute-start | bytes 36872 | tf_op jit(solution)/shard_map/ppermute | solution.py:342
  96.1 4.8 %collective-permute-start.5 = (bf16[416,128]{1,0:T(8,128)(2,1)S(1)}, bf16[416,128]{1,0:T(8,128)(2,1)S(1)}, u32[]{:S(2)}, u32[]{:S(2)}) collective-permute-start(bf16[416,128]{1,0:T(8,128)(2,1)S(1)} %last.1.refs_0_), channel_id=1, source_target_pairs={{0,2},{1,3},{2,0},{3,1},{4,6},{5,7},{6,4},{7,5},{8,10},{9,11},{10,... | collective-permute-start | bytes 319496 | tf_op jit(solution)/shard_map/ppermute | solution.py:342
  97.7 3.2 %collective-permute-start.6 = (bf16[416,128]{1,0:T(8,128)(2,1)S(1)}, bf16[416,128]{1,0:T(8,128)(2,1)S(1)}, u32[]{:S(2)}, u32[]{:S(2)}) collective-permute-start(bf16[416,128]{1,0:T(8,128)(2,1)S(1)} %last.1.refs_0_), channel_id=1, source_target_pairs={{0,1},{1,0},{2,3},{3,2},{4,5},{5,4},{6,7},{7,6},{8,9},{9,8},{10,11... | collective-permute-start | bytes 319496 | tf_op jit(solution)/shard_map/ppermute | solution.py:342
  100.9 1.3 %collective-permute-start.7 = (bf16[416,128]{1,0:T(8,128)(2,1)S(1)}, bf16[416,128]{1,0:T(8,128)(2,1)S(1)}, u32[]{:S(2)}, u32[]{:S(2)}) collective-permute-start(bf16[416,128]{1,0:T(8,128)(2,1)S(1)} %collective-permute-done.5.refs_1_), channel_id=1, source_target_pairs={{0,1},{1,0},{2,3},{3,2},{4,5},{5,4},{6,7},{7,6},{8,9},{9,8},{10,11... | collective-permute-start | bytes 319496 | tf_op jit(solution)/shard_map/ppermute | solution.py:342
  102.2 0.8 copy-start.4

commit v5 on v4

--- a/solution.py
+++ b/solution.py
@@ -366,11 +366,11 @@
     sums, sum_stats = local_call(functools.partial(scale_kernel, pairs, per), "scale", [sums_type, stats_type], block)
     sums = lax.reduce_precision(sums, 5, 10)
     got = flip(sums.astype(jnp.float16), bit).astype(F32)
-    got, rest_out = lax.optimization_barrier((got, rest_out))
+    got, got_stats, rest_out = lax.optimization_barrier((got, flip(sum_stats, bit), rest_out))
     rest_in = exchange(rest_out)
     message, = local_call(
         functools.partial(last_kernel, bit, pairs, per), "last", [message_type],
-        me, sums, got, sum_stats, flip(sum_stats, bit),
+        me, sums, got, sum_stats, got_stats,
     )
     other = flip(message, 2)
 

time: 108 us -> 96 us (0.89); the launches traced: 108 us -> 94.4 us
  waiting for transfers between devices: 67.5 us -> 55.2 us
  starting transfers between devices: 22.7 us -> 20.3 us
  local copies, waits for them, and re-layouts: 3.6 us -> 4.9 us
    ppermute x8, waiting for transfers between devices: 67.5 us -> 49.6 us  [flip(): return lax.ppermute(x, 'ctx', [(i, i ^ bit) for i in range(devices)])]
    all_to_all x2, waiting for transfers between devices: 0.01 us -> 5.65 us  [exchange(): return lax.all_to_all(x, 'ctx', split_axis=0, concat_axis=0, tiled=True)]
    ppermute x8, starting transfers between devices: 11.4 us -> 9.13 us  [flip(): return lax.ppermute(x, 'ctx', [(i, i ^ bit) for i in range(devices)])]
    unnamed x16 -> x20, local copies, waits for them, and re-layouts: 3.6 us -> 4.9 us
  transfers between devices with their start and end apart: 10 -> 10, of which waited for: 7 -> 8; matrix products, arithmetic and copies ran while one was open for 0% -> 0% of each run, Pallas kernels for 7% -> 8%
where the time goes in v5:
time: 96 us; the launch traced here: 94.4 us
  waiting for transfers between devices  55.2 us (58%)
  starting transfers between devices  20.3 us (21%)
  Pallas kernels  13 us (14%)
  local copies, waits for them, and re-layouts  4.9 us (5%)
    ppermute x8, waiting for transfers between devices, flip(): return lax.ppermute(x, 'ctx', [(i, i ^ bit) for i in range(devices)])  49.6 us
    all_to_all x2, starting transfers between devices, exchange(): return lax.all_to_all(x, 'ctx', split_axis=0, concat_axis=0, tiled=True)  11.2 us
    ppermute x8, starting transfers between devices, flip(): return lax.ppermute(x, 'ctx', [(i, i ^ bit) for i in range(devices)])  9.13 us
    all_to_all x2, waiting for transfers between devices, exchange(): return lax.all_to_all(x, 'ctx', split_axis=0, concat_axis=0, tiled=True)  5.65 us
    unnamed x20, local copies, waits for them, and re-layouts  4.9 us
    pallas_call x1, Pallas kernels, local(): pl.pallas_call(functools.partial(stage_kernel, devices, group, first), ou...  3.48 us
    pallas_call x1, Pallas kernels, local(): pl.pallas_call(functools.partial(attend_kernel, levels), out_shape=[jax.S...  3.47 us
    pallas_call x2, Pallas kernels, place(): pl.pallas_call(functools.partial(kernel, devices, group, first), out_shap...  3.34 us
  transfers between devices with their start and end apart: 10, of which 8 were waited for; matrix products, arithmetic and copies ran while one was open for 0% of the time, Pallas kernels for 8%

profile of v5, /device:TPU:0, one launch (start us, length us, event | category | flops | bytes accessed | tf_op | source)
XLA Modules:
  0.0 94.4 jit_solution(14681055505165541133)
XLA Ops:
  0.6 3.5 %stage.1 = (bf16[64,128,128]{2,1,0:T(8,128)(2,1)}, bf16[32,128,128]{2,1,0:T(8,128)(2,1)}, s32[48]{0:T(128)}) custom-call(s32[1]{0:T(128)} %bitcast.me_ref, s32[6,8,16]{2,1,0:T(8,128)} %dest_hbm.1, bf16[6,8,128,128]{3,2,1,0:T(8,128)(2,1)} %k_ref.3, bf16[6,8,128,128]{3,2,1,0:T(8,128)(2,1)} %v_ref.3), custom_call_target="tpu_custom_call" | custom-call | flops 1000 | bytes 1000 | tf_op jit(solution)/shard_map/stage/pallas_call | solution.py:302
  4.1 0.0 copy-start.2
  4.1 0.0 copy-start.5
  4.1 0.0 copy-start.8
  4.2 0.0 copy-start.9
  4.2 7.5 %all-to-all-start = ((bf16[64,128,128]{2,1,0:T(8,128)(2,1)}), bf16[64,128,128]{2,1,0:T(8,128)(2,1)S(1)}, u32[]{:S(2)}, u32[]{:S(2)}) async-start(bf16[64,128,128]{2,1,0:T(8,128)(2,1)} %get-tuple-element.32), calls=%async_computation | async-start | bytes 4194304 | tf_op jit(solution)/shard_map/all_to_all | solution.py:299
  11.7 0.0 copy-done.2
  11.7 0.0 copy-done.5
  11.7 0.0 copy-done.8
  11.7 0.0 copy-done.9
  11.7 0.0 copy-start
  11.8 1.4 %copy-done = bf16[6,8,128,128]{3,2,1,0:T(8,128)(2,1)S(1)} copy-done((bf16[6,8,128,128]{3,2,1,0:T(8,128)(2,1)S(1)}, bf16[6,8,128,128]{3,2,1,0:T(8,128)(2,1)}, u32[]{:S(2)}) %copy-start) | copy-done | bytes 1572888
  13.2 1.4 %copy-done.1 = bf16[6,8,128,128]{3,2,1,0:T(8,128)(2,1)S(1)} copy-done((bf16[6,8,128,128]{3,2,1,0:T(8,128)(2,1)S(1)}, bf16[6,8,128,128]{3,2,1,0:T(8,128)(2,1)}, u32[]{:S(2)}) %copy-start.1) | copy-done | bytes 1572888
  14.6 3.5 %attend.1 = (f32[2,32,128]{2,1,0:T(8,128)S(1)}, f32[2,400,128]{2,1,0:T(8,128)S(1)}, f32[2,400,128]{2,1,0:T(8,128)S(1)}) custom-call(s32[1]{0:T(128)} %bitcast.me_ref, s32[48]{0:T(128)S(1)} %copy-done.8, s32[6]{0:T(128)S(1)} %copy-done.9, s32[6,4,16]{2,1,0:T(4,128)S(1)} %bitcast.4, bf16[4,6,64,128]{3,2,1,0:T(8,128)(2,1)S(1)} %copy-done.2, ...), custom_call_target="tpu_custom_call" | custom-call | flops 1000 | bytes 1000 | tf_op jit(solution)/shard_map/attend/pallas_call | solution.py:324
  18.0 0.0 copy-start.3
  18.1 0.5 collective-permute-start
  18.5 1.4 %collective-permute-done.got = f32[2,400,128]{2,1,0:T(8,128)S(1)} collective-permute-done((f32[2,400,128]{2,1,0:T(8,128)S(1)}, f32[2,400,128]{2,1,0:T(8,128)S(1)}, u32[]{:S(2)}, u32[]{:S(2)}) %collective-permute-start) | collective-permute-done | bytes 409632 | tf_op jit(solution)/shard_map/ppermute | solution.py:342
  19.9 0.4 core.1
  20.3 2.0 %collective-permute-start.1 = (f32[400,128]{1,0:T(8,128)S(1)}, f32[400,128]{1,0:T(8,128)S(1)}, u32[]{:S(2)}, u32[]{:S(2)}) collective-permute-start(f32[400,128]{1,0:T(8,128)S(1)} %get-tuple-element.24), channel_id=1, source_target_pairs={{0,2},{1,3},{2,0},{3,1},{4,6},{5,7},{6,4},{7,5},{8,10},{9,11},{10,... | collective-permute-start | bytes 614408 | tf_op jit(solution)/shard_map/ppermute | solution.py:342
  22.3 13.0 %collective-permute-done.1.got = f32[400,128]{1,0:T(8,128)S(1)} collective-permute-done((f32[400,128]{1,0:T(8,128)S(1)}, f32[400,128]{1,0:T(8,128)S(1)}, u32[]{:S(2)}, u32[]{:S(2)}) %collective-permute-start.1) | collective-permute-done | bytes 204832 | tf_op jit(solution)/shard_map/ppermute | solution.py:342
  35.3 0.2 near.1.own
  35.5 0.1 collective-permute-start.2
  35.6 15.4 %collective-permute-done.2.got = f32[400,128]{1,0:T(8,128)S(1)} collective-permute-done((f32[400,128]{1,0:T(8,128)S(1)}, f32[400,128]{1,0:T(8,128)S(1)}, u32[]{:S(2)}, u32[]{:S(2)}) %collective-permute-start.2) | collective-permute-done | bytes 204832 | tf_op jit(solution)/shard_map/ppermute | solution.py:342
  51.0 0.2 far.1.block
  51.2 0.1 scale.1
  51.4 0.1 reduce-precision_convert_fusion
  51.5 4.6 %collective-permute-start.3 = (f16[384,128]{1,0:T(8,128)(2,1)S(1)}, f16[384,128]{1,0:T(8,128)(2,1)S(1)}, u32[]{:S(2)}, u32[]{:S(2)}) collective-permute-start(f16[384,128]{1,0:T(8,128)(2,1)S(1)} %get-tuple-element.34), channel_id=1, source_target_pairs={{0,8},{1,9},{2,10},{3,11},{4,12},{5,13},{6,14},{7,15},{8,0},{9,1},... | collective-permute-start | bytes 294920 | tf_op jit(solution)/shard_map/ppermute | solution.py:342
  56.0 0.1 collective-permute-start.4
  56.1 9.3 %collective-permute-done.3 = f16[384,128]{1,0:T(8,128)(2,1)S(1)} collective-permute-done((f16[384,128]{1,0:T(8,128)(2,1)S(1)}, f16[384,128]{1,0:T(8,128)(2,1)S(1)}, u32[]{:S(2)}, u32[]{:S(2)}) %collective-permute-start.3) | collective-permute-done | bytes 98336 | tf_op jit(solution)/shard_map/ppermute | solution.py:342
  65.4 0.1 collective-permute-done.4.got_stats
  65.5 0.0 copy-done.3
  65.5 0.6 copy-done.6
  66.1 0.0 all-to-all-done.got
  66.1 3.7 %all-to-all-start.1 = ((bf16[32,128,128]{2,1,0:T(8,128)(2,1)}), bf16[32,128,128]{2,1,0:T(8,128)(2,1)S(1)}, u32[]{:S(2)}, u32[]{:S(2)}) async-start(bf16[32,128,128]{2,1,0:T(8,128)(2,1)} %get-tuple-element.33), calls=%async_computation.1 | async-start | bytes 2097152 | tf_op jit(solution)/shard_map/all_to_all | solution.py:299
  69.8 0.0 copy-start.7
  69.8 0.7 copy-done.7
  70.5 0.3 last.1.refs_0_
  70.8 2.0 %collective-permute-start.5 = (bf16[416,128]{1,0:T(8,128)(2,1)S(1)}, bf16[416,128]{1,0:T(8,128)(2,1)S(1)}, u32[]{:S(2)}, u32[]{:S(2)}) collective-permute-start(bf16[416,128]{1,0:T(8,128)(2,1)S(1)} %last.1.refs_0_), channel_id=1, source_target_pairs={{0,2},{1,3},{2,0},{3,1},{4,6},{5,7},{6,4},{7,5},{8,10},{9,11},{10,... | collective-permute-start | bytes 319496 | tf_op jit(solution)/shard_map/ppermute | solution.py:342
  72.8 0.0 collective-permute-start.6
  72.8 9.1 %collective-permute-done.5.refs_1_ = bf16[416,128]{1,0:T(8,128)(2,1)S(1)} collective-permute-done((bf16[416,128]{1,0:T(8,128)(2,1)S(1)}, bf16[416,128]{1,0:T(8,128)(2,1)S(1)}, u32[]{:S(2)}, u32[]{:S(2)}) %collective-permute-start.5) | collective-permute-done | bytes 106528 | tf_op jit(solution)/shard_map/ppermute | solution.py:342
  81.9 0.0 collective-permute-start.7
  81.9 0.0 collective-permute-done.6.refs_2_
  81.9 1.3 %collective-permute-done.7.refs_3_ = bf16[416,128]{1,0:T(8,128)(2,1)S(1)} collective-permute-done((bf16[416,128]{1,0:T(8,128)(2,1)S(1)}, bf16[416,128]{1,0:T(8,128)(2,1)S(1)}, u32[]{:S(2)}, u32[]{:S(2)}) %collective-permute-start.7) | collective-permute-done | bytes 106528 | tf_op jit(solution)/shard_map/ppermute | solution.py:342
  83.2 0.8 copy-done.4
  84.0 1.4 %finish.1 = (bf16[4,384,128]{2,1,0:T(8,128)(2,1)}, f32[6,1,8]{2,1,0:T(1,128)}) custom-call(s32[1]{0:T(128)} %bitcast.me_ref, f32[2,32,128]{2,1,0:T(8,128)S(1)} %copy-done.4, bf16[416,128]{1,0:T(8,128)(2,1)S(1)} %last.1.refs_0_, bf16[416,128]{1,0:T(8,128)(2,1)S(1)} %collective-permute-done.5.refs_1_, bf16[416,128]{1,0:T(8,128)(2,1)S(1)} %collective-permute-done.6.refs_2_, ...), custom_call_target="tpu_custom_call" | custom-call | flops 1000 | bytes 1000 | tf_op jit(solution)/shard_map/finish/pallas_call | solution.py:393
  85.4 1.7 %place_keys.1 = bf16[6,8,128,128]{3,2,1,0:T(8,128)(2,1)} custom-call(s32[1]{0:T(128)} %bitcast.me_ref, s32[48]{0:T(128)S(1)} %copy-done.8, bf16[64,128,128]{2,1,0:T(8,128)(2,1)S(1)} %all-to-all-done.got), custom_call_target="tpu_custom_call" | custom-call | flops 1000 | bytes 1000 | tf_op jit(solution)/shard_map/place_keys/pallas_call | solution.py:378
  87.1 5.6 %all-to-all-done.1.got_rest = bf16[32,128,128]{2,1,0:T(8,128)(2,1)S(1)} async-done(((bf16[32,128,128]{2,1,0:T(8,128)(2,1)}), bf16[32,128,128]{2,1,0:T(8,128)(2,1)S(1)}, u32[]{:S(2)}, u32[]{:S(2)}) %all-to-all-start.1) | async-done | bytes 1048608 | tf_op jit(solution)/shard_map/all_to_all | solution.py:299
  92.8 1.7 %place_values.1 = bf16[6,8,128,128]{3,2,1,0:T(8,128)(2,1)} custom-call(s32[1]{0:T(128)} %bitcast.me_ref, s32[48]{0:T(128)S(1)} %copy-done.8, bf16[64,128,128]{2,1,0:T(8,128)(2,1)S(1)} %all-to-all-done.got, bf16[32,128,128]{2,1,0:T(8,128)(2,1)S(1)} %all-to-all-done.1.got_rest), custom_call_target="tpu_custom_call" | custom-call | flops 1000 | bytes 1000 | tf_op jit(solution)/shard_map/place_values/pallas_call | solution.py:378
  (4 shorter events, 0.0 us)
Async XLA Ops:
  4.1 7.6 %copy-start.2 = (bf16[4,6,64,128]{3,2,1,0:T(8,128)(2,1)S(1)}, bf16[4,6,64,128]{3,2,1,0:T(8,128)(2,1)}, u32[]{:S(2)}) copy-start(bf16[4,6,64,128]{3,2,1,0:T(8,128)(2,1)} %q_ref.1) | copy-start | bytes 1179652
  4.1 7.6 %copy-start.5 = (s32[4,6,16]{2,0,1:T(4,128)S(1)}, s32[4,6,16]{2,0,1:T(4,128)}, u32[]{:S(2)}) copy-start(s32[4,6,16]{2,0,1:T(4,128)} %param.10) | copy-start | bytes 4612
  4.1 7.6 %copy-start.8 = (s32[48]{0:T(128)S(1)}, s32[48]{0:T(128)}, u32[]{:S(2)}) copy-start(s32[48]{0:T(128)} %get-tuple-element.19.table) | copy-start | bytes 580
  4.2 7.6 %copy-start.9 = (s32[6]{0:T(128)S(1)}, s32[6]{0:T(128)}, u32[]{:S(2)}) copy-start(s32[6]{0:T(128)} %len_hbm.1) | copy-start | bytes 76
  4.2 61.9 %all-to-all-start = ((bf16[64,128,128]{2,1,0:T(8,128)(2,1)}), bf16[64,128,128]{2,1,0:T(8,128)(2,1)S(1)}, u32[]{:S(2)}, u32[]{:S(2)}) async-start(bf16[64,128,128]{2,1,0:T(8,128)(2,1)} %get-tuple-element.32), calls=%async_computation | async-start | bytes 4194304 | tf_op jit(solution)/shard_map/all_to_all | solution.py:299
  11.7 1.4 %copy-start = (bf16[6,8,128,128]{3,2,1,0:T(8,128)(2,1)S(1)}, bf16[6,8,128,128]{3,2,1,0:T(8,128)(2,1)}, u32[]{:S(2)}) copy-start(bf16[6,8,128,128]{3,2,1,0:T(8,128)(2,1)} %k_ref.3) | copy-start | bytes 4718596
  13.2 1.4 %copy-start.1 = (bf16[6,8,128,128]{3,2,1,0:T(8,128)(2,1)S(1)}, bf16[6,8,128,128]{3,2,1,0:T(8,128)(2,1)}, u32[]{:S(2)}) copy-start(bf16[6,8,128,128]{3,2,1,0:T(8,128)(2,1)} %v_ref.3) | copy-start | bytes 4718596
  18.0 47.5 %copy-start.3 = (f32[2,32,128]{2,1,0:T(8,128)}, f32[2,32,128]{2,1,0:T(8,128)S(1)}, u32[]{:S(2)}) copy-start(f32[2,32,128]{2,1,0:T(8,128)S(1)} %get-tuple-element.20.stats_ref) | copy-start | bytes 98308
  18.1 1.8 %collective-permute-start = (f32[2,400,128]{2,1,0:T(8,128)S(1)}, f32[2,400,128]{2,1,0:T(8,128)S(1)}, u32[]{:S(2)}, u32[]{:S(2)}) collective-permute-start(f32[2,400,128]{2,1,0:T(8,128)S(1)} %get-tuple-element.22), channel_id=1, source_target_pairs={{0,1},{1,0},{2,3},{3,2},{4,5},{5,4},{6,7},{7,6},{8,9},{9,8},{10,11... | collective-permute-start | bytes 1228808 | tf_op jit(solution)/shard_map/ppermute | solution.py:342
  20.3 15.0 %collective-permute-start.1 = (f32[400,128]{1,0:T(8,128)S(1)}, f32[400,128]{1,0:T(8,128)S(1)}, u32[]{:S(2)}, u32[]{:S(2)}) collective-permute-start(f32[400,128]{1,0:T(8,128)S(1)} %get-tuple-element.24), channel_id=1, source_target_pairs={{0,2},{1,3},{2,0},{3,1},{4,6},{5,7},{6,4},{7,5},{8,10},{9,11},{10,... | collective-permute-start | bytes 614408 | tf_op jit(solution)/shard_map/ppermute | solution.py:342
  35.5 15.5 %collective-permute-start.2 = (f32[400,128]{1,0:T(8,128)S(1)}, f32[400,128]{1,0:T(8,128)S(1)}, u32[]{:S(2)}, u32[]{:S(2)}) collective-permute-start(f32[400,128]{1,0:T(8,128)S(1)} %near.1.own), channel_id=1, source_target_pairs={{0,4},{1,5},{2,6},{3,7},{4,0},{5,1},{6,2},{7,3},{8,12},{9,13},{10,... | collective-permute-start | bytes 614408 | tf_op jit(solution)/shard_map/ppermute | solution.py:342
  51.5 13.9 %collective-permute-start.3 = (f16[384,128]{1,0:T(8,128)(2,1)S(1)}, f16[384,128]{1,0:T(8,128)(2,1)S(1)}, u32[]{:S(2)}, u32[]{:S(2)}) collective-permute-start(f16[384,128]{1,0:T(8,128)(2,1)S(1)} %get-tuple-element.34), channel_id=1, source_target_pairs={{0,8},{1,9},{2,10},{3,11},{4,12},{5,13},{6,14},{7,15},{8,0},{9,1},... | collective-permute-start | bytes 294920 | tf_op jit(solution)/shard_map/ppermute | solution.py:342
  56.0 9.5 %collective-permute-start.4 = (f32[24,128]{1,0:T(8,128)S(1)}, f32[24,128]{1,0:T(8,128)S(1)}, u32[]{:S(2)}, u32[]{:S(2)}) collective-permute-start(f32[24,128]{1,0:T(8,128)S(1)} %get-tuple-element.26.own_stats), channel_id=1, source_target_pairs={{0,8},{1,9},{2,10},{3,11},{4,12},{5,13},{6,14},{7,15},{8,0},{9,1},... | collective-permute-start | bytes 36872 | tf_op jit(solution)/shard_map/ppermute | solution.py:342
  65.5 0.6 copy-start.6
  66.1 26.6 %all-to-all-start.1 = ((bf16[32,128,128]{2,1,0:T(8,128)(2,1)}), bf16[32,128,128]{2,1,0:T(8,128)(2,1)S(1)}, u32[]{:S(2)}, u32[]{:S(2)}) async-start(bf16[32,128,128]{2,1,0:T(8,128)(2,1)} %get-tuple-element.33), calls=%async_computation.1 | async-start | bytes 2097152 | tf_op jit(solution)/shard_map/all_to_all | solution.py:299
  69.8 0.7 copy-start.7
  70.8 11.1 %collective-permute-start.5 = (bf16[416,128]{1,0:T(8,128)(2,1)S(1)}, bf16[416,128]{1,0:T(8,128)(2,1)S(1)}, u32[]{:S(2)}, u32[]{:S(2)}) collective-permute-start(bf16[416,128]{1,0:T(8,128)(2,1)S(1)} %last.1.refs_0_), channel_id=1, source_target_pairs={{0,2},{1,3},{2,0},{3,1},{4,6},{5,7},{6,4},{7,5},{8,10},{9,11},{10,... | collective-permute-start | bytes 319496 | tf_op jit(solution)/shard_map/ppermute | solution.py:342
  72.8 9.1 %collective-permute-start.6 = (bf16[416,128]{1,0:T(8,128)(2,1)S(1)}, bf16[416,128]{1,0:T(8,128)(2,1)S(1)}, u32[]{:S(2)}, u32[]{:S(2)}) collective-permute-start(bf16[416,128]{1,0:T(8,128)(2,1)S(1)} %last.1.refs_0_), channel_id=1, source_target_pairs={{0,1},{1,0},{2,3},{3,2},{4,5},{5,4},{6,7},{7,6},{8,9},{9,8},{10,11... | collective-permute-start | bytes 319496 | tf_op jit(solution)/shard_map/ppermute | solution.py:342
  81.9 1.3 %collective-permute-start.7 = (bf16[416,128]{1,0:T(8,128)(2,1)S(1)}, bf16[416,128]{1,0:T(8,128)(2,1)S(1)}, u32[]{:S(2)}, u32[]{:S(2)}) collective-permute-start(bf16[416,128]{1,0:T(8,128)(2,1)S(1)} %collective-permute-done.5.refs_1_), channel_id=1, source_target_pairs={{0,1},{1,0},{2,3},{3,2},{4,5},{5,4},{6,7},{7,6},{8,9},{9,8},{10,11... | collective-permute-start | bytes 319496 | tf_op jit(solution)/shard_map/ppermute | solution.py:342
  83.2 0.8 copy-start.4

commit v6 on v5

--- a/solution.py
+++ b/solution.py
@@ -53,7 +53,7 @@
             rank = counts[offset]
             counts[offset] = rank + 1
             table[offset * group + rank] = row * heads + head
-            target = jnp.bitwise_and(me + offset, devices - 1)
+            target = turn_of(jnp.bitwise_and(me + offset, devices - 1), devices)
             pltpu.make_async_copy(k_vm.at[row, head], buf.at[target * first + rank], sem.at[1]).start()
 
             @pl.when(rank < first - group)
@@ -249,7 +249,7 @@
     heads = out.shape[1]
     me = me_ref[0]
     for offset in range(devices):
-        source = jnp.bitwise_and(me + devices - offset, devices - 1)
+        source = turn_of(jnp.bitwise_and(me + devices - offset, devices - 1), devices)
         for k in range(group):
             put(got.at[source * first + k], table[offset * group + k], heads, out, sem)
     pltpu.make_async_copy(out, out, sem).wait()
@@ -260,12 +260,16 @@
     me = me_ref[0]
     rest = 2 * group - first
     for offset in range(devices):
-        source = jnp.bitwise_and(me + devices - offset, devices - 1)
+        source = turn_of(jnp.bitwise_and(me + devices - offset, devices - 1), devices)
         for k in range(group):
             at = group + k
             src = got.at[source * first + at] if at < first else got_rest.at[source * rest + at - first]
             put(src, table[offset * group + k], heads, out, sem)
     pltpu.make_async_copy(out, out, sem).wait()
+
+
+def turn_of(index, devices):
+    return lax.rem(index, devices // 2) * 2 + index // (devices // 2)
 
 
 def put(src, pair, heads, out, sem):
@@ -295,8 +299,10 @@
     def tiles_type(count):
         return jax.ShapeDtypeStruct((devices * count, span, width), BF16)
 
+    order = [turn // 2 + turn % 2 * (devices // 2) for turn in range(devices)]
+
     def exchange(x):
-        return lax.all_to_all(x, "ctx", split_axis=0, concat_axis=0, tiled=True)
+        return lax.all_to_all(x, "ctx", split_axis=0, concat_axis=0, axis_index_groups=[order], tiled=True)
 
 
     tiles_out, rest_out, table = pl.pallas_call(

time: 96 us -> 99.4 us (1.035); the launches traced: 94.4 us -> 99 us
  starting transfers between devices: 20.3 us -> 23.1 us
  waiting for transfers between devices: 55.2 us -> 57 us
    all_to_all x2, waiting for transfers between devices: 5.65 us -> 8.53 us  [exchange(): lax.all_to_all(x, 'ctx', split_axis=0, concat_axis=0, axis_index_groups=[...]
    ppermute x8, starting transfers between devices: 9.13 us -> 10.9 us  [flip(): return lax.ppermute(x, 'ctx', [(i, i ^ bit) for i in range(devices)])]
    ppermute x8, waiting for transfers between devices: 49.6 us -> 48.5 us  [flip(): return lax.ppermute(x, 'ctx', [(i, i ^ bit) for i in range(devices)])]
    all_to_all x2, starting transfers between devices: 11.2 us -> 12.2 us  [exchange(): lax.all_to_all(x, 'ctx', split_axis=0, concat_axis=0, axis_index_groups=[...]
where the time goes in v6:
time: 99.4 us; the launch traced here: 99 us
  waiting for transfers between devices  57 us (57%)
  starting transfers between devices  23.1 us (23%)
  Pallas kernels  13 us (13%)
  local copies, waits for them, and re-layouts  4.9 us (5%)
    ppermute x8, waiting for transfers between devices, flip(): return lax.ppermute(x, 'ctx', [(i, i ^ bit) for i in range(devices)])  48.5 us
    all_to_all x2, starting transfers between devices, exchange(): lax.all_to_all(x, 'ctx', split_axis=0, concat_axis=0, axis_index_groups=[...  12.2 us
    ppermute x8, starting transfers between devices, flip(): return lax.ppermute(x, 'ctx', [(i, i ^ bit) for i in range(devices)])  10.9 us
    all_to_all x2, waiting for transfers between devices, exchange(): lax.all_to_all(x, 'ctx', split_axis=0, concat_axis=0, axis_index_groups=[...  8.53 us
    unnamed x20, local copies, waits for them, and re-layouts  4.9 us
    pallas_call x1, Pallas kernels, local(): pl.pallas_call(functools.partial(stage_kernel, devices, group, first), ou...  3.48 us
    pallas_call x1, Pallas kernels, local(): pl.pallas_call(functools.partial(attend_kernel, levels), out_shape=[jax.S...  3.47 us
    pallas_call x2, Pallas kernels, place(): pl.pallas_call(functools.partial(kernel, devices, group, first), out_shap...  3.34 us
  transfers between devices with their start and end apart: 10, of which 8 were waited for; matrix products, arithmetic and copies ran while one was open for 0% of the time, Pallas kernels for 8%

profile of v6, /device:TPU:0, one launch (start us, length us, event | category | flops | bytes accessed | tf_op | source)
XLA Modules:
  0.0 99.0 jit_solution(7079587445009533872)
XLA Ops:
  0.6 3.5 %stage.1 = (bf16[64,128,128]{2,1,0:T(8,128)(2,1)}, bf16[32,128,128]{2,1,0:T(8,128)(2,1)}, s32[48]{0:T(128)}) custom-call(s32[1]{0:T(128)} %bitcast.me_ref, s32[6,8,16]{2,1,0:T(8,128)} %dest_hbm.1, bf16[6,8,128,128]{3,2,1,0:T(8,128)(2,1)} %k_ref.3, bf16[6,8,128,128]{3,2,1,0:T(8,128)(2,1)} %v_ref.3), custom_call_target="tpu_custom_call" | custom-call | flops 1000 | bytes 1000 | tf_op jit(solution)/shard_map/stage/pallas_call | solution.py:308
  4.1 0.0 copy-start.2
  4.1 0.0 copy-start.5
  4.1 0.0 copy-start.8
  4.2 0.0 copy-start.9
  4.2 7.5 %all-to-all-start = ((bf16[64,128,128]{2,1,0:T(8,128)(2,1)}), bf16[64,128,128]{2,1,0:T(8,128)(2,1)S(1)}, u32[]{:S(2)}, u32[]{:S(2)}) async-start(bf16[64,128,128]{2,1,0:T(8,128)(2,1)} %get-tuple-element.32), calls=%async_computation | async-start | bytes 4194304 | tf_op jit(solution)/shard_map/all_to_all | solution.py:305
  11.7 0.0 copy-done.2
  11.7 0.0 copy-done.5
  11.7 0.0 copy-done.8
  11.7 0.0 copy-done.9
  11.8 0.0 copy-start
  11.8 1.4 %copy-done = bf16[6,8,128,128]{3,2,1,0:T(8,128)(2,1)S(1)} copy-done((bf16[6,8,128,128]{3,2,1,0:T(8,128)(2,1)S(1)}, bf16[6,8,128,128]{3,2,1,0:T(8,128)(2,1)}, u32[]{:S(2)}) %copy-start) | copy-done | bytes 1572888
  13.2 1.4 %copy-done.1 = bf16[6,8,128,128]{3,2,1,0:T(8,128)(2,1)S(1)} copy-done((bf16[6,8,128,128]{3,2,1,0:T(8,128)(2,1)S(1)}, bf16[6,8,128,128]{3,2,1,0:T(8,128)(2,1)}, u32[]{:S(2)}) %copy-start.1) | copy-done | bytes 1572888
  14.6 3.5 %attend.1 = (f32[2,32,128]{2,1,0:T(8,128)S(1)}, f32[2,400,128]{2,1,0:T(8,128)S(1)}, f32[2,400,128]{2,1,0:T(8,128)S(1)}) custom-call(s32[1]{0:T(128)} %bitcast.me_ref, s32[48]{0:T(128)S(1)} %copy-done.8, s32[6]{0:T(128)S(1)} %copy-done.9, s32[6,4,16]{2,1,0:T(4,128)S(1)} %bitcast.4, bf16[4,6,64,128]{3,2,1,0:T(8,128)(2,1)S(1)} %copy-done.2, ...), custom_call_target="tpu_custom_call" | custom-call | flops 1000 | bytes 1000 | tf_op jit(solution)/shard_map/attend/pallas_call | solution.py:330
  18.0 0.0 copy-start.3
  18.1 0.5 collective-permute-start
  18.5 1.4 %collective-permute-done.got = f32[2,400,128]{2,1,0:T(8,128)S(1)} collective-permute-done((f32[2,400,128]{2,1,0:T(8,128)S(1)}, f32[2,400,128]{2,1,0:T(8,128)S(1)}, u32[]{:S(2)}, u32[]{:S(2)}) %collective-permute-start) | collective-permute-done | bytes 409632 | tf_op jit(solution)/shard_map/ppermute | solution.py:348
  19.9 0.4 core.1
  20.3 2.0 %collective-permute-start.1 = (f32[400,128]{1,0:T(8,128)S(1)}, f32[400,128]{1,0:T(8,128)S(1)}, u32[]{:S(2)}, u32[]{:S(2)}) collective-permute-start(f32[400,128]{1,0:T(8,128)S(1)} %get-tuple-element.24), channel_id=1, source_target_pairs={{0,2},{1,3},{2,0},{3,1},{4,6},{5,7},{6,4},{7,5},{8,10},{9,11},{10,... | collective-permute-start | bytes 614408 | tf_op jit(solution)/shard_map/ppermute | solution.py:348
  22.3 12.1 %collective-permute-done.1.got = f32[400,128]{1,0:T(8,128)S(1)} collective-permute-done((f32[400,128]{1,0:T(8,128)S(1)}, f32[400,128]{1,0:T(8,128)S(1)}, u32[]{:S(2)}, u32[]{:S(2)}) %collective-permute-start.1) | collective-permute-done | bytes 204832 | tf_op jit(solution)/shard_map/ppermute | solution.py:348
  34.3 0.2 near.1.own
  34.6 1.9 %collective-permute-start.2 = (f32[400,128]{1,0:T(8,128)S(1)}, f32[400,128]{1,0:T(8,128)S(1)}, u32[]{:S(2)}, u32[]{:S(2)}) collective-permute-start(f32[400,128]{1,0:T(8,128)S(1)} %near.1.own), channel_id=1, source_target_pairs={{0,4},{1,5},{2,6},{3,7},{4,0},{5,1},{6,2},{7,3},{8,12},{9,13},{10,... | collective-permute-start | bytes 614408 | tf_op jit(solution)/shard_map/ppermute | solution.py:348
  36.4 14.6 %collective-permute-done.2.got = f32[400,128]{1,0:T(8,128)S(1)} collective-permute-done((f32[400,128]{1,0:T(8,128)S(1)}, f32[400,128]{1,0:T(8,128)S(1)}, u32[]{:S(2)}, u32[]{:S(2)}) %collective-permute-start.2) | collective-permute-done | bytes 204832 | tf_op jit(solution)/shard_map/ppermute | solution.py:348
  51.0 0.2 far.1.block
  51.2 0.1 scale.1
  51.4 0.1 reduce-precision_convert_fusion
  51.5 4.5 %collective-permute-start.3 = (f16[384,128]{1,0:T(8,128)(2,1)S(1)}, f16[384,128]{1,0:T(8,128)(2,1)S(1)}, u32[]{:S(2)}, u32[]{:S(2)}) collective-permute-start(f16[384,128]{1,0:T(8,128)(2,1)S(1)} %get-tuple-element.34), channel_id=1, source_target_pairs={{0,8},{1,9},{2,10},{3,11},{4,12},{5,13},{6,14},{7,15},{8,0},{9,1},... | collective-permute-start | bytes 294920 | tf_op jit(solution)/shard_map/ppermute | solution.py:348
  56.0 0.1 collective-permute-start.4
  56.1 9.3 %collective-permute-done.3 = f16[384,128]{1,0:T(8,128)(2,1)S(1)} collective-permute-done((f16[384,128]{1,0:T(8,128)(2,1)S(1)}, f16[384,128]{1,0:T(8,128)(2,1)S(1)}, u32[]{:S(2)}, u32[]{:S(2)}) %collective-permute-start.3) | collective-permute-done | bytes 98336 | tf_op jit(solution)/shard_map/ppermute | solution.py:348
  65.4 0.1 collective-permute-done.4.got_stats
  65.5 0.0 copy-done.3
  65.5 0.6 copy-done.6
  66.1 0.0 all-to-all-done.got
  66.1 4.7 %all-to-all-start.1 = ((bf16[32,128,128]{2,1,0:T(8,128)(2,1)}), bf16[32,128,128]{2,1,0:T(8,128)(2,1)S(1)}, u32[]{:S(2)}, u32[]{:S(2)}) async-start(bf16[32,128,128]{2,1,0:T(8,128)(2,1)} %get-tuple-element.33), calls=%async_computation.1 | async-start | bytes 2097152 | tf_op jit(solution)/shard_map/all_to_all | solution.py:305
  70.8 0.0 copy-start.7
  70.8 0.7 copy-done.7
  71.5 0.3 last.1.refs_0_
  71.8 2.0 %collective-permute-start.5 = (bf16[416,128]{1,0:T(8,128)(2,1)S(1)}, bf16[416,128]{1,0:T(8,128)(2,1)S(1)}, u32[]{:S(2)}, u32[]{:S(2)}) collective-permute-start(bf16[416,128]{1,0:T(8,128)(2,1)S(1)} %last.1.refs_0_), channel_id=1, source_target_pairs={{0,2},{1,3},{2,0},{3,1},{4,6},{5,7},{6,4},{7,5},{8,10},{9,11},{10,... | collective-permute-start | bytes 319496 | tf_op jit(solution)/shard_map/ppermute | solution.py:348
  73.8 0.0 collective-permute-start.6
  73.8 9.8 %collective-permute-done.5.refs_1_ = bf16[416,128]{1,0:T(8,128)(2,1)S(1)} collective-permute-done((bf16[416,128]{1,0:T(8,128)(2,1)S(1)}, bf16[416,128]{1,0:T(8,128)(2,1)S(1)}, u32[]{:S(2)}, u32[]{:S(2)}) %collective-permute-start.5) | collective-permute-done | bytes 106528 | tf_op jit(solution)/shard_map/ppermute | solution.py:348
  83.6 0.0 collective-permute-start.7
  83.6 0.0 collective-permute-done.6.refs_2_
  83.6 1.3 %collective-permute-done.7.refs_3_ = bf16[416,128]{1,0:T(8,128)(2,1)S(1)} collective-permute-done((bf16[416,128]{1,0:T(8,128)(2,1)S(1)}, bf16[416,128]{1,0:T(8,128)(2,1)S(1)}, u32[]{:S(2)}, u32[]{:S(2)}) %collective-permute-start.7) | collective-permute-done | bytes 106528 | tf_op jit(solution)/shard_map/ppermute | solution.py:348
  84.9 0.8 copy-done.4
  85.7 1.4 %finish.1 = (bf16[4,384,128]{2,1,0:T(8,128)(2,1)}, f32[6,1,8]{2,1,0:T(1,128)}) custom-call(s32[1]{0:T(128)} %bitcast.me_ref, f32[2,32,128]{2,1,0:T(8,128)S(1)} %copy-done.4, bf16[416,128]{1,0:T(8,128)(2,1)S(1)} %last.1.refs_0_, bf16[416,128]{1,0:T(8,128)(2,1)S(1)} %collective-permute-done.5.refs_1_, bf16[416,128]{1,0:T(8,128)(2,1)S(1)} %collective-permute-done.6.refs_2_, ...), custom_call_target="tpu_custom_call" | custom-call | flops 1000 | bytes 1000 | tf_op jit(solution)/shard_map/finish/pallas_call | solution.py:399
  87.1 1.7 %place_keys.1 = bf16[6,8,128,128]{3,2,1,0:T(8,128)(2,1)} custom-call(s32[1]{0:T(128)} %bitcast.me_ref, s32[48]{0:T(128)S(1)} %copy-done.8, bf16[64,128,128]{2,1,0:T(8,128)(2,1)S(1)} %all-to-all-done.got), custom_call_target="tpu_custom_call" | custom-call | flops 1000 | bytes 1000 | tf_op jit(solution)/shard_map/place_keys/pallas_call | solution.py:384
  88.8 8.5 %all-to-all-done.1.got_rest = bf16[32,128,128]{2,1,0:T(8,128)(2,1)S(1)} async-done(((bf16[32,128,128]{2,1,0:T(8,128)(2,1)}), bf16[32,128,128]{2,1,0:T(8,128)(2,1)S(1)}, u32[]{:S(2)}, u32[]{:S(2)}) %all-to-all-start.1) | async-done | bytes 1048608 | tf_op jit(solution)/shard_map/all_to_all | solution.py:305
  97.3 1.7 %place_values.1 = bf16[6,8,128,128]{3,2,1,0:T(8,128)(2,1)} custom-call(s32[1]{0:T(128)} %bitcast.me_ref, s32[48]{0:T(128)S(1)} %copy-done.8, bf16[64,128,128]{2,1,0:T(8,128)(2,1)S(1)} %all-to-all-done.got, bf16[32,128,128]{2,1,0:T(8,128)(2,1)S(1)} %all-to-all-done.1.got_rest), custom_call_target="tpu_custom_call" | custom-call | flops 1000 | bytes 1000 | tf_op jit(solution)/shard_map/place_values/pallas_call | solution.py:384
  (4 shorter events, 0.0 us)
Async XLA Ops:
  4.1 7.6 %copy-start.2 = (bf16[4,6,64,128]{3,2,1,0:T(8,128)(2,1)S(1)}, bf16[4,6,64,128]{3,2,1,0:T(8,128)(2,1)}, u32[]{:S(2)}) copy-start(bf16[4,6,64,128]{3,2,1,0:T(8,128)(2,1)} %q_ref.1) | copy-start | bytes 1179652
  4.1 7.6 %copy-start.5 = (s32[4,6,16]{2,0,1:T(4,128)S(1)}, s32[4,6,16]{2,0,1:T(4,128)}, u32[]{:S(2)}) copy-start(s32[4,6,16]{2,0,1:T(4,128)} %param.10) | copy-start | bytes 4612
  4.1 7.6 %copy-start.8 = (s32[48]{0:T(128)S(1)}, s32[48]{0:T(128)}, u32[]{:S(2)}) copy-start(s32[48]{0:T(128)} %get-tuple-element.19.table) | copy-start | bytes 580
  4.2 7.6 %copy-start.9 = (s32[6]{0:T(128)S(1)}, s32[6]{0:T(128)}, u32[]{:S(2)}) copy-start(s32[6]{0:T(128)} %len_hbm.1) | copy-start | bytes 76
  4.2 61.9 %all-to-all-start = ((bf16[64,128,128]{2,1,0:T(8,128)(2,1)}), bf16[64,128,128]{2,1,0:T(8,128)(2,1)S(1)}, u32[]{:S(2)}, u32[]{:S(2)}) async-start(bf16[64,128,128]{2,1,0:T(8,128)(2,1)} %get-tuple-element.32), calls=%async_computation | async-start | bytes 4194304 | tf_op jit(solution)/shard_map/all_to_all | solution.py:305
  11.8 1.4 %copy-start = (bf16[6,8,128,128]{3,2,1,0:T(8,128)(2,1)S(1)}, bf16[6,8,128,128]{3,2,1,0:T(8,128)(2,1)}, u32[]{:S(2)}) copy-start(bf16[6,8,128,128]{3,2,1,0:T(8,128)(2,1)} %k_ref.3) | copy-start | bytes 4718596
  13.2 1.4 %copy-start.1 = (bf16[6,8,128,128]{3,2,1,0:T(8,128)(2,1)S(1)}, bf16[6,8,128,128]{3,2,1,0:T(8,128)(2,1)}, u32[]{:S(2)}) copy-start(bf16[6,8,128,128]{3,2,1,0:T(8,128)(2,1)} %v_ref.3) | copy-start | bytes 4718596
  18.0 47.4 %copy-start.3 = (f32[2,32,128]{2,1,0:T(8,128)}, f32[2,32,128]{2,1,0:T(8,128)S(1)}, u32[]{:S(2)}) copy-start(f32[2,32,128]{2,1,0:T(8,128)S(1)} %get-tuple-element.20.stats_ref) | copy-start | bytes 98308
  18.1 1.8 %collective-permute-start = (f32[2,400,128]{2,1,0:T(8,128)S(1)}, f32[2,400,128]{2,1,0:T(8,128)S(1)}, u32[]{:S(2)}, u32[]{:S(2)}) collective-permute-start(f32[2,400,128]{2,1,0:T(8,128)S(1)} %get-tuple-element.22), channel_id=1, source_target_pairs={{0,1},{1,0},{2,3},{3,2},{4,5},{5,4},{6,7},{7,6},{8,9},{9,8},{10,11... | collective-permute-start | bytes 1228808 | tf_op jit(solution)/shard_map/ppermute | solution.py:348
  20.3 14.0 %collective-permute-start.1 = (f32[400,128]{1,0:T(8,128)S(1)}, f32[400,128]{1,0:T(8,128)S(1)}, u32[]{:S(2)}, u32[]{:S(2)}) collective-permute-start(f32[400,128]{1,0:T(8,128)S(1)} %get-tuple-element.24), channel_id=1, source_target_pairs={{0,2},{1,3},{2,0},{3,1},{4,6},{5,7},{6,4},{7,5},{8,10},{9,11},{10,... | collective-permute-start | bytes 614408 | tf_op jit(solution)/shard_map/ppermute | solution.py:348
  34.6 16.4 %collective-permute-start.2 = (f32[400,128]{1,0:T(8,128)S(1)}, f32[400,128]{1,0:T(8,128)S(1)}, u32[]{:S(2)}, u32[]{:S(2)}) collective-permute-start(f32[400,128]{1,0:T(8,128)S(1)} %near.1.own), channel_id=1, source_target_pairs={{0,4},{1,5},{2,6},{3,7},{4,0},{5,1},{6,2},{7,3},{8,12},{9,13},{10,... | collective-permute-start | bytes 614408 | tf_op jit(solution)/shard_map/ppermute | solution.py:348
  51.5 13.8 %collective-permute-start.3 = (f16[384,128]{1,0:T(8,128)(2,1)S(1)}, f16[384,128]{1,0:T(8,128)(2,1)S(1)}, u32[]{:S(2)}, u32[]{:S(2)}) collective-permute-start(f16[384,128]{1,0:T(8,128)(2,1)S(1)} %get-tuple-element.34), channel_id=1, source_target_pairs={{0,8},{1,9},{2,10},{3,11},{4,12},{5,13},{6,14},{7,15},{8,0},{9,1},... | collective-permute-start | bytes 294920 | tf_op jit(solution)/shard_map/ppermute | solution.py:348
  56.0 9.5 %collective-permute-start.4 = (f32[24,128]{1,0:T(8,128)S(1)}, f32[24,128]{1,0:T(8,128)S(1)}, u32[]{:S(2)}, u32[]{:S(2)}) collective-permute-start(f32[24,128]{1,0:T(8,128)S(1)} %get-tuple-element.26.own_stats), channel_id=1, source_target_pairs={{0,8},{1,9},{2,10},{3,11},{4,12},{5,13},{6,14},{7,15},{8,0},{9,1},... | collective-permute-start | bytes 36872 | tf_op jit(solution)/shard_map/ppermute | solution.py:348
  65.5 0.6 copy-start.6
  66.1 31.3 %all-to-all-start.1 = ((bf16[32,128,128]{2,1,0:T(8,128)(2,1)}), bf16[32,128,128]{2,1,0:T(8,128)(2,1)S(1)}, u32[]{:S(2)}, u32[]{:S(2)}) async-start(bf16[32,128,128]{2,1,0:T(8,128)(2,1)} %get-tuple-element.33), calls=%async_computation.1 | async-start | bytes 2097152 | tf_op jit(solution)/shard_map/all_to_all | solution.py:305
  70.8 0.7 copy-start.7
  71.8 11.8 %collective-permute-start.5 = (bf16[416,128]{1,0:T(8,128)(2,1)S(1)}, bf16[416,128]{1,0:T(8,128)(2,1)S(1)}, u32[]{:S(2)}, u32[]{:S(2)}) collective-permute-start(bf16[416,128]{1,0:T(8,128)(2,1)S(1)} %last.1.refs_0_), channel_id=1, source_target_pairs={{0,2},{1,3},{2,0},{3,1},{4,6},{5,7},{6,4},{7,5},{8,10},{9,11},{10,... | collective-permute-start | bytes 319496 | tf_op jit(solution)/shard_map/ppermute | solution.py:348
  73.8 9.8 %collective-permute-start.6 = (bf16[416,128]{1,0:T(8,128)(2,1)S(1)}, bf16[416,128]{1,0:T(8,128)(2,1)S(1)}, u32[]{:S(2)}, u32[]{:S(2)}) collective-permute-start(bf16[416,128]{1,0:T(8,128)(2,1)S(1)} %last.1.refs_0_), channel_id=1, source_target_pairs={{0,1},{1,0},{2,3},{3,2},{4,5},{5,4},{6,7},{7,6},{8,9},{9,8},{10,11... | collective-permute-start | bytes 319496 | tf_op jit(solution)/shard_map/ppermute | solution.py:348
  83.6 1.3 %collective-permute-start.7 = (bf16[416,128]{1,0:T(8,128)(2,1)S(1)}, bf16[416,128]{1,0:T(8,128)(2,1)S(1)}, u32[]{:S(2)}, u32[]{:S(2)}) collective-permute-start(bf16[416,128]{1,0:T(8,128)(2,1)S(1)} %collective-permute-done.5.refs_1_), channel_id=1, source_target_pairs={{0,1},{1,0},{2,3},{3,2},{4,5},{5,4},{6,7},{7,6},{8,9},{9,8},{10,11... | collective-permute-start | bytes 319496 | tf_op jit(solution)/shard_map/ppermute | solution.py:348
  84.9 0.8 copy-start.4

commit v7 on v2

--- a/solution.py
+++ b/solution.py
@@ -22,7 +22,7 @@
 COST = pl.CostEstimate(flops=1000, bytes_accessed=1000, transcendentals=0)
 
 
-def stage_kernel(devices, group, me_ref, dest_hbm, k_ref, v_ref, buf, table, k_vm, v_vm, dest, counts, sem, load_sem):
+def stage_kernel(devices, group, dest_hbm, k_ref, v_ref, buf, table, k_vm, v_vm, dest, counts, sem, load_sem):
     rows, heads = k_ref.shape[:2]
     small = pltpu.make_async_copy(dest_hbm, dest, sem.at[0])
     small.start()
@@ -32,7 +32,7 @@
             copy = pltpu.make_async_copy(src.at[row], dst.at[row], load_sem.at[which, row])
             copy.start()
             loads.append(copy)
-    me = me_ref[0]
+    me = lax.axis_index("ctx")
 
     def clear(i, carry):
         counts[i] = 0
@@ -46,7 +46,7 @@
         loads[2 * row].wait()
         loads[2 * row + 1].wait()
 
-        for head in range(heads):
+        def send(head, carry):
             offset = dest[row, head, 0]
             rank = counts[offset]
             counts[offset] = rank + 1
@@ -54,13 +54,16 @@
             slot = jnp.bitwise_and(me + offset, devices - 1) * group + rank
             pltpu.make_async_copy(k_vm.at[row, head], buf.at[slot, 0], sem.at[1]).start()
             pltpu.make_async_copy(v_vm.at[row, head], buf.at[slot, 1], sem.at[2]).start()
+            return carry
+
+        lax.fori_loop(0, heads, send, 0)
     pltpu.make_async_copy(k_ref, k_vm, sem.at[1]).wait()
     pltpu.make_async_copy(v_ref, v_vm, sem.at[2]).wait()
 
 
 def attend_kernel(
     levels,
-    me_ref, table, len_hbm, kept_hbm, q_ref, k_ref, v_ref,
+    table, len_hbm, kept_hbm, q_ref, k_ref, v_ref,
     stats_ref, *rest,
 ):
     chunks = rest[:levels // 2]
@@ -68,7 +71,7 @@
     rows, heads, tile, width = k_ref.shape
     steps, _, q_heads, _ = q_ref.shape
     per = q_heads // heads
-    me = me_ref[0]
+    me = lax.axis_index("ctx")
 
     small = [
         pltpu.make_async_copy(len_hbm, len_ref, small_sem.at[0]),
@@ -151,8 +154,8 @@
     return peak, total, summed
 
 
-def merge_kernel(bit, pairs, per, me_ref, own, got, *outs):
-    swap = lax.rem(me_ref[0] // bit, 2) == 1
+def merge_kernel(bit, pairs, per, own, got, *outs):
+    swap = lax.rem(lax.axis_index("ctx") // bit, 2) == 1
     base = pairs * per
     for i, out in enumerate(outs):
         x, y = (own, got) if len(outs) == 1 else (own.at[i], got.at[i])
@@ -177,8 +180,8 @@
     stats[2 * per:, :] = scales
 
 
-def last_kernel(bit, pairs, per, me_ref, own, got, own_stats, got_stats, out):
-    swap = lax.rem(me_ref[0] // bit, 2) == 1
+def last_kernel(bit, pairs, per, own, got, own_stats, got_stats, out):
+    swap = lax.rem(lax.axis_index("ctx") // bit, 2) == 1
     base = pairs * per
     peak, total, summed = merge(swap, own, got, pairs, per, own_stats, got_stats)
     lane = lax.broadcasted_iota(jnp.int32, peak.shape, 1)
@@ -203,12 +206,13 @@
     out[base + 2 * per:base + 4 * per, :] = parts[2].astype(BF16)
 
 
-def finish_kernel(pairs, per, heads, levels, me_ref, stats_ref, *refs):
-    ins, (out, mass_ref, sem) = refs[:levels], refs[levels:]
+def finish_kernel(pairs, per, heads, levels, stats_ref, *refs):
+    me = lax.axis_index("ctx")
+    ins, (out, mass_ref, mass_vm, sem) = refs[:levels], refs[levels:]
     base = pairs * per
     copies = [
         pltpu.make_async_copy(
-            ins[level].at[:base], out.at[jnp.bitwise_xor(place_of(me_ref[0]), level)], sem.at[level]
+            ins[level].at[:base], out.at[jnp.bitwise_xor(place_of(me), level)], sem.at[level]
         )
         for level in range(levels)
     ]
@@ -226,15 +230,16 @@
         mass = mass + stats_ref[1, at:at + per, :] * coefficient
     mass = jnp.sum(mass, axis=0, keepdims=True)
     for row in range(pairs // heads):
-        mass_ref[row] = mass[:, row * heads:(row + 1) * heads]
+        mass_vm[row] = mass[:, row * heads:(row + 1) * heads]
+    copies.append(pltpu.make_async_copy(mass_vm, mass_ref, sem.at[levels]))
+    copies[-1].start()
     for copy in copies:
         copy.wait()
 
 
-def place_kernel(devices, group, me_ref, table, got_ref, k_ref, v_ref, me_out, sem):
+def place_kernel(devices, group, table, got_ref, k_ref, v_ref, sem):
     heads = k_ref.shape[1]
-    me = me_ref[0]
-    me_out[0] = me
+    me = lax.axis_index("ctx")
     for offset in range(devices):
         source = jnp.bitwise_and(me + devices - offset, devices - 1)
         for k in range(group):
@@ -261,7 +266,6 @@
     assert steps == levels and tile_dest.shape[2] == devices and pairs % 2 == 0 and pairs <= LANES // 2
     assert devices > levels and devices & (devices - 1) == 0 and width == LANES
 
-    me = lax.axis_index("ctx").astype(jnp.int32).reshape(1)
     kept = jnp.transpose(kept_tiles, (1, 0, 2))
     block_rows = rows * q_heads + 2 * per
     block_type = jax.ShapeDtypeStruct((block_rows, width), F32)
@@ -271,7 +275,7 @@
     tiles_out, table = pl.pallas_call(
         functools.partial(stage_kernel, devices, group),
         out_shape=[tiles_type, jax.ShapeDtypeStruct((devices * group,), jnp.int32)],
-        in_specs=[SMEM, HBM, HBM, HBM],
+        in_specs=[HBM, HBM, HBM],
         out_specs=[HBM, SMEM],
         scratch_shapes=[
             pltpu.VMEM(key_cache.shape, BF16),
@@ -284,7 +288,7 @@
         compiler_params=WHOLE,
         cost_estimate=COST,
         name="stage",
-    )(me, tile_dest, key_cache, value_cache)
+    )(tile_dest, key_cache, value_cache)
     tiles_in = lax.all_to_all(tiles_out, "ctx", split_axis=0, concat_axis=0, tiled=True)
 
     stats, *chunks = pl.pallas_call(
@@ -292,7 +296,7 @@
         out_shape=[
             jax.ShapeDtypeStruct((2, steps * per, LANES), F32),
         ] + [jax.ShapeDtypeStruct((2, block_rows, width), F32)] * 2,
-        in_specs=[SMEM, SMEM, HBM, HBM, VMEM, VMEM, VMEM],
+        in_specs=[SMEM, HBM, HBM, VMEM, VMEM, VMEM],
         out_specs=[VMEM] * 3,
         scratch_shapes=[
             pltpu.SMEM(row_lengths.shape, jnp.int32),
@@ -302,7 +306,7 @@
         compiler_params=PARAMS,
         cost_estimate=COST,
         name="attend",
-    )(me, table, row_lengths, kept, queries, key_cache, value_cache)
+    )(table, row_lengths, kept, queries, key_cache, value_cache)
 
     def flip(x, bit):
         return lax.ppermute(x, "ctx", [(i, i ^ bit) for i in range(devices)])
@@ -311,7 +315,7 @@
         return pl.pallas_call(
             kernel,
             out_shape=out_shape,
-            in_specs=[SMEM if x is me or x.shape == (1,) else VMEM for x in operands],
+            in_specs=[VMEM] * len(operands),
             out_specs=[VMEM] * len(out_shape),
             compiler_params=PARAMS,
             cost_estimate=COST,
@@ -319,7 +323,7 @@
         )(*operands)
 
     def merged(name, bit, own, got, out_shape):
-        return local_call(functools.partial(merge_kernel, bit, pairs, per), name, out_shape, me, own, got)
+        return local_call(functools.partial(merge_kernel, bit, pairs, per), name, out_shape, own, got)
 
     block, sent = merged("core", 1, chunks[0], flip(chunks[1], 1), [block_type] * 2)
     block, = merged("near", 2, block, flip(sent, 2), [block_type])
@@ -332,27 +336,27 @@
     sums, sum_stats = local_call(functools.partial(scale_kernel, pairs, per), "scale", [sums_type, stats_type], block)
     sums = lax.reduce_precision(sums, 5, 10)
     got = flip(sums.astype(jnp.float16), bit).astype(F32)
-    moved_keys, moved_values, me_next = pl.pallas_call(
+    message, = local_call(
+        functools.partial(last_kernel, bit, pairs, per), "last", [message_type],
+        sums, got, sum_stats, flip(sum_stats, bit),
+    )
+    other = flip(message, 2)
+
+    moved_keys, moved_values = pl.pallas_call(
         functools.partial(place_kernel, devices, group),
         out_shape=[
             jax.ShapeDtypeStruct(key_cache.shape, BF16),
             jax.ShapeDtypeStruct(value_cache.shape, BF16),
-            jax.ShapeDtypeStruct((1,), jnp.int32),
         ],
-        in_specs=[SMEM, SMEM, ANY],
-        out_specs=[HBM, HBM, SMEM],
+        in_specs=[SMEM, ANY],
+        out_specs=[HBM, HBM],
         scratch_shapes=[pltpu.SemaphoreType.DMA((2,))],
         compiler_params=PARAMS,
         cost_estimate=COST,
         name="place",
-    )(me, table, tiles_in)
-
-
-    message, = local_call(
-        functools.partial(last_kernel, bit, pairs, per), "last", [message_type],
-        me_next, sums, got, sum_stats, flip(sum_stats, bit),
-    )
-    other = flip(message, 2)
+    )(table, tiles_in)
+
+    other, moved_keys = lax.optimization_barrier((other, moved_keys))
     arrived = [message, other, flip(message, 1), flip(other, 1)]
 
     attn_out, mass = pl.pallas_call(
@@ -361,13 +365,13 @@
             jax.ShapeDtypeStruct((steps, rows * q_heads, width), BF16),
             jax.ShapeDtypeStruct((rows, 1, heads), F32),
         ],
-        in_specs=[SMEM, VMEM] + [VMEM] * levels,
-        out_specs=[HBM, VMEM],
-        scratch_shapes=[pltpu.SemaphoreType.DMA((levels,))],
+        in_specs=[VMEM] * (1 + levels),
+        out_specs=[HBM, HBM],
+        scratch_shapes=[pltpu.VMEM((rows, 1, heads), F32), pltpu.SemaphoreType.DMA((levels + 1,))],
         compiler_params=PARAMS,
         cost_estimate=COST,
         name="finish",
-    )(me, stats, *arrived)
+    )(stats, *arrived)
     return attn_out.reshape(queries.shape), jnp.transpose(mass, (0, 2, 1)), moved_keys, moved_values
 
 

time: 100 us -> 95.6 us (0.956)
  Pallas kernels: 13.8 us -> 11.3 us
  waiting for transfers between devices: 65.4 us -> 63.3 us
    ppermute x8, waiting for transfers between devices: 65.4 us -> 63.3 us  [flip(): return lax.ppermute(x, 'ctx', [(i, i ^ bit) for i in range(devices)])]
    pallas_call x5, Pallas kernels: 2.67 us -> 1.31 us  [local_call(): pl.pallas_call(kernel, out_shape=out_shape, in_specs=[VMEM] * len(operand...]
  transfers between devices with their start and end apart: 9 -> 9, of which waited for: 6 -> 7; matrix products, arithmetic and copies ran while one was open for 0% -> 0% of each run, Pallas kernels for 7% -> 7%
where the time goes in v7:
time: 95.6 us; the launch traced here: 95.3 us
  waiting for transfers between devices  63.3 us (66%)
  starting transfers between devices  16.2 us (17%)
  Pallas kernels  11.3 us (12%)
  local copies, waits for them, and re-layouts  3.49 us (4%)
    ppermute x8, waiting for transfers between devices, flip(): return lax.ppermute(x, 'ctx', [(i, i ^ bit) for i in range(devices)])  63.3 us
    ppermute x8, starting transfers between devices, flip(): return lax.ppermute(x, 'ctx', [(i, i ^ bit) for i in range(devices)])  8.72 us
    all_to_all x1, starting transfers between devices, local(): lax.all_to_all(tiles_out, 'ctx', split_axis=0, concat_axis=0, tiled=True)  7.52 us
    pallas_call x1, Pallas kernels, local(): pl.pallas_call(functools.partial(stage_kernel, devices, group), out_shape...  3.5 us
    unnamed x16, local copies, waits for them, and re-layouts  3.49 us
    pallas_call x1, Pallas kernels, local(): pl.pallas_call(functools.partial(attend_kernel, levels), out_shape=[jax.S...  3.46 us
    pallas_call x1, Pallas kernels, local(): pl.pallas_call(functools.partial(place_kernel, devices, group), out_shape...  2.19 us
  transfers between devices with their start and end apart: 9, of which 7 were waited for; matrix products, arithmetic and copies ran while one was open for 0% of the time, Pallas kernels for 7%

profile of v7, /device:TPU:0, one launch (start us, length us, event | category | flops | bytes accessed | tf_op | source)
XLA Modules:
  0.0 95.3 jit_solution(13604578474519928252)
XLA Ops:
  0.6 3.5 %stage.1 = (bf16[48,2,128,128]{3,2,1,0:T(8,128)(2,1)}, s32[48]{0:T(128)}) custom-call(s32[6,8,16]{2,1,0:T(8,128)} %dest_hbm.1, bf16[6,8,128,128]{3,2,1,0:T(8,128)(2,1)} %k_ref.3, bf16[6,8,128,128]{3,2,1,0:T(8,128)(2,1)} %v_ref.3), custom_call_target="tpu_custom_call" | custom-call | flops 1000 | bytes 1000 | tf_op jit(solution)/shard_map/stage/pallas_call | solution.py:275
  4.1 0.0 copy-start.2
  4.2 0.0 copy-start.5
  4.2 0.0 copy-start.6
  4.2 7.5 %all-to-all-start = ((bf16[48,2,128,128]{3,2,1,0:T(8,128)(2,1)}), bf16[48,2,128,128]{3,2,1,0:T(8,128)(2,1)S(1)}, u32[]{:S(2)}, u32[]{:S(2)}) async-start(bf16[48,2,128,128]{3,2,1,0:T(8,128)(2,1)} %get-tuple-element.27), calls=%async_computation | async-start | bytes 6291456 | tf_op jit(solution)/shard_map/all_to_all | solution.py:292
  11.7 0.0 copy-done.2
  11.7 0.0 copy-done.5
  11.7 0.0 copy-done.6
  11.7 0.0 copy-start
  11.7 1.4 %copy-done = bf16[6,8,128,128]{3,2,1,0:T(8,128)(2,1)S(1)} copy-done((bf16[6,8,128,128]{3,2,1,0:T(8,128)(2,1)S(1)}, bf16[6,8,128,128]{3,2,1,0:T(8,128)(2,1)}, u32[]{:S(2)}) %copy-start) | copy-done | bytes 1572888
  13.1 0.0 copy-start.1
  13.1 1.4 %copy-done.1 = bf16[6,8,128,128]{3,2,1,0:T(8,128)(2,1)S(1)} copy-done((bf16[6,8,128,128]{3,2,1,0:T(8,128)(2,1)S(1)}, bf16[6,8,128,128]{3,2,1,0:T(8,128)(2,1)}, u32[]{:S(2)}) %copy-start.1) | copy-done | bytes 1572888
  14.5 0.0 copy-start.7
  14.6 0.7 copy-done.7
  15.2 3.5 %attend.1 = (f32[2,32,128]{2,1,0:T(8,128)S(1)}, f32[2,400,128]{2,1,0:T(8,128)S(1)}, f32[2,400,128]{2,1,0:T(8,128)S(1)}) custom-call(s32[48]{0:T(128)S(1)} %copy-done.6, s32[6]{0:T(128)S(1)} %copy-done.7, s32[6,4,16]{2,1,0:T(4,128)S(1)} %bitcast.3, bf16[4,6,64,128]{3,2,1,0:T(8,128)(2,1)S(1)} %copy-done.2, bf16[6,8,128,128]{3,2,1,0:T(8,128)(2,1)S(1)} %copy-done, ...), custom_call_target="tpu_custom_call" | custom-call | flops 1000 | bytes 1000 | tf_op jit(solution)/shard_map/attend/pallas_call | solution.py:294
  18.7 0.0 copy-start.3
  18.7 0.5 collective-permute-start
  19.2 1.4 %collective-permute-done.got = f32[2,400,128]{2,1,0:T(8,128)S(1)} collective-permute-done((f32[2,400,128]{2,1,0:T(8,128)S(1)}, f32[2,400,128]{2,1,0:T(8,128)S(1)}, u32[]{:S(2)}, u32[]{:S(2)}) %collective-permute-start) | collective-permute-done | bytes 409632 | tf_op jit(solution)/shard_map/ppermute | solution.py:312
  20.5 0.4 core.1
  20.9 2.0 %collective-permute-start.1 = (f32[400,128]{1,0:T(8,128)S(1)}, f32[400,128]{1,0:T(8,128)S(1)}, u32[]{:S(2)}, u32[]{:S(2)}) collective-permute-start(f32[400,128]{1,0:T(8,128)S(1)} %get-tuple-element.24), channel_id=1, source_target_pairs={{0,2},{1,3},{2,0},{3,1},{4,6},{5,7},{6,4},{7,5},{8,10},{9,11},{10,... | collective-permute-start | bytes 614408 | tf_op jit(solution)/shard_map/ppermute | solution.py:312
  22.9 14.2 %collective-permute-done.1.got = f32[400,128]{1,0:T(8,128)S(1)} collective-permute-done((f32[400,128]{1,0:T(8,128)S(1)}, f32[400,128]{1,0:T(8,128)S(1)}, u32[]{:S(2)}, u32[]{:S(2)}) %collective-permute-start.1) | collective-permute-done | bytes 204832 | tf_op jit(solution)/shard_map/ppermute | solution.py:312
  37.1 0.2 near.1.own
  37.3 0.1 collective-permute-start.2
  37.4 30.5 %collective-permute-done.2.got = f32[400,128]{1,0:T(8,128)S(1)} collective-permute-done((f32[400,128]{1,0:T(8,128)S(1)}, f32[400,128]{1,0:T(8,128)S(1)}, u32[]{:S(2)}, u32[]{:S(2)}) %collective-permute-start.2) | collective-permute-done | bytes 204832 | tf_op jit(solution)/shard_map/ppermute | solution.py:312
  67.9 0.2 far.1.block
  68.1 0.1 scale.1
  68.3 0.1 reduce-precision_convert_fusion
  68.4 4.6 %collective-permute-start.3 = (f16[384,128]{1,0:T(8,128)(2,1)S(1)}, f16[384,128]{1,0:T(8,128)(2,1)S(1)}, u32[]{:S(2)}, u32[]{:S(2)}) collective-permute-start(f16[384,128]{1,0:T(8,128)(2,1)S(1)} %get-tuple-element.34), channel_id=1, source_target_pairs={{0,8},{1,9},{2,10},{3,11},{4,12},{5,13},{6,14},{7,15},{8,0},{9,1},... | collective-permute-start | bytes 294920 | tf_op jit(solution)/shard_map/ppermute | solution.py:312
  72.9 0.1 collective-permute-start.4
  73.0 14.9 %collective-permute-done.3 = f16[384,128]{1,0:T(8,128)(2,1)S(1)} collective-permute-done((f16[384,128]{1,0:T(8,128)(2,1)S(1)}, f16[384,128]{1,0:T(8,128)(2,1)S(1)}, u32[]{:S(2)}, u32[]{:S(2)}) %collective-permute-start.3) | collective-permute-done | bytes 98336 | tf_op jit(solution)/shard_map/ppermute | solution.py:312
  87.9 0.1 collective-permute-done.4.got_stats
  88.0 0.3 last.1.refs_0_
  88.3 0.0 copy-done.3
  88.4 1.6 %collective-permute-start.5 = (bf16[416,128]{1,0:T(8,128)(2,1)S(1)}, bf16[416,128]{1,0:T(8,128)(2,1)S(1)}, u32[]{:S(2)}, u32[]{:S(2)}) collective-permute-start(bf16[416,128]{1,0:T(8,128)(2,1)S(1)} %last.1.refs_0_), channel_id=1, source_target_pairs={{0,2},{1,3},{2,0},{3,1},{4,6},{5,7},{6,4},{7,5},{8,10},{9,11},{10,... | collective-permute-start | bytes 319496 | tf_op jit(solution)/shard_map/ppermute | solution.py:312
  89.9 0.0 copy-start.4
  89.9 0.0 collective-permute-start.6
  89.9 0.0 all-to-all-done.got_ref
  89.9 2.2 %place.1 = (bf16[6,8,128,128]{3,2,1,0:T(8,128)(2,1)}, bf16[6,8,128,128]{3,2,1,0:T(8,128)(2,1)}) custom-call(s32[48]{0:T(128)S(1)} %copy-done.6, bf16[48,2,128,128]{3,2,1,0:T(8,128)(2,1)S(1)} %all-to-all-done.got_ref), custom_call_target="tpu_custom_call" | custom-call | flops 1000 | bytes 1000 | tf_op jit(solution)/shard_map/place/pallas_call | solution.py:345
  92.1 1.0 %collective-permute-done.5.refs_1_ = bf16[416,128]{1,0:T(8,128)(2,1)S(1)} collective-permute-done((bf16[416,128]{1,0:T(8,128)(2,1)S(1)}, bf16[416,128]{1,0:T(8,128)(2,1)S(1)}, u32[]{:S(2)}, u32[]{:S(2)}) %collective-permute-start.5) | collective-permute-done | bytes 106528 | tf_op jit(solution)/shard_map/ppermute | solution.py:312
  93.1 0.0 collective-permute-start.7
  93.1 0.0 collective-permute-done.6.refs_2_
  93.1 1.3 %collective-permute-done.7.refs_3_ = bf16[416,128]{1,0:T(8,128)(2,1)S(1)} collective-permute-done((bf16[416,128]{1,0:T(8,128)(2,1)S(1)}, bf16[416,128]{1,0:T(8,128)(2,1)S(1)}, u32[]{:S(2)}, u32[]{:S(2)}) %collective-permute-start.7) | collective-permute-done | bytes 106528 | tf_op jit(solution)/shard_map/ppermute | solution.py:312
  94.4 0.0 copy-done.4
  94.4 0.9 finish.1
  (1 shorter events, 0.0 us)
Async XLA Ops:
  4.1 7.6 %copy-start.2 = (bf16[4,6,64,128]{3,2,1,0:T(8,128)(2,1)S(1)}, bf16[4,6,64,128]{3,2,1,0:T(8,128)(2,1)}, u32[]{:S(2)}) copy-start(bf16[4,6,64,128]{3,2,1,0:T(8,128)(2,1)} %q_ref.1) | copy-start | bytes 1179652
  4.2 7.6 %copy-start.5 = (s32[4,6,16]{2,0,1:T(4,128)S(1)}, s32[4,6,16]{2,0,1:T(4,128)}, u32[]{:S(2)}) copy-start(s32[4,6,16]{2,0,1:T(4,128)} %param.10) | copy-start | bytes 4612
  4.2 7.6 %copy-start.6 = (s32[48]{0:T(128)S(1)}, s32[48]{0:T(128)}, u32[]{:S(2)}) copy-start(s32[48]{0:T(128)} %get-tuple-element.19.table) | copy-start | bytes 580
  4.2 85.8 %all-to-all-start = ((bf16[48,2,128,128]{3,2,1,0:T(8,128)(2,1)}), bf16[48,2,128,128]{3,2,1,0:T(8,128)(2,1)S(1)}, u32[]{:S(2)}, u32[]{:S(2)}) async-start(bf16[48,2,128,128]{3,2,1,0:T(8,128)(2,1)} %get-tuple-element.27), calls=%async_computation | async-start | bytes 6291456 | tf_op jit(solution)/shard_map/all_to_all | solution.py:292
  11.7 1.4 %copy-start = (bf16[6,8,128,128]{3,2,1,0:T(8,128)(2,1)S(1)}, bf16[6,8,128,128]{3,2,1,0:T(8,128)(2,1)}, u32[]{:S(2)}) copy-start(bf16[6,8,128,128]{3,2,1,0:T(8,128)(2,1)} %k_ref.3) | copy-start | bytes 4718596
  13.1 1.4 %copy-start.1 = (bf16[6,8,128,128]{3,2,1,0:T(8,128)(2,1)S(1)}, bf16[6,8,128,128]{3,2,1,0:T(8,128)(2,1)}, u32[]{:S(2)}) copy-start(bf16[6,8,128,128]{3,2,1,0:T(8,128)(2,1)} %v_ref.3) | copy-start | bytes 4718596
  14.5 0.7 copy-start.7
  18.7 69.7 %copy-start.3 = (f32[2,32,128]{2,1,0:T(8,128)}, f32[2,32,128]{2,1,0:T(8,128)S(1)}, u32[]{:S(2)}) copy-start(f32[2,32,128]{2,1,0:T(8,128)S(1)} %get-tuple-element.20.stats_ref) | copy-start | bytes 98308
  18.7 1.8 %collective-permute-start = (f32[2,400,128]{2,1,0:T(8,128)S(1)}, f32[2,400,128]{2,1,0:T(8,128)S(1)}, u32[]{:S(2)}, u32[]{:S(2)}) collective-permute-start(f32[2,400,128]{2,1,0:T(8,128)S(1)} %get-tuple-element.22), channel_id=1, source_target_pairs={{0,1},{1,0},{2,3},{3,2},{4,5},{5,4},{6,7},{7,6},{8,9},{9,8},{10,11... | collective-permute-start | bytes 1228808 | tf_op jit(solution)/shard_map/ppermute | solution.py:312
  20.9 16.1 %collective-permute-start.1 = (f32[400,128]{1,0:T(8,128)S(1)}, f32[400,128]{1,0:T(8,128)S(1)}, u32[]{:S(2)}, u32[]{:S(2)}) collective-permute-start(f32[400,128]{1,0:T(8,128)S(1)} %get-tuple-element.24), channel_id=1, source_target_pairs={{0,2},{1,3},{2,0},{3,1},{4,6},{5,7},{6,4},{7,5},{8,10},{9,11},{10,... | collective-permute-start | bytes 614408 | tf_op jit(solution)/shard_map/ppermute | solution.py:312
  37.3 30.6 %collective-permute-start.2 = (f32[400,128]{1,0:T(8,128)S(1)}, f32[400,128]{1,0:T(8,128)S(1)}, u32[]{:S(2)}, u32[]{:S(2)}) collective-permute-start(f32[400,128]{1,0:T(8,128)S(1)} %near.1.own), channel_id=1, source_target_pairs={{0,4},{1,5},{2,6},{3,7},{4,0},{5,1},{6,2},{7,3},{8,12},{9,13},{10,... | collective-permute-start | bytes 614408 | tf_op jit(solution)/shard_map/ppermute | solution.py:312
  68.4 19.5 %collective-permute-start.3 = (f16[384,128]{1,0:T(8,128)(2,1)S(1)}, f16[384,128]{1,0:T(8,128)(2,1)S(1)}, u32[]{:S(2)}, u32[]{:S(2)}) collective-permute-start(f16[384,128]{1,0:T(8,128)(2,1)S(1)} %get-tuple-element.34), channel_id=1, source_target_pairs={{0,8},{1,9},{2,10},{3,11},{4,12},{5,13},{6,14},{7,15},{8,0},{9,1},... | collective-permute-start | bytes 294920 | tf_op jit(solution)/shard_map/ppermute | solution.py:312
  72.9 15.1 %collective-permute-start.4 = (f32[24,128]{1,0:T(8,128)S(1)}, f32[24,128]{1,0:T(8,128)S(1)}, u32[]{:S(2)}, u32[]{:S(2)}) collective-permute-start(f32[24,128]{1,0:T(8,128)S(1)} %get-tuple-element.26.own_stats), channel_id=1, source_target_pairs={{0,8},{1,9},{2,10},{3,11},{4,12},{5,13},{6,14},{7,15},{8,0},{9,1},... | collective-permute-start | bytes 36872 | tf_op jit(solution)/shard_map/ppermute | solution.py:312
  88.4 4.8 %collective-permute-start.5 = (bf16[416,128]{1,0:T(8,128)(2,1)S(1)}, bf16[416,128]{1,0:T(8,128)(2,1)S(1)}, u32[]{:S(2)}, u32[]{:S(2)}) collective-permute-start(bf16[416,128]{1,0:T(8,128)(2,1)S(1)} %last.1.refs_0_), channel_id=1, source_target_pairs={{0,2},{1,3},{2,0},{3,1},{4,6},{5,7},{6,4},{7,5},{8,10},{9,11},{10,... | collective-permute-start | bytes 319496 | tf_op jit(solution)/shard_map/ppermute | solution.py:312
  89.9 4.5 %copy-start.4 = (f32[2,32,128]{2,1,0:T(8,128)S(1)}, f32[2,32,128]{2,1,0:T(8,128)}, u32[]{:S(2)}) copy-start(f32[2,32,128]{2,1,0:T(8,128)} %copy-done.3) | copy-start | bytes 98308
  89.9 3.2 %collective-permute-start.6 = (bf16[416,128]{1,0:T(8,128)(2,1)S(1)}, bf16[416,128]{1,0:T(8,128)(2,1)S(1)}, u32[]{:S(2)}, u32[]{:S(2)}) collective-permute-start(bf16[416,128]{1,0:T(8,128)(2,1)S(1)} %last.1.refs_0_), channel_id=1, source_target_pairs={{0,1},{1,0},{2,3},{3,2},{4,5},{5,4},{6,7},{7,6},{8,9},{9,8},{10,11... | collective-permute-start | bytes 319496 | tf_op jit(solution)/shard_map/ppermute | solution.py:312
  93.1 1.3 %collective-permute-start.7 = (bf16[416,128]{1,0:T(8,128)(2,1)S(1)}, bf16[416,128]{1,0:T(8,128)(2,1)S(1)}, u32[]{:S(2)}, u32[]{:S(2)}) collective-permute-start(bf16[416,128]{1,0:T(8,128)(2,1)S(1)} %collective-permute-done.5.refs_1_), channel_id=1, source_target_pairs={{0,1},{1,0},{2,3},{3,2},{4,5},{5,4},{6,7},{7,6},{8,9},{9,8},{10,11... | collective-permute-start | bytes 319496 | tf_op jit(solution)/shard_map/ppermute | solution.py:312

commit v8 on v7

--- a/solution.py
+++ b/solution.py
@@ -166,6 +166,22 @@
         out[base + per:base + 2 * per, :] = total
 
 
+def halve_kernel(bit, pairs, per, own, got, kept, sent, work):
+    index = lax.axis_index("ctx")
+    peak, total, summed = merge(lax.rem(index // bit, 2) == 1, own, got, pairs, per)
+    share = pairs // 2
+    base = share * per
+    for half in range(2):
+        for i in range(share):
+            work[half, i * per:(i + 1) * per, :] = summed(half * share + i)
+        for i, x in enumerate((peak, total)):
+            at = base + i * per
+            work[half, at:at + per, :] = pltpu.roll(x, LANES - share, 1) if half else x
+    mine = lax.rem(index // (2 * bit), 2)
+    kept[...] = work[mine]
+    sent[...] = work[1 - mine]
+
+
 def scale_kernel(pairs, per, block, sums, stats):
     lane = lax.broadcasted_iota(jnp.int32, (per, LANES), 1)
     base = pairs * per
@@ -207,31 +223,40 @@
 
 
 def finish_kernel(pairs, per, heads, levels, stats_ref, *refs):
+    ins, (out, mass_ref, mass_vm, sem) = refs[:2 * levels], refs[2 * levels:]
     me = lax.axis_index("ctx")
-    ins, (out, mass_ref, mass_vm, sem) = refs[:levels], refs[levels:]
-    base = pairs * per
-    copies = [
-        pltpu.make_async_copy(
-            ins[level].at[:base], out.at[jnp.bitwise_xor(place_of(me), level)], sem.at[level]
-        )
-        for level in range(levels)
-    ]
-    for copy in copies:
-        copy.start()
+    share = pairs // 2
+    base = share * per
+    mine = lax.rem(me // levels, 2)
+    copies = []
+    for level in range(levels):
+        for far in range(2):
+            step, half = jnp.bitwise_xor(place_of(me), level), jnp.bitwise_xor(mine, far)
+            i = 2 * level + far
+            copies.append(pltpu.make_async_copy(ins[i].at[:base], out.at[step, half], sem.at[i]))
+            copies[i].start()
     lane = lax.broadcasted_iota(jnp.int32, (2 * per, LANES), 1)
-    mass = jnp.zeros((per, LANES), F32)
+    masses = [jnp.zeros((per, LANES), F32)] * 2
     for level in range(levels):
-        packed = ins[level][base:base + 2 * per, :].astype(F32)
-        third = ins[level][base + 2 * per:base + 4 * per, :].astype(F32)
-        both = third + pltpu.roll(packed, LANES // 2, 1) + packed
-        both = jnp.where(lane < pairs, both, 1.0)
-        at = level * per
-        coefficient = jnp.exp(jnp.minimum(stats_ref[0, at:at + per, :] - both[:per], 0.0)) / both[per:]
-        mass = mass + stats_ref[1, at:at + per, :] * coefficient
-    mass = jnp.sum(mass, axis=0, keepdims=True)
-    for row in range(pairs // heads):
-        mass_vm[row] = mass[:, row * heads:(row + 1) * heads]
-    copies.append(pltpu.make_async_copy(mass_vm, mass_ref, sem.at[levels]))
+        rows = slice(level * per, (level + 1) * per)
+        own_peak, own_total = stats_ref[0, rows, :], stats_ref[1, rows, :]
+        for far in range(2):
+            message = ins[2 * level + far]
+            packed = message[base:base + 2 * per, :].astype(F32)
+            third = message[base + 2 * per:base + 4 * per, :].astype(F32)
+            both = third + pltpu.roll(packed, LANES // 2, 1) + packed
+            both = jnp.where(lane < share, both, 1.0)
+            second = jnp.bitwise_xor(mine, far) == 1
+            peak, total = [
+                jnp.where(second, pltpu.roll(x, LANES - share, 1), x) for x in (own_peak, own_total)
+            ]
+            mass = total * (jnp.exp(jnp.minimum(peak - both[:per], 0.0)) / both[per:])
+            masses = [masses[0] + jnp.where(second, 0.0, mass), masses[1] + jnp.where(second, mass, 0.0)]
+    for half in range(2):
+        mass = jnp.sum(masses[half], axis=0, keepdims=True)
+        for i in range(share // heads):
+            mass_vm[half * (share // heads) + i] = mass[:, i * heads:(i + 1) * heads]
+    copies.append(pltpu.make_async_copy(mass_vm, mass_ref, sem.at[2 * levels]))
     copies[-1].start()
     for copy in copies:
         copy.wait()
@@ -264,12 +289,15 @@
     group = -(-pairs // devices)
     levels = 4
     assert steps == levels and tile_dest.shape[2] == devices and pairs % 2 == 0 and pairs <= LANES // 2
-    assert devices > levels and devices & (devices - 1) == 0 and width == LANES
+    assert devices > 2 * levels and devices & (devices - 1) == 0 and width == LANES
+    assert pairs % (2 * heads) == 0
+    share = pairs // 2
 
     kept = jnp.transpose(kept_tiles, (1, 0, 2))
     block_rows = rows * q_heads + 2 * per
     block_type = jax.ShapeDtypeStruct((block_rows, width), F32)
-    message_type = jax.ShapeDtypeStruct((rows * q_heads + 4 * per, width), BF16)
+    half_type = jax.ShapeDtypeStruct((share * per + 2 * per, width), F32)
+    message_type = jax.ShapeDtypeStruct((share * per + 4 * per, width), BF16)
     tiles_type = jax.ShapeDtypeStruct((devices * group, 2, span, width), BF16)
 
     tiles_out, table = pl.pallas_call(
@@ -311,36 +339,42 @@
     def flip(x, bit):
         return lax.ppermute(x, "ctx", [(i, i ^ bit) for i in range(devices)])
 
-    def local_call(kernel, name, out_shape, *operands):
+    def local_call(kernel, name, out_shape, *operands, scratch=()):
         return pl.pallas_call(
             kernel,
             out_shape=out_shape,
             in_specs=[VMEM] * len(operands),
             out_specs=[VMEM] * len(out_shape),
+            scratch_shapes=scratch,
             compiler_params=PARAMS,
             cost_estimate=COST,
             name=name,
         )(*operands)
 
-    def merged(name, bit, own, got, out_shape):
-        return local_call(functools.partial(merge_kernel, bit, pairs, per), name, out_shape, own, got)
-
-    block, sent = merged("core", 1, chunks[0], flip(chunks[1], 1), [block_type] * 2)
-    block, = merged("near", 2, block, flip(sent, 2), [block_type])
-    bit = levels
-    while 2 * bit < devices:
-        block, = merged("far", bit, block, flip(block, bit), [block_type])
+    block, sent = local_call(
+        functools.partial(merge_kernel, 1, pairs, per), "core", [block_type] * 2, chunks[0], flip(chunks[1], 1)
+    )
+    block, sent = local_call(
+        functools.partial(halve_kernel, 2, pairs, per), "near", [half_type] * 2, block, flip(sent, 2),
+        scratch=[pltpu.VMEM((2,) + half_type.shape, F32)],
+    )
+    bit, got = levels, flip(sent, levels)
+    while True:
+        block, = local_call(functools.partial(merge_kernel, bit, share, per), "far", [half_type], block, got)
         bit *= 2
-    sums_type = jax.ShapeDtypeStruct((rows * q_heads, width), F32)
+        if 2 * bit == devices:
+            break
+        got = flip(block, bit)
+    sums_type = jax.ShapeDtypeStruct((share * per, width), F32)
     stats_type = jax.ShapeDtypeStruct((3 * per, width), F32)
-    sums, sum_stats = local_call(functools.partial(scale_kernel, pairs, per), "scale", [sums_type, stats_type], block)
+    sums, sum_stats = local_call(functools.partial(scale_kernel, share, per), "scale", [sums_type, stats_type], block)
     sums = lax.reduce_precision(sums, 5, 10)
     got = flip(sums.astype(jnp.float16), bit).astype(F32)
     message, = local_call(
-        functools.partial(last_kernel, bit, pairs, per), "last", [message_type],
+        functools.partial(last_kernel, bit, share, per), "last", [message_type],
         sums, got, sum_stats, flip(sum_stats, bit),
     )
-    other = flip(message, 2)
+    near = [message, flip(message, levels), flip(message, 2), flip(message, 2 + levels)]
 
     moved_keys, moved_values = pl.pallas_call(
         functools.partial(place_kernel, devices, group),
@@ -356,18 +390,19 @@
         name="place",
     )(table, tiles_in)
 
-    other, moved_keys = lax.optimization_barrier((other, moved_keys))
-    arrived = [message, other, flip(message, 1), flip(other, 1)]
+    *forward, moved_keys = lax.optimization_barrier((*near[1:], moved_keys))
+    near = [message, *forward]
+    arrived = near + [flip(x, 1) for x in near]
 
     attn_out, mass = pl.pallas_call(
         functools.partial(finish_kernel, pairs, per, heads, levels),
         out_shape=[
-            jax.ShapeDtypeStruct((steps, rows * q_heads, width), BF16),
+            jax.ShapeDtypeStruct((steps, 2, share * per, width), BF16),
             jax.ShapeDtypeStruct((rows, 1, heads), F32),
         ],
-        in_specs=[VMEM] * (1 + levels),
+        in_specs=[VMEM] * (1 + 2 * levels),
         out_specs=[HBM, HBM],
-        scratch_shapes=[pltpu.VMEM((rows, 1, heads), F32), pltpu.SemaphoreType.DMA((levels + 1,))],
+        scratch_shapes=[pltpu.VMEM((rows, 1, heads), F32), pltpu.SemaphoreType.DMA((2 * levels + 1,))],
         compiler_params=PARAMS,
         cost_estimate=COST,
         name="finish",

time: 95.6 us -> 95 us (level)
  waiting for transfers between devices: 63.3 us -> 60 us
  starting transfers between devices: 16.2 us -> 19.3 us
    ppermute x8 -> x12, waiting for transfers between devices: 63.3 us -> 60 us  [flip(): return lax.ppermute(x, 'ctx', [(i, i ^ bit) for i in range(devices)])]
    ppermute x8 -> x12, starting transfers between devices: 8.72 us -> 11.7 us  [flip(): return lax.ppermute(x, 'ctx', [(i, i ^ bit) for i in range(devices)])]
  transfers between devices with their start and end apart: 9 -> 13, of which waited for: 7 -> 8; matrix products, arithmetic and copies ran while one was open for 0% -> 0% of each run, Pallas kernels for 7% -> 7%
where the time goes in v8:
time: 95 us; the launch traced here: 94.8 us
  waiting for transfers between devices  60 us (63%)
  starting transfers between devices  19.3 us (20%)
  Pallas kernels  11.1 us (12%)
  local copies, waits for them, and re-layouts  3.49 us (4%)
    ppermute x12, waiting for transfers between devices, flip(): return lax.ppermute(x, 'ctx', [(i, i ^ bit) for i in range(devices)])  60 us
    ppermute x12, starting transfers between devices, flip(): return lax.ppermute(x, 'ctx', [(i, i ^ bit) for i in range(devices)])  11.7 us
    all_to_all x1, starting transfers between devices, local(): lax.all_to_all(tiles_out, 'ctx', split_axis=0, concat_axis=0, tiled=True)  7.55 us
    pallas_call x1, Pallas kernels, local(): pl.pallas_call(functools.partial(stage_kernel, devices, group), out_shape...  3.51 us
    unnamed x16, local copies, waits for them, and re-layouts  3.49 us
    pallas_call x1, Pallas kernels, local(): pl.pallas_call(functools.partial(attend_kernel, levels), out_shape=[jax.S...  3.46 us
    pallas_call x1, Pallas kernels, local(): pl.pallas_call(functools.partial(place_kernel, devices, group), out_shape...  2.19 us
  transfers between devices with their start and end apart: 13, of which 8 were waited for; matrix products, arithmetic and copies ran while one was open for 0% of the time, Pallas kernels for 7%

profile of v8, /device:TPU:0, one launch (start us, length us, event | category | flops | bytes accessed | tf_op | source)
XLA Modules:
  0.0 94.8 jit_solution(5776747853155709893)
XLA Ops:
  0.6 3.5 %stage.1 = (bf16[48,2,128,128]{3,2,1,0:T(8,128)(2,1)}, s32[48]{0:T(128)}) custom-call(s32[6,8,16]{2,1,0:T(8,128)} %dest_hbm.1, bf16[6,8,128,128]{3,2,1,0:T(8,128)(2,1)} %k_ref.3, bf16[6,8,128,128]{3,2,1,0:T(8,128)(2,1)} %v_ref.3), custom_call_target="tpu_custom_call" | custom-call | flops 1000 | bytes 1000 | tf_op jit(solution)/shard_map/stage/pallas_call | solution.py:303
  4.1 0.0 copy-start.2
  4.2 0.0 copy-start.5
  4.2 0.0 copy-start.6
  4.2 7.5 %all-to-all-start = ((bf16[48,2,128,128]{3,2,1,0:T(8,128)(2,1)}), bf16[48,2,128,128]{3,2,1,0:T(8,128)(2,1)S(1)}, u32[]{:S(2)}, u32[]{:S(2)}) async-start(bf16[48,2,128,128]{3,2,1,0:T(8,128)(2,1)} %get-tuple-element.33), calls=%async_computation | async-start | bytes 6291456 | tf_op jit(solution)/shard_map/all_to_all | solution.py:320
  11.7 0.0 copy-done.2
  11.8 0.0 copy-done.5
  11.8 0.0 copy-done.6
  11.8 0.0 copy-start
  11.8 1.4 %copy-done = bf16[6,8,128,128]{3,2,1,0:T(8,128)(2,1)S(1)} copy-done((bf16[6,8,128,128]{3,2,1,0:T(8,128)(2,1)S(1)}, bf16[6,8,128,128]{3,2,1,0:T(8,128)(2,1)}, u32[]{:S(2)}) %copy-start) | copy-done | bytes 1572888
  13.2 1.4 %copy-done.1 = bf16[6,8,128,128]{3,2,1,0:T(8,128)(2,1)S(1)} copy-done((bf16[6,8,128,128]{3,2,1,0:T(8,128)(2,1)S(1)}, bf16[6,8,128,128]{3,2,1,0:T(8,128)(2,1)}, u32[]{:S(2)}) %copy-start.1) | copy-done | bytes 1572888
  14.6 0.7 copy-done.7
  15.2 3.5 %attend.1 = (f32[2,32,128]{2,1,0:T(8,128)S(1)}, f32[2,400,128]{2,1,0:T(8,128)S(1)}, f32[2,400,128]{2,1,0:T(8,128)S(1)}) custom-call(s32[48]{0:T(128)S(1)} %copy-done.6, s32[6]{0:T(128)S(1)} %copy-done.7, s32[6,4,16]{2,1,0:T(4,128)S(1)} %bitcast.3, bf16[4,6,64,128]{3,2,1,0:T(8,128)(2,1)S(1)} %copy-done.2, bf16[6,8,128,128]{3,2,1,0:T(8,128)(2,1)S(1)} %copy-done, ...), custom_call_target="tpu_custom_call" | custom-call | flops 1000 | bytes 1000 | tf_op jit(solution)/shard_map/attend/pallas_call | solution.py:322
  18.7 0.0 copy-start.3
  18.7 0.5 collective-permute-start
  19.2 1.4 %collective-permute-done.got = f32[2,400,128]{2,1,0:T(8,128)S(1)} collective-permute-done((f32[2,400,128]{2,1,0:T(8,128)S(1)}, f32[2,400,128]{2,1,0:T(8,128)S(1)}, u32[]{:S(2)}, u32[]{:S(2)}) %collective-permute-start) | collective-permute-done | bytes 409632 | tf_op jit(solution)/shard_map/ppermute | solution.py:340
  20.6 0.4 core.1
  21.0 2.0 %collective-permute-start.1 = (f32[400,128]{1,0:T(8,128)S(1)}, f32[400,128]{1,0:T(8,128)S(1)}, u32[]{:S(2)}, u32[]{:S(2)}) collective-permute-start(f32[400,128]{1,0:T(8,128)S(1)} %get-tuple-element.28), channel_id=1, source_target_pairs={{0,2},{1,3},{2,0},{3,1},{4,6},{5,7},{6,4},{7,5},{8,10},{9,11},{10,... | collective-permute-start | bytes 614408 | tf_op jit(solution)/shard_map/ppermute | solution.py:340
  22.9 14.2 %collective-permute-done.1.got = f32[400,128]{1,0:T(8,128)S(1)} collective-permute-done((f32[400,128]{1,0:T(8,128)S(1)}, f32[400,128]{1,0:T(8,128)S(1)}, u32[]{:S(2)}, u32[]{:S(2)}) %collective-permute-start.1) | collective-permute-done | bytes 204832 | tf_op jit(solution)/shard_map/ppermute | solution.py:340
  37.1 0.3 near.1
  37.4 0.1 collective-permute-start.2
  37.5 28.4 %collective-permute-done.2.got = f32[208,128]{1,0:T(8,128)S(1)} collective-permute-done((f32[208,128]{1,0:T(8,128)S(1)}, f32[208,128]{1,0:T(8,128)S(1)}, u32[]{:S(2)}, u32[]{:S(2)}) %collective-permute-start.2) | collective-permute-done | bytes 106528 | tf_op jit(solution)/shard_map/ppermute | solution.py:340
  65.8 0.2 far.1.block
  66.0 0.1 scale.1
  66.1 0.1 reduce-precision_convert_fusion
  66.1 4.6 %collective-permute-start.3 = (f16[192,128]{1,0:T(8,128)(2,1)S(1)}, f16[192,128]{1,0:T(8,128)(2,1)S(1)}, u32[]{:S(2)}, u32[]{:S(2)}) collective-permute-start(f16[192,128]{1,0:T(8,128)(2,1)S(1)} %get-tuple-element.42), channel_id=1, source_target_pairs={{0,8},{1,9},{2,10},{3,11},{4,12},{5,13},{6,14},{7,15},{8,0},{9,1},... | collective-permute-start | bytes 147464 | tf_op jit(solution)/shard_map/ppermute | solution.py:340
  70.7 0.1 collective-permute-start.4
  70.8 15.0 %collective-permute-done.3 = f16[192,128]{1,0:T(8,128)(2,1)S(1)} collective-permute-done((f16[192,128]{1,0:T(8,128)(2,1)S(1)}, f16[192,128]{1,0:T(8,128)(2,1)S(1)}, u32[]{:S(2)}, u32[]{:S(2)}) %collective-permute-start.3) | collective-permute-done | bytes 49184 | tf_op jit(solution)/shard_map/ppermute | solution.py:340
  85.8 0.1 collective-permute-done.4.got_stats
  86.0 0.2 last.1.refs_0_
  86.2 0.1 collective-permute-start.7
  86.2 1.6 %collective-permute-start.6 = (bf16[224,128]{1,0:T(8,128)(2,1)S(1)}, bf16[224,128]{1,0:T(8,128)(2,1)S(1)}, u32[]{:S(2)}, u32[]{:S(2)}) collective-permute-start(bf16[224,128]{1,0:T(8,128)(2,1)S(1)} %last.1.refs_0_), channel_id=1, source_target_pairs={{0,2},{1,3},{2,0},{3,1},{4,6},{5,7},{6,4},{7,5},{8,10},{9,11},{10,... | collective-permute-start | bytes 172040 | tf_op jit(solution)/shard_map/ppermute | solution.py:340
  87.8 1.9 %collective-permute-start.5 = (bf16[224,128]{1,0:T(8,128)(2,1)S(1)}, bf16[224,128]{1,0:T(8,128)(2,1)S(1)}, u32[]{:S(2)}, u32[]{:S(2)}) collective-permute-start(bf16[224,128]{1,0:T(8,128)(2,1)S(1)} %last.1.refs_0_), channel_id=1, source_target_pairs={{0,4},{1,5},{2,6},{3,7},{4,0},{5,1},{6,2},{7,3},{8,12},{9,13},{10,... | collective-permute-start | bytes 172040 | tf_op jit(solution)/shard_map/ppermute | solution.py:340
  89.7 0.0 collective-permute-start.8
  89.7 0.0 all-to-all-done.got_ref
  89.7 2.2 %place.1 = (bf16[6,8,128,128]{3,2,1,0:T(8,128)(2,1)}, bf16[6,8,128,128]{3,2,1,0:T(8,128)(2,1)}) custom-call(s32[48]{0:T(128)S(1)} %copy-done.6, bf16[48,2,128,128]{3,2,1,0:T(8,128)(2,1)S(1)} %all-to-all-done.got_ref), custom_call_target="tpu_custom_call" | custom-call | flops 1000 | bytes 1000 | tf_op jit(solution)/shard_map/place/pallas_call | solution.py:379
  91.9 0.0 collective-permute-done.7.refs_3_
  91.9 0.0 collective-permute-done.6.refs_2_
  91.9 0.0 collective-permute-done.5.refs_1_
  92.0 0.5 collective-permute-start.9
  92.5 0.1 collective-permute-start.10
  92.6 0.4 collective-permute-start.11
  93.0 0.0 collective-permute-done.8.refs_4_
  93.0 0.4 collective-permute-done.9.refs_5_
  93.4 0.4 collective-permute-done.10.refs_6_
  93.8 0.2 collective-permute-done.11.refs_7_
  93.9 0.0 copy-done.4
  93.9 0.8 finish.1
  (5 shorter events, 0.0 us)
Async XLA Ops:
  4.1 7.6 %copy-start.2 = (bf16[4,6,64,128]{3,2,1,0:T(8,128)(2,1)S(1)}, bf16[4,6,64,128]{3,2,1,0:T(8,128)(2,1)}, u32[]{:S(2)}) copy-start(bf16[4,6,64,128]{3,2,1,0:T(8,128)(2,1)} %q_ref.1) | copy-start | bytes 1179652
  4.2 7.6 %copy-start.5 = (s32[4,6,16]{2,0,1:T(4,128)S(1)}, s32[4,6,16]{2,0,1:T(4,128)}, u32[]{:S(2)}) copy-start(s32[4,6,16]{2,0,1:T(4,128)} %param.10) | copy-start | bytes 4612
  4.2 7.6 %copy-start.6 = (s32[48]{0:T(128)S(1)}, s32[48]{0:T(128)}, u32[]{:S(2)}) copy-start(s32[48]{0:T(128)} %get-tuple-element.23.table) | copy-start | bytes 580
  4.2 85.5 %all-to-all-start = ((bf16[48,2,128,128]{3,2,1,0:T(8,128)(2,1)}), bf16[48,2,128,128]{3,2,1,0:T(8,128)(2,1)S(1)}, u32[]{:S(2)}, u32[]{:S(2)}) async-start(bf16[48,2,128,128]{3,2,1,0:T(8,128)(2,1)} %get-tuple-element.33), calls=%async_computation | async-start | bytes 6291456 | tf_op jit(solution)/shard_map/all_to_all | solution.py:320
  11.8 1.4 %copy-start = (bf16[6,8,128,128]{3,2,1,0:T(8,128)(2,1)S(1)}, bf16[6,8,128,128]{3,2,1,0:T(8,128)(2,1)}, u32[]{:S(2)}) copy-start(bf16[6,8,128,128]{3,2,1,0:T(8,128)(2,1)} %k_ref.3) | copy-start | bytes 4718596
  13.2 1.4 %copy-start.1 = (bf16[6,8,128,128]{3,2,1,0:T(8,128)(2,1)S(1)}, bf16[6,8,128,128]{3,2,1,0:T(8,128)(2,1)}, u32[]{:S(2)}) copy-start(bf16[6,8,128,128]{3,2,1,0:T(8,128)(2,1)} %v_ref.3) | copy-start | bytes 4718596
  14.6 0.7 copy-start.7
  18.7 71.0 %copy-start.3 = (f32[2,32,128]{2,1,0:T(8,128)}, f32[2,32,128]{2,1,0:T(8,128)S(1)}, u32[]{:S(2)}) copy-start(f32[2,32,128]{2,1,0:T(8,128)S(1)} %get-tuple-element.24.stats_ref) | copy-start | bytes 98308
  18.7 1.8 %collective-permute-start = (f32[2,400,128]{2,1,0:T(8,128)S(1)}, f32[2,400,128]{2,1,0:T(8,128)S(1)}, u32[]{:S(2)}, u32[]{:S(2)}) collective-permute-start(f32[2,400,128]{2,1,0:T(8,128)S(1)} %get-tuple-element.26), channel_id=1, source_target_pairs={{0,1},{1,0},{2,3},{3,2},{4,5},{5,4},{6,7},{7,6},{8,9},{9,8},{10,11... | collective-permute-start | bytes 1228808 | tf_op jit(solution)/shard_map/ppermute | solution.py:340
  21.0 16.1 %collective-permute-start.1 = (f32[400,128]{1,0:T(8,128)S(1)}, f32[400,128]{1,0:T(8,128)S(1)}, u32[]{:S(2)}, u32[]{:S(2)}) collective-permute-start(f32[400,128]{1,0:T(8,128)S(1)} %get-tuple-element.28), channel_id=1, source_target_pairs={{0,2},{1,3},{2,0},{3,1},{4,6},{5,7},{6,4},{7,5},{8,10},{9,11},{10,... | collective-permute-start | bytes 614408 | tf_op jit(solution)/shard_map/ppermute | solution.py:340
  37.4 28.4 %collective-permute-start.2 = (f32[208,128]{1,0:T(8,128)S(1)}, f32[208,128]{1,0:T(8,128)S(1)}, u32[]{:S(2)}, u32[]{:S(2)}) collective-permute-start(f32[208,128]{1,0:T(8,128)S(1)} %get-tuple-element.30), channel_id=1, source_target_pairs={{0,4},{1,5},{2,6},{3,7},{4,0},{5,1},{6,2},{7,3},{8,12},{9,13},{10,... | collective-permute-start | bytes 319496 | tf_op jit(solution)/shard_map/ppermute | solution.py:340
  66.1 19.7 %collective-permute-start.3 = (f16[192,128]{1,0:T(8,128)(2,1)S(1)}, f16[192,128]{1,0:T(8,128)(2,1)S(1)}, u32[]{:S(2)}, u32[]{:S(2)}) collective-permute-start(f16[192,128]{1,0:T(8,128)(2,1)S(1)} %get-tuple-element.42), channel_id=1, source_target_pairs={{0,8},{1,9},{2,10},{3,11},{4,12},{5,13},{6,14},{7,15},{8,0},{9,1},... | collective-permute-start | bytes 147464 | tf_op jit(solution)/shard_map/ppermute | solution.py:340
  70.7 15.2 %collective-permute-start.4 = (f32[24,128]{1,0:T(8,128)S(1)}, f32[24,128]{1,0:T(8,128)S(1)}, u32[]{:S(2)}, u32[]{:S(2)}) collective-permute-start(f32[24,128]{1,0:T(8,128)S(1)} %get-tuple-element.32.own_stats), channel_id=1, source_target_pairs={{0,8},{1,9},{2,10},{3,11},{4,12},{5,13},{6,14},{7,15},{8,0},{9,1},... | collective-permute-start | bytes 36872 | tf_op jit(solution)/shard_map/ppermute | solution.py:340
  86.2 5.8 %collective-permute-start.7 = (bf16[224,128]{1,0:T(8,128)(2,1)S(1)}, bf16[224,128]{1,0:T(8,128)(2,1)S(1)}, u32[]{:S(2)}, u32[]{:S(2)}) collective-permute-start(bf16[224,128]{1,0:T(8,128)(2,1)S(1)} %last.1.refs_0_), channel_id=1, source_target_pairs={{0,6},{1,7},{2,4},{3,5},{4,2},{5,3},{6,0},{7,1},{8,14},{9,15},{10,... | collective-permute-start | bytes 172040 | tf_op jit(solution)/shard_map/ppermute | solution.py:340
  86.2 5.7 %collective-permute-start.6 = (bf16[224,128]{1,0:T(8,128)(2,1)S(1)}, bf16[224,128]{1,0:T(8,128)(2,1)S(1)}, u32[]{:S(2)}, u32[]{:S(2)}) collective-permute-start(bf16[224,128]{1,0:T(8,128)(2,1)S(1)} %last.1.refs_0_), channel_id=1, source_target_pairs={{0,2},{1,3},{2,0},{3,1},{4,6},{5,7},{6,4},{7,5},{8,10},{9,11},{10,... | collective-permute-start | bytes 172040 | tf_op jit(solution)/shard_map/ppermute | solution.py:340
  87.8 4.2 %collective-permute-start.5 = (bf16[224,128]{1,0:T(8,128)(2,1)S(1)}, bf16[224,128]{1,0:T(8,128)(2,1)S(1)}, u32[]{:S(2)}, u32[]{:S(2)}) collective-permute-start(bf16[224,128]{1,0:T(8,128)(2,1)S(1)} %last.1.refs_0_), channel_id=1, source_target_pairs={{0,4},{1,5},{2,6},{3,7},{4,0},{5,1},{6,2},{7,3},{8,12},{9,13},{10,... | collective-permute-start | bytes 172040 | tf_op jit(solution)/shard_map/ppermute | solution.py:340
  89.7 3.3 %collective-permute-start.8 = (bf16[224,128]{1,0:T(8,128)(2,1)S(1)}, bf16[224,128]{1,0:T(8,128)(2,1)S(1)}, u32[]{:S(2)}, u32[]{:S(2)}) collective-permute-start(bf16[224,128]{1,0:T(8,128)(2,1)S(1)} %last.1.refs_0_), channel_id=1, source_target_pairs={{0,1},{1,0},{2,3},{3,2},{4,5},{5,4},{6,7},{7,6},{8,9},{9,8},{10,11... | collective-permute-start | bytes 172040 | tf_op jit(solution)/shard_map/ppermute | solution.py:340
  89.7 4.2 %copy-start.4 = (f32[2,32,128]{2,1,0:T(8,128)S(1)}, f32[2,32,128]{2,1,0:T(8,128)}, u32[]{:S(2)}) copy-start(f32[2,32,128]{2,1,0:T(8,128)} %copy-done.3) | copy-start | bytes 98308
  92.0 1.4 %collective-permute-start.9 = (bf16[224,128]{1,0:T(8,128)(2,1)S(1)}, bf16[224,128]{1,0:T(8,128)(2,1)S(1)}, u32[]{:S(2)}, u32[]{:S(2)}) collective-permute-start(bf16[224,128]{1,0:T(8,128)(2,1)S(1)} %collective-permute-done.5.refs_1_), channel_id=1, source_target_pairs={{0,1},{1,0},{2,3},{3,2},{4,5},{5,4},{6,7},{7,6},{8,9},{9,8},{10,11... | collective-permute-start | bytes 172040 | tf_op jit(solution)/shard_map/ppermute | solution.py:340
  92.5 1.2 %collective-permute-start.10 = (bf16[224,128]{1,0:T(8,128)(2,1)S(1)}, bf16[224,128]{1,0:T(8,128)(2,1)S(1)}, u32[]{:S(2)}, u32[]{:S(2)}) collective-permute-start(bf16[224,128]{1,0:T(8,128)(2,1)S(1)} %collective-permute-done.6.refs_2_), channel_id=1, source_target_pairs={{0,1},{1,0},{2,3},{3,2},{4,5},{5,4},{6,7},{7,6},{8,9},{9,8},{10,11... | collective-permute-start | bytes 172040 | tf_op jit(solution)/shard_map/ppermute | solution.py:340
  92.6 1.3 %collective-permute-start.11 = (bf16[224,128]{1,0:T(8,128)(2,1)S(1)}, bf16[224,128]{1,0:T(8,128)(2,1)S(1)}, u32[]{:S(2)}, u32[]{:S(2)}) collective-permute-start(bf16[224,128]{1,0:T(8,128)(2,1)S(1)} %collective-permute-done.7.refs_3_), channel_id=1, source_target_pairs={{0,1},{1,0},{2,3},{3,2},{4,5},{5,4},{6,7},{7,6},{8,9},{9,8},{10,11... | collective-permute-start | bytes 172040 | tf_op jit(solution)/shard_map/ppermute | solution.py:340

commit v9 on v8

--- a/solution.py
+++ b/solution.py
@@ -22,7 +22,9 @@
 COST = pl.CostEstimate(flops=1000, bytes_accessed=1000, transcendentals=0)
 
 
-def stage_kernel(devices, group, dest_hbm, k_ref, v_ref, buf, table, k_vm, v_vm, dest, counts, sem, load_sem):
+def stage_kernel(
+    devices, group, first, dest_hbm, k_ref, v_ref, buf, buf_rest, table, k_vm, v_vm, dest, counts, sem, load_sem
+):
     rows, heads = k_ref.shape[:2]
     small = pltpu.make_async_copy(dest_hbm, dest, sem.at[0])
     small.start()
@@ -51,9 +53,18 @@
             rank = counts[offset]
             counts[offset] = rank + 1
             table[offset * group + rank] = row * heads + head
-            slot = jnp.bitwise_and(me + offset, devices - 1) * group + rank
-            pltpu.make_async_copy(k_vm.at[row, head], buf.at[slot, 0], sem.at[1]).start()
-            pltpu.make_async_copy(v_vm.at[row, head], buf.at[slot, 1], sem.at[2]).start()
+            target = jnp.bitwise_and(me + offset, devices - 1)
+            pltpu.make_async_copy(k_vm.at[row, head], buf.at[target * first + rank], sem.at[1]).start()
+
+            @pl.when(rank < first - group)
+            def _():
+                at = target * first + group + rank
+                pltpu.make_async_copy(v_vm.at[row, head], buf.at[at], sem.at[2]).start()
+
+            @pl.when(rank >= first - group)
+            def _():
+                at = target * (2 * group - first) + rank + group - first
+                pltpu.make_async_copy(v_vm.at[row, head], buf_rest.at[at], sem.at[2]).start()
             return carry
 
         lax.fori_loop(0, heads, send, 0)
@@ -262,22 +273,33 @@
         copy.wait()
 
 
-def place_kernel(devices, group, table, got_ref, k_ref, v_ref, sem):
-    heads = k_ref.shape[1]
+def place_keys_kernel(devices, group, first, table, got, out, sem):
+    heads = out.shape[1]
     me = lax.axis_index("ctx")
     for offset in range(devices):
         source = jnp.bitwise_and(me + devices - offset, devices - 1)
         for k in range(group):
-            pair = table[offset * group + k]
-
-            @pl.when(pair >= 0)
-            def _():
-                row, head = pair // heads, lax.rem(pair, heads)
-                for which, ref in enumerate((k_ref, v_ref)):
-                    src = got_ref.at[source * group + k, which]
-                    pltpu.make_async_copy(src, ref.at[row, head], sem.at[which]).start()
-    pltpu.make_async_copy(k_ref, k_ref, sem.at[0]).wait()
-    pltpu.make_async_copy(v_ref, v_ref, sem.at[1]).wait()
+            put(got.at[source * first + k], table[offset * group + k], heads, out, sem)
+    pltpu.make_async_copy(out, out, sem).wait()
+
+
+def place_values_kernel(devices, group, first, table, got, got_rest, out, sem):
+    heads = out.shape[1]
+    me = lax.axis_index("ctx")
+    rest = 2 * group - first
+    for offset in range(devices):
+        source = jnp.bitwise_and(me + devices - offset, devices - 1)
+        for k in range(group):
+            at = group + k
+            src = got.at[source * first + at] if at < first else got_rest.at[source * rest + at - first]
+            put(src, table[offset * group + k], heads, out, sem)
+    pltpu.make_async_copy(out, out, sem).wait()
+
+
+def put(src, pair, heads, out, sem):
+    @pl.when(pair >= 0)
+    def _():
+        pltpu.make_async_copy(src, out.at[pair // heads, lax.rem(pair, heads)], sem).start()
 
 
 def local(queries, key_cache, value_cache, row_lengths, kept_tiles, tile_dest):
@@ -298,13 +320,23 @@
     block_type = jax.ShapeDtypeStruct((block_rows, width), F32)
     half_type = jax.ShapeDtypeStruct((share * per + 2 * per, width), F32)
     message_type = jax.ShapeDtypeStruct((share * per + 4 * per, width), BF16)
-    tiles_type = jax.ShapeDtypeStruct((devices * group, 2, span, width), BF16)
-
-    tiles_out, table = pl.pallas_call(
-        functools.partial(stage_kernel, devices, group),
-        out_shape=[tiles_type, jax.ShapeDtypeStruct((devices * group,), jnp.int32)],
+    first = 2 * group - max(1, 2 * group // 3)
+
+    def tiles_type(count):
+        return jax.ShapeDtypeStruct((devices * count, span, width), BF16)
+
+    def exchange(x):
+        return lax.all_to_all(x, "ctx", split_axis=0, concat_axis=0, tiled=True)
+
+
+    tiles_out, rest_out, table = pl.pallas_call(
+        functools.partial(stage_kernel, devices, group, first),
+        out_shape=[
+            tiles_type(first), tiles_type(2 * group - first),
+            jax.ShapeDtypeStruct((devices * group,), jnp.int32),
+        ],
         in_specs=[HBM, HBM, HBM],
-        out_specs=[HBM, SMEM],
+        out_specs=[HBM, HBM, SMEM],
         scratch_shapes=[
             pltpu.VMEM(key_cache.shape, BF16),
             pltpu.VMEM(value_cache.shape, BF16),
@@ -317,7 +349,7 @@
         cost_estimate=COST,
         name="stage",
     )(tile_dest, key_cache, value_cache)
-    tiles_in = lax.all_to_all(tiles_out, "ctx", split_axis=0, concat_axis=0, tiled=True)
+    tiles_in = exchange(tiles_out)
 
     stats, *chunks = pl.pallas_call(
         functools.partial(attend_kernel, levels),
@@ -370,28 +402,27 @@
     sums, sum_stats = local_call(functools.partial(scale_kernel, share, per), "scale", [sums_type, stats_type], block)
     sums = lax.reduce_precision(sums, 5, 10)
     got = flip(sums.astype(jnp.float16), bit).astype(F32)
+    got, got_stats, rest_out = lax.optimization_barrier((got, flip(sum_stats, bit), rest_out))
+    rest_in = exchange(rest_out)
     message, = local_call(
-        functools.partial(last_kernel, bit, share, per), "last", [message_type],
-        sums, got, sum_stats, flip(sum_stats, bit),
+        functools.partial(last_kernel, bit, share, per), "last", [message_type], sums, got, sum_stats, got_stats,
     )
     near = [message, flip(message, levels), flip(message, 2), flip(message, 2 + levels)]
 
-    moved_keys, moved_values = pl.pallas_call(
-        functools.partial(place_kernel, devices, group),
-        out_shape=[
-            jax.ShapeDtypeStruct(key_cache.shape, BF16),
-            jax.ShapeDtypeStruct(value_cache.shape, BF16),
-        ],
-        in_specs=[SMEM, ANY],
-        out_specs=[HBM, HBM],
-        scratch_shapes=[pltpu.SemaphoreType.DMA((2,))],
-        compiler_params=PARAMS,
-        cost_estimate=COST,
-        name="place",
-    )(table, tiles_in)
-
-    *forward, moved_keys = lax.optimization_barrier((*near[1:], moved_keys))
-    near = [message, *forward]
+    def place(kernel, name, *got):
+        return pl.pallas_call(
+            functools.partial(kernel, devices, group, first),
+            out_shape=jax.ShapeDtypeStruct(key_cache.shape, BF16),
+            in_specs=[SMEM] + [ANY] * len(got),
+            out_specs=HBM,
+            scratch_shapes=[pltpu.SemaphoreType.DMA],
+            compiler_params=PARAMS,
+            cost_estimate=COST,
+            name=name,
+        )(table, *got)
+
+    moved_keys = place(place_keys_kernel, "place_keys", tiles_in)
+    moved_values = place(place_values_kernel, "place_values", tiles_in, rest_in)
     arrived = near + [flip(x, 1) for x in near]
 
     attn_out, mass = pl.pallas_call(

time: 95 us -> 94.8 us (level); the launches traced: 94.8 us -> 93.1 us
  waiting for transfers between devices: 60 us -> 54.7 us
  starting transfers between devices: 19.3 us -> 22.4 us
  Pallas kernels: 11.1 us -> 12.2 us
    ppermute x12, waiting for transfers between devices: 60 us -> 54.7 us  [flip(): return lax.ppermute(x, 'ctx', [(i, i ^ bit) for i in range(devices)])]
    all_to_all x1 -> x2, starting transfers between devices: 7.55 us -> 11.2 us  [exchange(): return lax.all_to_all(x, 'ctx', split_axis=0, concat_axis=0, tiled=True)]
    pallas_call x2 -> x3, Pallas kernels: 5.7 us -> 6.83 us  [the longest x1 3.48 us: local(): pl.pallas_call(functools.partial(stage_kernel, devices, group, first), ou...]
    unnamed x16 -> x12, local copies, waits for them, and re-layouts: 3.49 us -> 2.84 us
  transfers between devices with their start and end apart: 13 -> 14, of which waited for: 8 -> 10; matrix products, arithmetic and copies ran while one was open for 0% -> 0% of each run, Pallas kernels for 7% -> 8%
where the time goes in v9:
time: 94.8 us; the launch traced here: 93.1 us
  waiting for transfers between devices  54.7 us (58%)
  starting transfers between devices  22.4 us (24%)
  Pallas kernels  12.2 us (13%)
  local copies, waits for them, and re-layouts  2.84 us (3%)
    ppermute x12, waiting for transfers between devices, flip(): return lax.ppermute(x, 'ctx', [(i, i ^ bit) for i in range(devices)])  54.7 us
    all_to_all x2, starting transfers between devices, exchange(): return lax.all_to_all(x, 'ctx', split_axis=0, concat_axis=0, tiled=True)  11.2 us
    ppermute x12, starting transfers between devices, flip(): return lax.ppermute(x, 'ctx', [(i, i ^ bit) for i in range(devices)])  11.2 us
    pallas_call x1, Pallas kernels, local(): pl.pallas_call(functools.partial(stage_kernel, devices, group, first), ou...  3.48 us
    pallas_call x1, Pallas kernels, local(): pl.pallas_call(functools.partial(attend_kernel, levels), out_shape=[jax.S...  3.46 us
    pallas_call x2, Pallas kernels, place(): pl.pallas_call(functools.partial(kernel, devices, group, first), out_shap...  3.35 us
    unnamed x12, local copies, waits for them, and re-layouts  2.84 us
  transfers between devices with their start and end apart: 14, of which 10 were waited for; matrix products, arithmetic and copies ran while one was open for 0% of the time, Pallas kernels for 8%

profile of v9, /device:TPU:0, one launch (start us, length us, event | category | flops | bytes accessed | tf_op | source)
XLA Modules:
  0.0 93.1 jit_solution(7047964520311583040)
XLA Ops:
  0.6 3.5 %stage.1 = (bf16[64,128,128]{2,1,0:T(8,128)(2,1)}, bf16[32,128,128]{2,1,0:T(8,128)(2,1)}, s32[48]{0:T(128)}) custom-call(s32[6,8,16]{2,1,0:T(8,128)} %dest_hbm.1, bf16[6,8,128,128]{3,2,1,0:T(8,128)(2,1)} %k_ref.3, bf16[6,8,128,128]{3,2,1,0:T(8,128)(2,1)} %v_ref.3), custom_call_target="tpu_custom_call" | custom-call | flops 1000 | bytes 1000 | tf_op jit(solution)/shard_map/stage/pallas_call | solution.py:332
  4.1 0.0 copy-start.2
  4.1 0.0 copy-start.3
  4.1 0.0 copy-start.4
  4.2 0.0 copy-start.5
  4.2 7.5 %all-to-all-start = ((bf16[64,128,128]{2,1,0:T(8,128)(2,1)}), bf16[64,128,128]{2,1,0:T(8,128)(2,1)S(1)}, u32[]{:S(2)}, u32[]{:S(2)}) async-start(bf16[64,128,128]{2,1,0:T(8,128)(2,1)} %get-tuple-element.36), calls=%async_computation | async-start | bytes 4194304 | tf_op jit(solution)/shard_map/all_to_all | solution.py:329
  11.7 0.0 copy-done.2
  11.7 0.0 copy-done.3
  11.7 0.0 copy-start
  11.8 1.4 %copy-done = bf16[6,8,128,128]{3,2,1,0:T(8,128)(2,1)S(1)} copy-done((bf16[6,8,128,128]{3,2,1,0:T(8,128)(2,1)S(1)}, bf16[6,8,128,128]{3,2,1,0:T(8,128)(2,1)}, u32[]{:S(2)}) %copy-start) | copy-done | bytes 1572888
  13.2 1.4 %copy-done.1 = bf16[6,8,128,128]{3,2,1,0:T(8,128)(2,1)S(1)} copy-done((bf16[6,8,128,128]{3,2,1,0:T(8,128)(2,1)S(1)}, bf16[6,8,128,128]{3,2,1,0:T(8,128)(2,1)}, u32[]{:S(2)}) %copy-start.1) | copy-done | bytes 1572888
  14.6 3.5 %attend.1 = (f32[2,32,128]{2,1,0:T(8,128)S(1)}, f32[2,400,128]{2,1,0:T(8,128)S(1)}, f32[2,400,128]{2,1,0:T(8,128)S(1)}) custom-call(s32[48]{0:T(128)S(1)} %copy-done.4, s32[6]{0:T(128)S(1)} %copy-done.5, s32[6,4,16]{2,1,0:T(4,128)S(1)} %bitcast.3, bf16[4,6,64,128]{3,2,1,0:T(8,128)(2,1)S(1)} %copy-done.2, bf16[6,8,128,128]{3,2,1,0:T(8,128)(2,1)S(1)} %copy-done, ...), custom_call_target="tpu_custom_call" | custom-call | flops 1000 | bytes 1000 | tf_op jit(solution)/shard_map/attend/pallas_call | solution.py:354
  18.0 0.5 collective-permute-start
  18.5 1.4 %collective-permute-done.got = f32[2,400,128]{2,1,0:T(8,128)S(1)} collective-permute-done((f32[2,400,128]{2,1,0:T(8,128)S(1)}, f32[2,400,128]{2,1,0:T(8,128)S(1)}, u32[]{:S(2)}, u32[]{:S(2)}) %collective-permute-start) | collective-permute-done | bytes 409632 | tf_op jit(solution)/shard_map/ppermute | solution.py:372
  19.9 0.4 core.1
  20.3 2.0 %collective-permute-start.1 = (f32[400,128]{1,0:T(8,128)S(1)}, f32[400,128]{1,0:T(8,128)S(1)}, u32[]{:S(2)}, u32[]{:S(2)}) collective-permute-start(f32[400,128]{1,0:T(8,128)S(1)} %get-tuple-element.26), channel_id=1, source_target_pairs={{0,2},{1,3},{2,0},{3,1},{4,6},{5,7},{6,4},{7,5},{8,10},{9,11},{10,... | collective-permute-start | bytes 614408 | tf_op jit(solution)/shard_map/ppermute | solution.py:372
  22.2 13.0 %collective-permute-done.1.got = f32[400,128]{1,0:T(8,128)S(1)} collective-permute-done((f32[400,128]{1,0:T(8,128)S(1)}, f32[400,128]{1,0:T(8,128)S(1)}, u32[]{:S(2)}, u32[]{:S(2)}) %collective-permute-start.1) | collective-permute-done | bytes 204832 | tf_op jit(solution)/shard_map/ppermute | solution.py:372
  35.3 0.3 near.1
  35.5 0.1 collective-permute-start.2
  35.6 13.3 %collective-permute-done.2.got = f32[208,128]{1,0:T(8,128)S(1)} collective-permute-done((f32[208,128]{1,0:T(8,128)S(1)}, f32[208,128]{1,0:T(8,128)S(1)}, u32[]{:S(2)}, u32[]{:S(2)}) %collective-permute-start.2) | collective-permute-done | bytes 106528 | tf_op jit(solution)/shard_map/ppermute | solution.py:372
  48.9 0.2 far.1.block
  49.0 0.1 scale.1
  49.1 0.1 reduce-precision_convert_fusion
  49.2 4.6 %collective-permute-start.3 = (f16[192,128]{1,0:T(8,128)(2,1)S(1)}, f16[192,128]{1,0:T(8,128)(2,1)S(1)}, u32[]{:S(2)}, u32[]{:S(2)}) collective-permute-start(f16[192,128]{1,0:T(8,128)(2,1)S(1)} %get-tuple-element.38), channel_id=1, source_target_pairs={{0,8},{1,9},{2,10},{3,11},{4,12},{5,13},{6,14},{7,15},{8,0},{9,1},... | collective-permute-start | bytes 147464 | tf_op jit(solution)/shard_map/ppermute | solution.py:372
  53.8 0.1 collective-permute-start.4
  53.9 9.4 %collective-permute-done.3 = f16[192,128]{1,0:T(8,128)(2,1)S(1)} collective-permute-done((f16[192,128]{1,0:T(8,128)(2,1)S(1)}, f16[192,128]{1,0:T(8,128)(2,1)S(1)}, u32[]{:S(2)}, u32[]{:S(2)}) %collective-permute-start.3) | collective-permute-done | bytes 49184 | tf_op jit(solution)/shard_map/ppermute | solution.py:372
  63.3 0.1 collective-permute-done.4.got_stats
  63.4 0.0 all-to-all-done.got
  63.4 3.7 %all-to-all-start.1 = ((bf16[32,128,128]{2,1,0:T(8,128)(2,1)}), bf16[32,128,128]{2,1,0:T(8,128)(2,1)S(1)}, u32[]{:S(2)}, u32[]{:S(2)}) async-start(bf16[32,128,128]{2,1,0:T(8,128)(2,1)} %get-tuple-element.37), calls=%async_computation.1 | async-start | bytes 2097152 | tf_op jit(solution)/shard_map/all_to_all | solution.py:329
  67.1 0.2 last.1.refs_0_
  67.3 2.9 %collective-permute-start.7 = (bf16[224,128]{1,0:T(8,128)(2,1)S(1)}, bf16[224,128]{1,0:T(8,128)(2,1)S(1)}, u32[]{:S(2)}, u32[]{:S(2)}) collective-permute-start(bf16[224,128]{1,0:T(8,128)(2,1)S(1)} %last.1.refs_0_), channel_id=1, source_target_pairs={{0,6},{1,7},{2,4},{3,5},{4,2},{5,3},{6,0},{7,1},{8,14},{9,15},{10,... | collective-permute-start | bytes 172040 | tf_op jit(solution)/shard_map/ppermute | solution.py:372
  70.2 0.6 collective-permute-start.6
  70.8 0.1 collective-permute-start.5
  70.9 0.0 collective-permute-start.8
  70.9 15.7 %collective-permute-done.7.refs_3_ = bf16[224,128]{1,0:T(8,128)(2,1)S(1)} collective-permute-done((bf16[224,128]{1,0:T(8,128)(2,1)S(1)}, bf16[224,128]{1,0:T(8,128)(2,1)S(1)}, u32[]{:S(2)}, u32[]{:S(2)}) %collective-permute-start.7) | collective-permute-done | bytes 57376 | tf_op jit(solution)/shard_map/ppermute | solution.py:372
  86.6 0.0 collective-permute-start.11
  86.6 0.0 collective-permute-done.6.refs_2_
  86.6 0.5 collective-permute-start.10
  87.1 0.5 collective-permute-done.5.refs_1_
  87.7 0.0 collective-permute-start.9
  87.7 0.0 collective-permute-done.8.refs_4_
  87.7 0.2 collective-permute-done.11.refs_7_
  87.9 0.2 collective-permute-done.10.refs_6_
  88.0 0.9 collective-permute-done.9.refs_5_
  88.9 0.8 finish.1
  89.7 1.7 %place_keys.1 = bf16[6,8,128,128]{3,2,1,0:T(8,128)(2,1)} custom-call(s32[48]{0:T(128)S(1)} %copy-done.4, bf16[64,128,128]{2,1,0:T(8,128)(2,1)S(1)} %all-to-all-done.got), custom_call_target="tpu_custom_call" | custom-call | flops 1000 | bytes 1000 | tf_op jit(solution)/shard_map/place_keys/pallas_call | solution.py:413
  91.4 0.0 all-to-all-done.1.got_rest
  91.4 1.7 %place_values.1 = bf16[6,8,128,128]{3,2,1,0:T(8,128)(2,1)} custom-call(s32[48]{0:T(128)S(1)} %copy-done.4, bf16[64,128,128]{2,1,0:T(8,128)(2,1)S(1)} %all-to-all-done.got, bf16[32,128,128]{2,1,0:T(8,128)(2,1)S(1)} %all-to-all-done.1.got_rest), custom_call_target="tpu_custom_call" | custom-call | flops 1000 | bytes 1000 | tf_op jit(solution)/shard_map/place_values/pallas_call | solution.py:413
  (4 shorter events, 0.0 us)
Async XLA Ops:
  4.1 7.6 %copy-start.2 = (bf16[4,6,64,128]{3,2,1,0:T(8,128)(2,1)S(1)}, bf16[4,6,64,128]{3,2,1,0:T(8,128)(2,1)}, u32[]{:S(2)}) copy-start(bf16[4,6,64,128]{3,2,1,0:T(8,128)(2,1)} %q_ref.1) | copy-start | bytes 1179652
  4.1 7.6 %copy-start.3 = (s32[4,6,16]{2,0,1:T(4,128)S(1)}, s32[4,6,16]{2,0,1:T(4,128)}, u32[]{:S(2)}) copy-start(s32[4,6,16]{2,0,1:T(4,128)} %param.10) | copy-start | bytes 4612
  4.1 7.6 %copy-start.4 = (s32[48]{0:T(128)S(1)}, s32[48]{0:T(128)}, u32[]{:S(2)}) copy-start(s32[48]{0:T(128)} %get-tuple-element.21.table) | copy-start | bytes 580
  4.2 7.6 %copy-start.5 = (s32[6]{0:T(128)S(1)}, s32[6]{0:T(128)}, u32[]{:S(2)}) copy-start(s32[6]{0:T(128)} %len_hbm.1) | copy-start | bytes 76
  4.2 59.2 %all-to-all-start = ((bf16[64,128,128]{2,1,0:T(8,128)(2,1)}), bf16[64,128,128]{2,1,0:T(8,128)(2,1)S(1)}, u32[]{:S(2)}, u32[]{:S(2)}) async-start(bf16[64,128,128]{2,1,0:T(8,128)(2,1)} %get-tuple-element.36), calls=%async_computation | async-start | bytes 4194304 | tf_op jit(solution)/shard_map/all_to_all | solution.py:329
  11.7 1.4 %copy-start = (bf16[6,8,128,128]{3,2,1,0:T(8,128)(2,1)S(1)}, bf16[6,8,128,128]{3,2,1,0:T(8,128)(2,1)}, u32[]{:S(2)}) copy-start(bf16[6,8,128,128]{3,2,1,0:T(8,128)(2,1)} %k_ref.3) | copy-start | bytes 4718596
  13.2 1.4 %copy-start.1 = (bf16[6,8,128,128]{3,2,1,0:T(8,128)(2,1)S(1)}, bf16[6,8,128,128]{3,2,1,0:T(8,128)(2,1)}, u32[]{:S(2)}) copy-start(bf16[6,8,128,128]{3,2,1,0:T(8,128)(2,1)} %v_ref.3) | copy-start | bytes 4718596
  18.0 1.8 %collective-permute-start = (f32[2,400,128]{2,1,0:T(8,128)S(1)}, f32[2,400,128]{2,1,0:T(8,128)S(1)}, u32[]{:S(2)}, u32[]{:S(2)}) collective-permute-start(f32[2,400,128]{2,1,0:T(8,128)S(1)} %get-tuple-element.24), channel_id=1, source_target_pairs={{0,1},{1,0},{2,3},{3,2},{4,5},{5,4},{6,7},{7,6},{8,9},{9,8},{10,11... | collective-permute-start | bytes 1228808 | tf_op jit(solution)/shard_map/ppermute | solution.py:372
  20.3 15.0 %collective-permute-start.1 = (f32[400,128]{1,0:T(8,128)S(1)}, f32[400,128]{1,0:T(8,128)S(1)}, u32[]{:S(2)}, u32[]{:S(2)}) collective-permute-start(f32[400,128]{1,0:T(8,128)S(1)} %get-tuple-element.26), channel_id=1, source_target_pairs={{0,2},{1,3},{2,0},{3,1},{4,6},{5,7},{6,4},{7,5},{8,10},{9,11},{10,... | collective-permute-start | bytes 614408 | tf_op jit(solution)/shard_map/ppermute | solution.py:372
  35.5 13.4 %collective-permute-start.2 = (f32[208,128]{1,0:T(8,128)S(1)}, f32[208,128]{1,0:T(8,128)S(1)}, u32[]{:S(2)}, u32[]{:S(2)}) collective-permute-start(f32[208,128]{1,0:T(8,128)S(1)} %get-tuple-element.28), channel_id=1, source_target_pairs={{0,4},{1,5},{2,6},{3,7},{4,0},{5,1},{6,2},{7,3},{8,12},{9,13},{10,... | collective-permute-start | bytes 319496 | tf_op jit(solution)/shard_map/ppermute | solution.py:372
  49.2 14.1 %collective-permute-start.3 = (f16[192,128]{1,0:T(8,128)(2,1)S(1)}, f16[192,128]{1,0:T(8,128)(2,1)S(1)}, u32[]{:S(2)}, u32[]{:S(2)}) collective-permute-start(f16[192,128]{1,0:T(8,128)(2,1)S(1)} %get-tuple-element.38), channel_id=1, source_target_pairs={{0,8},{1,9},{2,10},{3,11},{4,12},{5,13},{6,14},{7,15},{8,0},{9,1},... | collective-permute-start | bytes 147464 | tf_op jit(solution)/shard_map/ppermute | solution.py:372
  53.8 9.6 %collective-permute-start.4 = (f32[24,128]{1,0:T(8,128)S(1)}, f32[24,128]{1,0:T(8,128)S(1)}, u32[]{:S(2)}, u32[]{:S(2)}) collective-permute-start(f32[24,128]{1,0:T(8,128)S(1)} %get-tuple-element.30.own_stats), channel_id=1, source_target_pairs={{0,8},{1,9},{2,10},{3,11},{4,12},{5,13},{6,14},{7,15},{8,0},{9,1},... | collective-permute-start | bytes 36872 | tf_op jit(solution)/shard_map/ppermute | solution.py:372
  63.4 28.0 %all-to-all-start.1 = ((bf16[32,128,128]{2,1,0:T(8,128)(2,1)}), bf16[32,128,128]{2,1,0:T(8,128)(2,1)S(1)}, u32[]{:S(2)}, u32[]{:S(2)}) async-start(bf16[32,128,128]{2,1,0:T(8,128)(2,1)} %get-tuple-element.37), calls=%async_computation.1 | async-start | bytes 2097152 | tf_op jit(solution)/shard_map/all_to_all | solution.py:329
  67.3 19.3 %collective-permute-start.7 = (bf16[224,128]{1,0:T(8,128)(2,1)S(1)}, bf16[224,128]{1,0:T(8,128)(2,1)S(1)}, u32[]{:S(2)}, u32[]{:S(2)}) collective-permute-start(bf16[224,128]{1,0:T(8,128)(2,1)S(1)} %last.1.refs_0_), channel_id=1, source_target_pairs={{0,6},{1,7},{2,4},{3,5},{4,2},{5,3},{6,0},{7,1},{8,14},{9,15},{10,... | collective-permute-start | bytes 172040 | tf_op jit(solution)/shard_map/ppermute | solution.py:372
  70.2 16.4 %collective-permute-start.6 = (bf16[224,128]{1,0:T(8,128)(2,1)S(1)}, bf16[224,128]{1,0:T(8,128)(2,1)S(1)}, u32[]{:S(2)}, u32[]{:S(2)}) collective-permute-start(bf16[224,128]{1,0:T(8,128)(2,1)S(1)} %last.1.refs_0_), channel_id=1, source_target_pairs={{0,2},{1,3},{2,0},{3,1},{4,6},{5,7},{6,4},{7,5},{8,10},{9,11},{10,... | collective-permute-start | bytes 172040 | tf_op jit(solution)/shard_map/ppermute | solution.py:372
  70.8 16.9 %collective-permute-start.5 = (bf16[224,128]{1,0:T(8,128)(2,1)S(1)}, bf16[224,128]{1,0:T(8,128)(2,1)S(1)}, u32[]{:S(2)}, u32[]{:S(2)}) collective-permute-start(bf16[224,128]{1,0:T(8,128)(2,1)S(1)} %last.1.refs_0_), channel_id=1, source_target_pairs={{0,4},{1,5},{2,6},{3,7},{4,0},{5,1},{6,2},{7,3},{8,12},{9,13},{10,... | collective-permute-start | bytes 172040 | tf_op jit(solution)/shard_map/ppermute | solution.py:372
  70.9 16.8 %collective-permute-start.8 = (bf16[224,128]{1,0:T(8,128)(2,1)S(1)}, bf16[224,128]{1,0:T(8,128)(2,1)S(1)}, u32[]{:S(2)}, u32[]{:S(2)}) collective-permute-start(bf16[224,128]{1,0:T(8,128)(2,1)S(1)} %last.1.refs_0_), channel_id=1, source_target_pairs={{0,1},{1,0},{2,3},{3,2},{4,5},{5,4},{6,7},{7,6},{8,9},{9,8},{10,11... | collective-permute-start | bytes 172040 | tf_op jit(solution)/shard_map/ppermute | solution.py:372
  86.6 1.2 %collective-permute-start.11 = (bf16[224,128]{1,0:T(8,128)(2,1)S(1)}, bf16[224,128]{1,0:T(8,128)(2,1)S(1)}, u32[]{:S(2)}, u32[]{:S(2)}) collective-permute-start(bf16[224,128]{1,0:T(8,128)(2,1)S(1)} %collective-permute-done.7.refs_3_), channel_id=1, source_target_pairs={{0,1},{1,0},{2,3},{3,2},{4,5},{5,4},{6,7},{7,6},{8,9},{9,8},{10,11... | collective-permute-start | bytes 172040 | tf_op jit(solution)/shard_map/ppermute | solution.py:372
  86.6 1.4 %collective-permute-start.10 = (bf16[224,128]{1,0:T(8,128)(2,1)S(1)}, bf16[224,128]{1,0:T(8,128)(2,1)S(1)}, u32[]{:S(2)}, u32[]{:S(2)}) collective-permute-start(bf16[224,128]{1,0:T(8,128)(2,1)S(1)} %collective-permute-done.6.refs_2_), channel_id=1, source_target_pairs={{0,1},{1,0},{2,3},{3,2},{4,5},{5,4},{6,7},{7,6},{8,9},{9,8},{10,11... | collective-permute-start | bytes 172040 | tf_op jit(solution)/shard_map/ppermute | solution.py:372
  87.7 1.2 %collective-permute-start.9 = (bf16[224,128]{1,0:T(8,128)(2,1)S(1)}, bf16[224,128]{1,0:T(8,128)(2,1)S(1)}, u32[]{:S(2)}, u32[]{:S(2)}) collective-permute-start(bf16[224,128]{1,0:T(8,128)(2,1)S(1)} %collective-permute-done.5.refs_1_), channel_id=1, source_target_pairs={{0,1},{1,0},{2,3},{3,2},{4,5},{5,4},{6,7},{7,6},{8,9},{9,8},{10,11... | collective-permute-start | bytes 172040 | tf_op jit(solution)/shard_map/ppermute | solution.py:372

commit v10 on v9

--- a/solution.py
+++ b/solution.py
@@ -423,6 +423,8 @@
 
     moved_keys = place(place_keys_kernel, "place_keys", tiles_in)
     moved_values = place(place_values_kernel, "place_values", tiles_in, rest_in)
+    *forward, moved_keys = lax.optimization_barrier((*near[1:], moved_keys))
+    near = [message, *forward]
     arrived = near + [flip(x, 1) for x in near]
 
     attn_out, mass = pl.pallas_call(

time: 94.8 us -> 95 us (level)
    ppermute x12, waiting for transfers between devices: 54.7 us -> 52.3 us  [flip(): return lax.ppermute(x, 'ctx', [(i, i ^ bit) for i in range(devices)])]
    all_to_all x2, waiting for transfers between devices: 0.01 us -> 2.26 us  [exchange(): return lax.all_to_all(x, 'ctx', split_axis=0, concat_axis=0, tiled=True)]
  transfers between devices with their start and end apart: 14 -> 14, of which waited for: 10 -> 8; matrix products, arithmetic and copies ran while one was open for 0% -> 0% of each run, Pallas kernels for 8% -> 8%
where the time goes in v10:
time: 95 us; the launch traced here: 93.8 us
  waiting for transfers between devices  54.6 us (57%)
  starting transfers between devices  22.4 us (24%)
  Pallas kernels  13.1 us (14%)
  local copies, waits for them, and re-layouts  2.84 us (3%)
    ppermute x12, waiting for transfers between devices, flip(): return lax.ppermute(x, 'ctx', [(i, i ^ bit) for i in range(devices)])  52.3 us
    all_to_all x2, starting transfers between devices, exchange(): return lax.all_to_all(x, 'ctx', split_axis=0, concat_axis=0, tiled=True)  11.2 us
    ppermute x12, starting transfers between devices, flip(): return lax.ppermute(x, 'ctx', [(i, i ^ bit) for i in range(devices)])  11.2 us
    pallas_call x1, Pallas kernels, local(): pl.pallas_call(functools.partial(stage_kernel, devices, group, first), ou...  3.48 us
    pallas_call x1, Pallas kernels, local(): pl.pallas_call(functools.partial(attend_kernel, levels), out_shape=[jax.S...  3.46 us
    pallas_call x2, Pallas kernels, place(): pl.pallas_call(functools.partial(kernel, devices, group, first), out_shap...  3.34 us
    unnamed x12, local copies, waits for them, and re-layouts  2.84 us
    all_to_all x2, waiting for transfers between devices, exchange(): return lax.all_to_all(x, 'ctx', split_axis=0, concat_axis=0, tiled=True)  2.26 us
  transfers between devices with their start and end apart: 14, of which 8 were waited for; matrix products, arithmetic and copies ran while one was open for 0% of the time, Pallas kernels for 8%

profile of v10, /device:TPU:0, one launch (start us, length us, event | category | flops | bytes accessed | tf_op | source)
XLA Modules:
  0.0 93.8 jit_solution(5648274534076077204)
XLA Ops:
  0.6 3.5 %stage.1 = (bf16[64,128,128]{2,1,0:T(8,128)(2,1)}, bf16[32,128,128]{2,1,0:T(8,128)(2,1)}, s32[48]{0:T(128)}) custom-call(s32[6,8,16]{2,1,0:T(8,128)} %dest_hbm.1, bf16[6,8,128,128]{3,2,1,0:T(8,128)(2,1)} %k_ref.3, bf16[6,8,128,128]{3,2,1,0:T(8,128)(2,1)} %v_ref.3), custom_call_target="tpu_custom_call" | custom-call | flops 1000 | bytes 1000 | tf_op jit(solution)/shard_map/stage/pallas_call | solution.py:332
  4.1 0.0 copy-start.2
  4.1 0.0 copy-start.3
  4.1 0.0 copy-start.4
  4.2 0.0 copy-start.5
  4.2 7.5 %all-to-all-start = ((bf16[64,128,128]{2,1,0:T(8,128)(2,1)}), bf16[64,128,128]{2,1,0:T(8,128)(2,1)S(1)}, u32[]{:S(2)}, u32[]{:S(2)}) async-start(bf16[64,128,128]{2,1,0:T(8,128)(2,1)} %get-tuple-element.38), calls=%async_computation | async-start | bytes 4194304 | tf_op jit(solution)/shard_map/all_to_all | solution.py:329
  11.7 0.0 copy-done.2
  11.7 0.0 copy-done.3
  11.7 0.0 copy-start
  11.8 1.4 %copy-done = bf16[6,8,128,128]{3,2,1,0:T(8,128)(2,1)S(1)} copy-done((bf16[6,8,128,128]{3,2,1,0:T(8,128)(2,1)S(1)}, bf16[6,8,128,128]{3,2,1,0:T(8,128)(2,1)}, u32[]{:S(2)}) %copy-start) | copy-done | bytes 1572888
  13.2 1.4 %copy-done.1 = bf16[6,8,128,128]{3,2,1,0:T(8,128)(2,1)S(1)} copy-done((bf16[6,8,128,128]{3,2,1,0:T(8,128)(2,1)S(1)}, bf16[6,8,128,128]{3,2,1,0:T(8,128)(2,1)}, u32[]{:S(2)}) %copy-start.1) | copy-done | bytes 1572888
  14.6 3.5 %attend.1 = (f32[2,32,128]{2,1,0:T(8,128)S(1)}, f32[2,400,128]{2,1,0:T(8,128)S(1)}, f32[2,400,128]{2,1,0:T(8,128)S(1)}) custom-call(s32[48]{0:T(128)S(1)} %copy-done.4, s32[6]{0:T(128)S(1)} %copy-done.5, s32[6,4,16]{2,1,0:T(4,128)S(1)} %bitcast.3, bf16[4,6,64,128]{3,2,1,0:T(8,128)(2,1)S(1)} %copy-done.2, bf16[6,8,128,128]{3,2,1,0:T(8,128)(2,1)S(1)} %copy-done, ...), custom_call_target="tpu_custom_call" | custom-call | flops 1000 | bytes 1000 | tf_op jit(solution)/shard_map/attend/pallas_call | solution.py:354
  18.0 0.5 collective-permute-start
  18.5 1.4 %collective-permute-done.got = f32[2,400,128]{2,1,0:T(8,128)S(1)} collective-permute-done((f32[2,400,128]{2,1,0:T(8,128)S(1)}, f32[2,400,128]{2,1,0:T(8,128)S(1)}, u32[]{:S(2)}, u32[]{:S(2)}) %collective-permute-start) | collective-permute-done | bytes 409632 | tf_op jit(solution)/shard_map/ppermute | solution.py:372
  19.9 0.4 core.1
  20.3 2.0 %collective-permute-start.1 = (f32[400,128]{1,0:T(8,128)S(1)}, f32[400,128]{1,0:T(8,128)S(1)}, u32[]{:S(2)}, u32[]{:S(2)}) collective-permute-start(f32[400,128]{1,0:T(8,128)S(1)} %get-tuple-element.30), channel_id=1, source_target_pairs={{0,2},{1,3},{2,0},{3,1},{4,6},{5,7},{6,4},{7,5},{8,10},{9,11},{10,... | collective-permute-start | bytes 614408 | tf_op jit(solution)/shard_map/ppermute | solution.py:372
  22.2 13.0 %collective-permute-done.1.got = f32[400,128]{1,0:T(8,128)S(1)} collective-permute-done((f32[400,128]{1,0:T(8,128)S(1)}, f32[400,128]{1,0:T(8,128)S(1)}, u32[]{:S(2)}, u32[]{:S(2)}) %collective-permute-start.1) | collective-permute-done | bytes 204832 | tf_op jit(solution)/shard_map/ppermute | solution.py:372
  35.3 0.3 near.1
  35.5 0.1 collective-permute-start.2
  35.6 13.3 %collective-permute-done.2.got = f32[208,128]{1,0:T(8,128)S(1)} collective-permute-done((f32[208,128]{1,0:T(8,128)S(1)}, f32[208,128]{1,0:T(8,128)S(1)}, u32[]{:S(2)}, u32[]{:S(2)}) %collective-permute-start.2) | collective-permute-done | bytes 106528 | tf_op jit(solution)/shard_map/ppermute | solution.py:372
  48.9 0.2 far.1.block
  49.0 0.1 scale.1
  49.1 0.1 reduce-precision_convert_fusion
  49.2 4.6 %collective-permute-start.3 = (f16[192,128]{1,0:T(8,128)(2,1)S(1)}, f16[192,128]{1,0:T(8,128)(2,1)S(1)}, u32[]{:S(2)}, u32[]{:S(2)}) collective-permute-start(f16[192,128]{1,0:T(8,128)(2,1)S(1)} %get-tuple-element.46), channel_id=1, source_target_pairs={{0,8},{1,9},{2,10},{3,11},{4,12},{5,13},{6,14},{7,15},{8,0},{9,1},... | collective-permute-start | bytes 147464 | tf_op jit(solution)/shard_map/ppermute | solution.py:372
  53.8 0.1 collective-permute-start.4
  53.9 9.4 %collective-permute-done.3 = f16[192,128]{1,0:T(8,128)(2,1)S(1)} collective-permute-done((f16[192,128]{1,0:T(8,128)(2,1)S(1)}, f16[192,128]{1,0:T(8,128)(2,1)S(1)}, u32[]{:S(2)}, u32[]{:S(2)}) %collective-permute-start.3) | collective-permute-done | bytes 49184 | tf_op jit(solution)/shard_map/ppermute | solution.py:372
  63.3 0.1 collective-permute-done.4.got_stats
  63.4 0.0 all-to-all-done.got
  63.4 3.7 %all-to-all-start.1 = ((bf16[32,128,128]{2,1,0:T(8,128)(2,1)}), bf16[32,128,128]{2,1,0:T(8,128)(2,1)S(1)}, u32[]{:S(2)}, u32[]{:S(2)}) async-start(bf16[32,128,128]{2,1,0:T(8,128)(2,1)} %get-tuple-element.45), calls=%async_computation.1 | async-start | bytes 2097152 | tf_op jit(solution)/shard_map/all_to_all | solution.py:329
  67.1 0.2 last.1.refs_0_
  67.3 2.0 %collective-permute-start.5 = (bf16[224,128]{1,0:T(8,128)(2,1)S(1)}, bf16[224,128]{1,0:T(8,128)(2,1)S(1)}, u32[]{:S(2)}, u32[]{:S(2)}) collective-permute-start(bf16[224,128]{1,0:T(8,128)(2,1)S(1)} %last.1.refs_0_), channel_id=1, source_target_pairs={{0,4},{1,5},{2,6},{3,7},{4,0},{5,1},{6,2},{7,3},{8,12},{9,13},{10,... | collective-permute-start | bytes 172040 | tf_op jit(solution)/shard_map/ppermute | solution.py:372
  69.3 1.5 %collective-permute-start.6 = (bf16[224,128]{1,0:T(8,128)(2,1)S(1)}, bf16[224,128]{1,0:T(8,128)(2,1)S(1)}, u32[]{:S(2)}, u32[]{:S(2)}) collective-permute-start(bf16[224,128]{1,0:T(8,128)(2,1)S(1)} %last.1.refs_0_), channel_id=1, source_target_pairs={{0,2},{1,3},{2,0},{3,1},{4,6},{5,7},{6,4},{7,5},{8,10},{9,11},{10,... | collective-permute-start | bytes 172040 | tf_op jit(solution)/shard_map/ppermute | solution.py:372
  70.8 0.1 collective-permute-start.7
  70.9 0.0 collective-permute-start.8
  70.9 1.7 %place_keys.1 = bf16[6,8,128,128]{3,2,1,0:T(8,128)(2,1)} custom-call(s32[48]{0:T(128)S(1)} %copy-done.4, bf16[64,128,128]{2,1,0:T(8,128)(2,1)S(1)} %all-to-all-done.got), custom_call_target="tpu_custom_call" | custom-call | flops 1000 | bytes 1000 | tf_op jit(solution)/shard_map/place_keys/pallas_call | solution.py:413
  72.6 14.0 %collective-permute-done.5.refs_1_ = bf16[224,128]{1,0:T(8,128)(2,1)S(1)} collective-permute-done((bf16[224,128]{1,0:T(8,128)(2,1)S(1)}, bf16[224,128]{1,0:T(8,128)(2,1)S(1)}, u32[]{:S(2)}, u32[]{:S(2)}) %collective-permute-start.5) | collective-permute-done | bytes 57376 | tf_op jit(solution)/shard_map/ppermute | solution.py:372
  86.6 0.0 collective-permute-done.6.refs_2_
  86.6 1.0 %collective-permute-done.7.refs_3_ = bf16[224,128]{1,0:T(8,128)(2,1)S(1)} collective-permute-done((bf16[224,128]{1,0:T(8,128)(2,1)S(1)}, bf16[224,128]{1,0:T(8,128)(2,1)S(1)}, u32[]{:S(2)}, u32[]{:S(2)}) %collective-permute-start.7) | collective-permute-done | bytes 57376 | tf_op jit(solution)/shard_map/ppermute | solution.py:372
  87.7 0.0 collective-permute-start.10
  87.7 0.5 collective-permute-start.11
  88.2 0.0 collective-permute-start.9
  88.2 2.3 %all-to-all-done.1.got_rest = bf16[32,128,128]{2,1,0:T(8,128)(2,1)S(1)} async-done(((bf16[32,128,128]{2,1,0:T(8,128)(2,1)}), bf16[32,128,128]{2,1,0:T(8,128)(2,1)S(1)}, u32[]{:S(2)}, u32[]{:S(2)}) %all-to-all-start.1) | async-done | bytes 1048608 | tf_op jit(solution)/shard_map/all_to_all | solution.py:329
  90.4 1.7 %place_values.1 = bf16[6,8,128,128]{3,2,1,0:T(8,128)(2,1)} custom-call(s32[48]{0:T(128)S(1)} %copy-done.4, bf16[64,128,128]{2,1,0:T(8,128)(2,1)S(1)} %all-to-all-done.got, bf16[32,128,128]{2,1,0:T(8,128)(2,1)S(1)} %all-to-all-done.1.got_rest), custom_call_target="tpu_custom_call" | custom-call | flops 1000 | bytes 1000 | tf_op jit(solution)/shard_map/place_values/pallas_call | solution.py:413
  92.1 0.0 collective-permute-done.8.refs_4_
  92.1 0.0 collective-permute-done.10.refs_6_
  92.1 0.0 collective-permute-done.11.refs_7_
  92.1 0.0 collective-permute-done.9.refs_5_
  92.1 1.7 %finish.1 = (bf16[4,2,192,128]{3,2,1,0:T(8,128)(2,1)}, f32[6,1,8]{2,1,0:T(1,128)}) custom-call(f32[2,32,128]{2,1,0:T(8,128)S(1)} %get-tuple-element.26.stats_ref, bf16[224,128]{1,0:T(8,128)(2,1)S(1)} %last.1.refs_0_, bf16[224,128]{1,0:T(8,128)(2,1)S(1)} %collective-permute-done.5.refs_1_, bf16[224,128]{1,0:T(8,128)(2,1)S(1)} %collective-permute-done.6.refs_2_, ...), custom_call_target="tpu_custom_call" | custom-call | flops 1000 | bytes 1000 | tf_op jit(solution)/shard_map/finish/pallas_call | solution.py:430
  (4 shorter events, 0.0 us)
Async XLA Ops:
  4.1 7.6 %copy-start.2 = (bf16[4,6,64,128]{3,2,1,0:T(8,128)(2,1)S(1)}, bf16[4,6,64,128]{3,2,1,0:T(8,128)(2,1)}, u32[]{:S(2)}) copy-start(bf16[4,6,64,128]{3,2,1,0:T(8,128)(2,1)} %q_ref.1) | copy-start | bytes 1179652
  4.1 7.6 %copy-start.3 = (s32[4,6,16]{2,0,1:T(4,128)S(1)}, s32[4,6,16]{2,0,1:T(4,128)}, u32[]{:S(2)}) copy-start(s32[4,6,16]{2,0,1:T(4,128)} %param.10) | copy-start | bytes 4612
  4.1 7.6 %copy-start.4 = (s32[48]{0:T(128)S(1)}, s32[48]{0:T(128)}, u32[]{:S(2)}) copy-start(s32[48]{0:T(128)} %get-tuple-element.25.table) | copy-start | bytes 580
  4.2 7.6 %copy-start.5 = (s32[6]{0:T(128)S(1)}, s32[6]{0:T(128)}, u32[]{:S(2)}) copy-start(s32[6]{0:T(128)} %len_hbm.1) | copy-start | bytes 76
  4.2 59.2 %all-to-all-start = ((bf16[64,128,128]{2,1,0:T(8,128)(2,1)}), bf16[64,128,128]{2,1,0:T(8,128)(2,1)S(1)}, u32[]{:S(2)}, u32[]{:S(2)}) async-start(bf16[64,128,128]{2,1,0:T(8,128)(2,1)} %get-tuple-element.38), calls=%async_computation | async-start | bytes 4194304 | tf_op jit(solution)/shard_map/all_to_all | solution.py:329
  11.7 1.4 %copy-start = (bf16[6,8,128,128]{3,2,1,0:T(8,128)(2,1)S(1)}, bf16[6,8,128,128]{3,2,1,0:T(8,128)(2,1)}, u32[]{:S(2)}) copy-start(bf16[6,8,128,128]{3,2,1,0:T(8,128)(2,1)} %k_ref.3) | copy-start | bytes 4718596
  13.2 1.4 %copy-start.1 = (bf16[6,8,128,128]{3,2,1,0:T(8,128)(2,1)S(1)}, bf16[6,8,128,128]{3,2,1,0:T(8,128)(2,1)}, u32[]{:S(2)}) copy-start(bf16[6,8,128,128]{3,2,1,0:T(8,128)(2,1)} %v_ref.3) | copy-start | bytes 4718596
  18.0 1.8 %collective-permute-start = (f32[2,400,128]{2,1,0:T(8,128)S(1)}, f32[2,400,128]{2,1,0:T(8,128)S(1)}, u32[]{:S(2)}, u32[]{:S(2)}) collective-permute-start(f32[2,400,128]{2,1,0:T(8,128)S(1)} %get-tuple-element.28), channel_id=1, source_target_pairs={{0,1},{1,0},{2,3},{3,2},{4,5},{5,4},{6,7},{7,6},{8,9},{9,8},{10,11... | collective-permute-start | bytes 1228808 | tf_op jit(solution)/shard_map/ppermute | solution.py:372
  20.3 15.0 %collective-permute-start.1 = (f32[400,128]{1,0:T(8,128)S(1)}, f32[400,128]{1,0:T(8,128)S(1)}, u32[]{:S(2)}, u32[]{:S(2)}) collective-permute-start(f32[400,128]{1,0:T(8,128)S(1)} %get-tuple-element.30), channel_id=1, source_target_pairs={{0,2},{1,3},{2,0},{3,1},{4,6},{5,7},{6,4},{7,5},{8,10},{9,11},{10,... | collective-permute-start | bytes 614408 | tf_op jit(solution)/shard_map/ppermute | solution.py:372
  35.5 13.4 %collective-permute-start.2 = (f32[208,128]{1,0:T(8,128)S(1)}, f32[208,128]{1,0:T(8,128)S(1)}, u32[]{:S(2)}, u32[]{:S(2)}) collective-permute-start(f32[208,128]{1,0:T(8,128)S(1)} %get-tuple-element.32), channel_id=1, source_target_pairs={{0,4},{1,5},{2,6},{3,7},{4,0},{5,1},{6,2},{7,3},{8,12},{9,13},{10,... | collective-permute-start | bytes 319496 | tf_op jit(solution)/shard_map/ppermute | solution.py:372
  49.2 14.1 %collective-permute-start.3 = (f16[192,128]{1,0:T(8,128)(2,1)S(1)}, f16[192,128]{1,0:T(8,128)(2,1)S(1)}, u32[]{:S(2)}, u32[]{:S(2)}) collective-permute-start(f16[192,128]{1,0:T(8,128)(2,1)S(1)} %get-tuple-element.46), channel_id=1, source_target_pairs={{0,8},{1,9},{2,10},{3,11},{4,12},{5,13},{6,14},{7,15},{8,0},{9,1},... | collective-permute-start | bytes 147464 | tf_op jit(solution)/shard_map/ppermute | solution.py:372
  53.8 9.6 %collective-permute-start.4 = (f32[24,128]{1,0:T(8,128)S(1)}, f32[24,128]{1,0:T(8,128)S(1)}, u32[]{:S(2)}, u32[]{:S(2)}) collective-permute-start(f32[24,128]{1,0:T(8,128)S(1)} %get-tuple-element.34.own_stats), channel_id=1, source_target_pairs={{0,8},{1,9},{2,10},{3,11},{4,12},{5,13},{6,14},{7,15},{8,0},{9,1},... | collective-permute-start | bytes 36872 | tf_op jit(solution)/shard_map/ppermute | solution.py:372
  63.4 27.0 %all-to-all-start.1 = ((bf16[32,128,128]{2,1,0:T(8,128)(2,1)}), bf16[32,128,128]{2,1,0:T(8,128)(2,1)S(1)}, u32[]{:S(2)}, u32[]{:S(2)}) async-start(bf16[32,128,128]{2,1,0:T(8,128)(2,1)} %get-tuple-element.45), calls=%async_computation.1 | async-start | bytes 2097152 | tf_op jit(solution)/shard_map/all_to_all | solution.py:329
  67.3 19.3 %collective-permute-start.5 = (bf16[224,128]{1,0:T(8,128)(2,1)S(1)}, bf16[224,128]{1,0:T(8,128)(2,1)S(1)}, u32[]{:S(2)}, u32[]{:S(2)}) collective-permute-start(bf16[224,128]{1,0:T(8,128)(2,1)S(1)} %last.1.refs_0_), channel_id=1, source_target_pairs={{0,4},{1,5},{2,6},{3,7},{4,0},{5,1},{6,2},{7,3},{8,12},{9,13},{10,... | collective-permute-start | bytes 172040 | tf_op jit(solution)/shard_map/ppermute | solution.py:372
  69.3 17.3 %collective-permute-start.6 = (bf16[224,128]{1,0:T(8,128)(2,1)S(1)}, bf16[224,128]{1,0:T(8,128)(2,1)S(1)}, u32[]{:S(2)}, u32[]{:S(2)}) collective-permute-start(bf16[224,128]{1,0:T(8,128)(2,1)S(1)} %last.1.refs_0_), channel_id=1, source_target_pairs={{0,2},{1,3},{2,0},{3,1},{4,6},{5,7},{6,4},{7,5},{8,10},{9,11},{10,... | collective-permute-start | bytes 172040 | tf_op jit(solution)/shard_map/ppermute | solution.py:372
  70.8 16.9 %collective-permute-start.7 = (bf16[224,128]{1,0:T(8,128)(2,1)S(1)}, bf16[224,128]{1,0:T(8,128)(2,1)S(1)}, u32[]{:S(2)}, u32[]{:S(2)}) collective-permute-start(bf16[224,128]{1,0:T(8,128)(2,1)S(1)} %last.1.refs_0_), channel_id=1, source_target_pairs={{0,6},{1,7},{2,4},{3,5},{4,2},{5,3},{6,0},{7,1},{8,14},{9,15},{10,... | collective-permute-start | bytes 172040 | tf_op jit(solution)/shard_map/ppermute | solution.py:372
  70.9 21.2 %collective-permute-start.8 = (bf16[224,128]{1,0:T(8,128)(2,1)S(1)}, bf16[224,128]{1,0:T(8,128)(2,1)S(1)}, u32[]{:S(2)}, u32[]{:S(2)}) collective-permute-start(bf16[224,128]{1,0:T(8,128)(2,1)S(1)} %last.1.refs_0_), channel_id=1, source_target_pairs={{0,1},{1,0},{2,3},{3,2},{4,5},{5,4},{6,7},{7,6},{8,9},{9,8},{10,11... | collective-permute-start | bytes 172040 | tf_op jit(solution)/shard_map/ppermute | solution.py:372
  87.7 4.5 %collective-permute-start.10 = (bf16[224,128]{1,0:T(8,128)(2,1)S(1)}, bf16[224,128]{1,0:T(8,128)(2,1)S(1)}, u32[]{:S(2)}, u32[]{:S(2)}) collective-permute-start(bf16[224,128]{1,0:T(8,128)(2,1)S(1)} %collective-permute-done.6.refs_2_), channel_id=1, source_target_pairs={{0,1},{1,0},{2,3},{3,2},{4,5},{5,4},{6,7},{7,6},{8,9},{9,8},{10,11... | collective-permute-start | bytes 172040 | tf_op jit(solution)/shard_map/ppermute | solution.py:372
  87.7 4.5 %collective-permute-start.11 = (bf16[224,128]{1,0:T(8,128)(2,1)S(1)}, bf16[224,128]{1,0:T(8,128)(2,1)}, u32[]{:S(2)}, u32[]{:S(2)}) collective-permute-start(bf16[224,128]{1,0:T(8,128)(2,1)S(1)} %collective-permute-done.7.refs_3_), channel_id=1, source_target_pairs={{0,1},{1,0},{2,3},{3,2},{4,5},{5,4},{6,7},{7,6},{8,9},{9,8},{10,11... | collective-permute-start | bytes 172040 | tf_op jit(solution)/shard_map/ppermute | solution.py:372
  88.2 4.0 %collective-permute-start.9 = (bf16[224,128]{1,0:T(8,128)(2,1)S(1)}, bf16[224,128]{1,0:T(8,128)(2,1)}, u32[]{:S(2)}, u32[]{:S(2)}) collective-permute-start(bf16[224,128]{1,0:T(8,128)(2,1)S(1)} %collective-permute-done.5.refs_1_), channel_id=1, source_target_pairs={{0,1},{1,0},{2,3},{3,2},{4,5},{5,4},{6,7},{7,6},{8,9},{9,8},{10,11... | collective-permute-start | bytes 172040 | tf_op jit(solution)/shard_map/ppermute | solution.py:372

commit v11 on v10

--- a/solution.py
+++ b/solution.py
@@ -422,7 +422,6 @@
         )(table, *got)
 
     moved_keys = place(place_keys_kernel, "place_keys", tiles_in)
-    moved_values = place(place_values_kernel, "place_values", tiles_in, rest_in)
     *forward, moved_keys = lax.optimization_barrier((*near[1:], moved_keys))
     near = [message, *forward]
     arrived = near + [flip(x, 1) for x in near]
@@ -440,6 +439,8 @@
         cost_estimate=COST,
         name="finish",
     )(stats, *arrived)
+    rest_in, mass = lax.optimization_barrier((rest_in, mass))
+    moved_values = place(place_values_kernel, "place_values", tiles_in, rest_in)
     return attn_out.reshape(queries.shape), jnp.transpose(mass, (0, 2, 1)), moved_keys, moved_values
 
 

time: 95 us -> 93.9 us (0.988)
    all_to_all x2, waiting for transfers between devices: 2.26 us -> 0.17 us  [exchange(): return lax.all_to_all(x, 'ctx', split_axis=0, concat_axis=0, tiled=True)]
    ppermute x12, waiting for transfers between devices: 52.3 us -> 53.5 us  [flip(): return lax.ppermute(x, 'ctx', [(i, i ^ bit) for i in range(devices)])]
  transfers between devices with their start and end apart: 14 -> 14, of which waited for: 8 -> 11; matrix products, arithmetic and copies ran while one was open for 0% -> 0% of each run, Pallas kernels for 8% -> 8%
where the time goes in v11:
time: 93.9 us; the launch traced here: 92.1 us
  waiting for transfers between devices  53.7 us (57%)
  starting transfers between devices  22.4 us (24%)
  Pallas kernels  12.2 us (13%)
  local copies, waits for them, and re-layouts  2.84 us (3%)
    ppermute x12, waiting for transfers between devices, flip(): return lax.ppermute(x, 'ctx', [(i, i ^ bit) for i in range(devices)])  53.5 us
    all_to_all x2, starting transfers between devices, exchange(): return lax.all_to_all(x, 'ctx', split_axis=0, concat_axis=0, tiled=True)  11.2 us
    ppermute x12, starting transfers between devices, flip(): return lax.ppermute(x, 'ctx', [(i, i ^ bit) for i in range(devices)])  11.2 us
    pallas_call x1, Pallas kernels, local(): pl.pallas_call(functools.partial(stage_kernel, devices, group, first), ou...  3.48 us
    pallas_call x1, Pallas kernels, local(): pl.pallas_call(functools.partial(attend_kernel, levels), out_shape=[jax.S...  3.46 us
    pallas_call x2, Pallas kernels, place(): pl.pallas_call(functools.partial(kernel, devices, group, first), out_shap...  3.34 us
    unnamed x12, local copies, waits for them, and re-layouts  2.84 us
  transfers between devices with their start and end apart: 14, of which 11 were waited for; matrix products, arithmetic and copies ran while one was open for 0% of the time, Pallas kernels for 8%

profile of v11, /device:TPU:0, one launch (start us, length us, event | category | flops | bytes accessed | tf_op | source)
XLA Modules:
  0.0 92.1 jit_solution(10754353729834400154)
XLA Ops:
  0.6 3.5 %stage.1 = (bf16[64,128,128]{2,1,0:T(8,128)(2,1)}, bf16[32,128,128]{2,1,0:T(8,128)(2,1)}, s32[48]{0:T(128)}) custom-call(s32[6,8,16]{2,1,0:T(8,128)} %dest_hbm.1, bf16[6,8,128,128]{3,2,1,0:T(8,128)(2,1)} %k_ref.3, bf16[6,8,128,128]{3,2,1,0:T(8,128)(2,1)} %v_ref.3), custom_call_target="tpu_custom_call" | custom-call | flops 1000 | bytes 1000 | tf_op jit(solution)/shard_map/stage/pallas_call | solution.py:332
  4.1 0.0 copy-start.2
  4.1 0.0 copy-start.3
  4.1 0.0 copy-start.4
  4.2 0.0 copy-start.5
  4.2 7.5 %all-to-all-start = ((bf16[64,128,128]{2,1,0:T(8,128)(2,1)}), bf16[64,128,128]{2,1,0:T(8,128)(2,1)S(1)}, u32[]{:S(2)}, u32[]{:S(2)}) async-start(bf16[64,128,128]{2,1,0:T(8,128)(2,1)} %get-tuple-element.40), calls=%async_computation | async-start | bytes 4194304 | tf_op jit(solution)/shard_map/all_to_all | solution.py:329
  11.7 0.0 copy-done.2
  11.7 0.0 copy-done.3
  11.7 0.0 copy-start
  11.8 1.4 %copy-done = bf16[6,8,128,128]{3,2,1,0:T(8,128)(2,1)S(1)} copy-done((bf16[6,8,128,128]{3,2,1,0:T(8,128)(2,1)S(1)}, bf16[6,8,128,128]{3,2,1,0:T(8,128)(2,1)}, u32[]{:S(2)}) %copy-start) | copy-done | bytes 1572888
  13.2 1.4 %copy-done.1 = bf16[6,8,128,128]{3,2,1,0:T(8,128)(2,1)S(1)} copy-done((bf16[6,8,128,128]{3,2,1,0:T(8,128)(2,1)S(1)}, bf16[6,8,128,128]{3,2,1,0:T(8,128)(2,1)}, u32[]{:S(2)}) %copy-start.1) | copy-done | bytes 1572888
  14.6 3.5 %attend.1 = (f32[2,32,128]{2,1,0:T(8,128)S(1)}, f32[2,400,128]{2,1,0:T(8,128)S(1)}, f32[2,400,128]{2,1,0:T(8,128)S(1)}) custom-call(s32[48]{0:T(128)S(1)} %copy-done.4, s32[6]{0:T(128)S(1)} %copy-done.5, s32[6,4,16]{2,1,0:T(4,128)S(1)} %bitcast.3, bf16[4,6,64,128]{3,2,1,0:T(8,128)(2,1)S(1)} %copy-done.2, bf16[6,8,128,128]{3,2,1,0:T(8,128)(2,1)S(1)} %copy-done, ...), custom_call_target="tpu_custom_call" | custom-call | flops 1000 | bytes 1000 | tf_op jit(solution)/shard_map/attend/pallas_call | solution.py:354
  18.0 0.5 collective-permute-start
  18.5 1.4 %collective-permute-done.got = f32[2,400,128]{2,1,0:T(8,128)S(1)} collective-permute-done((f32[2,400,128]{2,1,0:T(8,128)S(1)}, f32[2,400,128]{2,1,0:T(8,128)S(1)}, u32[]{:S(2)}, u32[]{:S(2)}) %collective-permute-start) | collective-permute-done | bytes 409632 | tf_op jit(solution)/shard_map/ppermute | solution.py:372
  19.9 0.4 core.1
  20.3 2.0 %collective-permute-start.1 = (f32[400,128]{1,0:T(8,128)S(1)}, f32[400,128]{1,0:T(8,128)S(1)}, u32[]{:S(2)}, u32[]{:S(2)}) collective-permute-start(f32[400,128]{1,0:T(8,128)S(1)} %get-tuple-element.32), channel_id=1, source_target_pairs={{0,2},{1,3},{2,0},{3,1},{4,6},{5,7},{6,4},{7,5},{8,10},{9,11},{10,... | collective-permute-start | bytes 614408 | tf_op jit(solution)/shard_map/ppermute | solution.py:372
  22.2 13.0 %collective-permute-done.1.got = f32[400,128]{1,0:T(8,128)S(1)} collective-permute-done((f32[400,128]{1,0:T(8,128)S(1)}, f32[400,128]{1,0:T(8,128)S(1)}, u32[]{:S(2)}, u32[]{:S(2)}) %collective-permute-start.1) | collective-permute-done | bytes 204832 | tf_op jit(solution)/shard_map/ppermute | solution.py:372
  35.3 0.3 near.1
  35.5 0.1 collective-permute-start.2
  35.6 13.3 %collective-permute-done.2.got = f32[208,128]{1,0:T(8,128)S(1)} collective-permute-done((f32[208,128]{1,0:T(8,128)S(1)}, f32[208,128]{1,0:T(8,128)S(1)}, u32[]{:S(2)}, u32[]{:S(2)}) %collective-permute-start.2) | collective-permute-done | bytes 106528 | tf_op jit(solution)/shard_map/ppermute | solution.py:372
  48.9 0.2 far.1.block
  49.0 0.1 scale.1
  49.1 0.1 reduce-precision_convert_fusion
  49.2 4.6 %collective-permute-start.3 = (f16[192,128]{1,0:T(8,128)(2,1)S(1)}, f16[192,128]{1,0:T(8,128)(2,1)S(1)}, u32[]{:S(2)}, u32[]{:S(2)}) collective-permute-start(f16[192,128]{1,0:T(8,128)(2,1)S(1)} %get-tuple-element.50), channel_id=1, source_target_pairs={{0,8},{1,9},{2,10},{3,11},{4,12},{5,13},{6,14},{7,15},{8,0},{9,1},... | collective-permute-start | bytes 147464 | tf_op jit(solution)/shard_map/ppermute | solution.py:372
  53.8 0.1 collective-permute-start.4
  53.9 9.4 %collective-permute-done.3 = f16[192,128]{1,0:T(8,128)(2,1)S(1)} collective-permute-done((f16[192,128]{1,0:T(8,128)(2,1)S(1)}, f16[192,128]{1,0:T(8,128)(2,1)S(1)}, u32[]{:S(2)}, u32[]{:S(2)}) %collective-permute-start.3) | collective-permute-done | bytes 49184 | tf_op jit(solution)/shard_map/ppermute | solution.py:372
  63.3 0.1 collective-permute-done.4.got_stats
  63.4 0.0 all-to-all-done.got
  63.4 3.7 %all-to-all-start.1 = ((bf16[32,128,128]{2,1,0:T(8,128)(2,1)}), bf16[32,128,128]{2,1,0:T(8,128)(2,1)S(1)}, u32[]{:S(2)}, u32[]{:S(2)}) async-start(bf16[32,128,128]{2,1,0:T(8,128)(2,1)} %get-tuple-element.45), calls=%async_computation.1 | async-start | bytes 2097152 | tf_op jit(solution)/shard_map/all_to_all | solution.py:329
  67.1 0.2 last.1.refs_0_
  67.3 2.0 %collective-permute-start.5 = (bf16[224,128]{1,0:T(8,128)(2,1)S(1)}, bf16[224,128]{1,0:T(8,128)(2,1)S(1)}, u32[]{:S(2)}, u32[]{:S(2)}) collective-permute-start(bf16[224,128]{1,0:T(8,128)(2,1)S(1)} %last.1.refs_0_), channel_id=1, source_target_pairs={{0,4},{1,5},{2,6},{3,7},{4,0},{5,1},{6,2},{7,3},{8,12},{9,13},{10,... | collective-permute-start | bytes 172040 | tf_op jit(solution)/shard_map/ppermute | solution.py:372
  69.3 1.5 %collective-permute-start.6 = (bf16[224,128]{1,0:T(8,128)(2,1)S(1)}, bf16[224,128]{1,0:T(8,128)(2,1)S(1)}, u32[]{:S(2)}, u32[]{:S(2)}) collective-permute-start(bf16[224,128]{1,0:T(8,128)(2,1)S(1)} %last.1.refs_0_), channel_id=1, source_target_pairs={{0,2},{1,3},{2,0},{3,1},{4,6},{5,7},{6,4},{7,5},{8,10},{9,11},{10,... | collective-permute-start | bytes 172040 | tf_op jit(solution)/shard_map/ppermute | solution.py:372
  70.8 0.1 collective-permute-start.7
  70.9 0.0 collective-permute-start.8
  70.9 1.7 %place_keys.1 = bf16[6,8,128,128]{3,2,1,0:T(8,128)(2,1)} custom-call(s32[48]{0:T(128)S(1)} %copy-done.4, bf16[64,128,128]{2,1,0:T(8,128)(2,1)S(1)} %all-to-all-done.got), custom_call_target="tpu_custom_call" | custom-call | flops 1000 | bytes 1000 | tf_op jit(solution)/shard_map/place_keys/pallas_call | solution.py:413
  72.6 14.0 %collective-permute-done.5.refs_1_ = bf16[224,128]{1,0:T(8,128)(2,1)S(1)} collective-permute-done((bf16[224,128]{1,0:T(8,128)(2,1)S(1)}, bf16[224,128]{1,0:T(8,128)(2,1)S(1)}, u32[]{:S(2)}, u32[]{:S(2)}) %collective-permute-start.5) | collective-permute-done | bytes 57376 | tf_op jit(solution)/shard_map/ppermute | solution.py:372
  86.6 0.0 collective-permute-done.6.refs_2_
  86.6 1.0 %collective-permute-done.7.refs_3_ = bf16[224,128]{1,0:T(8,128)(2,1)S(1)} collective-permute-done((bf16[224,128]{1,0:T(8,128)(2,1)S(1)}, bf16[224,128]{1,0:T(8,128)(2,1)S(1)}, u32[]{:S(2)}, u32[]{:S(2)}) %collective-permute-start.7) | collective-permute-done | bytes 57376 | tf_op jit(solution)/shard_map/ppermute | solution.py:372
  87.7 0.0 collective-permute-start.9
  87.7 0.5 collective-permute-start.10
  88.2 0.0 collective-permute-start.11
  88.2 0.0 collective-permute-done.8.refs_4_
  88.2 0.7 collective-permute-done.9.refs_5_
  88.9 0.2 collective-permute-done.10.refs_6_
  89.1 0.4 collective-permute-done.11.refs_7_
  89.4 0.8 finish.1
  90.2 0.2 all-to-all-done.1.got_rest
  90.4 1.7 %place_values.1 = bf16[6,8,128,128]{3,2,1,0:T(8,128)(2,1)} custom-call(s32[48]{0:T(128)S(1)} %copy-done.4, bf16[64,128,128]{2,1,0:T(8,128)(2,1)S(1)} %all-to-all-done.got, bf16[32,128,128]{2,1,0:T(8,128)(2,1)S(1)} %all-to-all-done.1.got_rest), custom_call_target="tpu_custom_call" | custom-call | flops 1000 | bytes 1000 | tf_op jit(solution)/shard_map/place_values/pallas_call | solution.py:413
  (4 shorter events, 0.0 us)
Async XLA Ops:
  4.1 7.6 %copy-start.2 = (bf16[4,6,64,128]{3,2,1,0:T(8,128)(2,1)S(1)}, bf16[4,6,64,128]{3,2,1,0:T(8,128)(2,1)}, u32[]{:S(2)}) copy-start(bf16[4,6,64,128]{3,2,1,0:T(8,128)(2,1)} %q_ref.1) | copy-start | bytes 1179652
  4.1 7.6 %copy-start.3 = (s32[4,6,16]{2,0,1:T(4,128)S(1)}, s32[4,6,16]{2,0,1:T(4,128)}, u32[]{:S(2)}) copy-start(s32[4,6,16]{2,0,1:T(4,128)} %param.10) | copy-start | bytes 4612
  4.1 7.6 %copy-start.4 = (s32[48]{0:T(128)S(1)}, s32[48]{0:T(128)}, u32[]{:S(2)}) copy-start(s32[48]{0:T(128)} %get-tuple-element.27.table) | copy-start | bytes 580
  4.2 7.6 %copy-start.5 = (s32[6]{0:T(128)S(1)}, s32[6]{0:T(128)}, u32[]{:S(2)}) copy-start(s32[6]{0:T(128)} %len_hbm.1) | copy-start | bytes 76
  4.2 59.2 %all-to-all-start = ((bf16[64,128,128]{2,1,0:T(8,128)(2,1)}), bf16[64,128,128]{2,1,0:T(8,128)(2,1)S(1)}, u32[]{:S(2)}, u32[]{:S(2)}) async-start(bf16[64,128,128]{2,1,0:T(8,128)(2,1)} %get-tuple-element.40), calls=%async_computation | async-start | bytes 4194304 | tf_op jit(solution)/shard_map/all_to_all | solution.py:329
  11.7 1.4 %copy-start = (bf16[6,8,128,128]{3,2,1,0:T(8,128)(2,1)S(1)}, bf16[6,8,128,128]{3,2,1,0:T(8,128)(2,1)}, u32[]{:S(2)}) copy-start(bf16[6,8,128,128]{3,2,1,0:T(8,128)(2,1)} %k_ref.3) | copy-start | bytes 4718596
  13.2 1.4 %copy-start.1 = (bf16[6,8,128,128]{3,2,1,0:T(8,128)(2,1)S(1)}, bf16[6,8,128,128]{3,2,1,0:T(8,128)(2,1)}, u32[]{:S(2)}) copy-start(bf16[6,8,128,128]{3,2,1,0:T(8,128)(2,1)} %v_ref.3) | copy-start | bytes 4718596
  18.0 1.8 %collective-permute-start = (f32[2,400,128]{2,1,0:T(8,128)S(1)}, f32[2,400,128]{2,1,0:T(8,128)S(1)}, u32[]{:S(2)}, u32[]{:S(2)}) collective-permute-start(f32[2,400,128]{2,1,0:T(8,128)S(1)} %get-tuple-element.30), channel_id=1, source_target_pairs={{0,1},{1,0},{2,3},{3,2},{4,5},{5,4},{6,7},{7,6},{8,9},{9,8},{10,11... | collective-permute-start | bytes 1228808 | tf_op jit(solution)/shard_map/ppermute | solution.py:372
  20.3 15.0 %collective-permute-start.1 = (f32[400,128]{1,0:T(8,128)S(1)}, f32[400,128]{1,0:T(8,128)S(1)}, u32[]{:S(2)}, u32[]{:S(2)}) collective-permute-start(f32[400,128]{1,0:T(8,128)S(1)} %get-tuple-element.32), channel_id=1, source_target_pairs={{0,2},{1,3},{2,0},{3,1},{4,6},{5,7},{6,4},{7,5},{8,10},{9,11},{10,... | collective-permute-start | bytes 614408 | tf_op jit(solution)/shard_map/ppermute | solution.py:372
  35.5 13.4 %collective-permute-start.2 = (f32[208,128]{1,0:T(8,128)S(1)}, f32[208,128]{1,0:T(8,128)S(1)}, u32[]{:S(2)}, u32[]{:S(2)}) collective-permute-start(f32[208,128]{1,0:T(8,128)S(1)} %get-tuple-element.34), channel_id=1, source_target_pairs={{0,4},{1,5},{2,6},{3,7},{4,0},{5,1},{6,2},{7,3},{8,12},{9,13},{10,... | collective-permute-start | bytes 319496 | tf_op jit(solution)/shard_map/ppermute | solution.py:372
  49.2 14.1 %collective-permute-start.3 = (f16[192,128]{1,0:T(8,128)(2,1)S(1)}, f16[192,128]{1,0:T(8,128)(2,1)S(1)}, u32[]{:S(2)}, u32[]{:S(2)}) collective-permute-start(f16[192,128]{1,0:T(8,128)(2,1)S(1)} %get-tuple-element.50), channel_id=1, source_target_pairs={{0,8},{1,9},{2,10},{3,11},{4,12},{5,13},{6,14},{7,15},{8,0},{9,1},... | collective-permute-start | bytes 147464 | tf_op jit(solution)/shard_map/ppermute | solution.py:372
  53.8 9.6 %collective-permute-start.4 = (f32[24,128]{1,0:T(8,128)S(1)}, f32[24,128]{1,0:T(8,128)S(1)}, u32[]{:S(2)}, u32[]{:S(2)}) collective-permute-start(f32[24,128]{1,0:T(8,128)S(1)} %get-tuple-element.36.own_stats), channel_id=1, source_target_pairs={{0,8},{1,9},{2,10},{3,11},{4,12},{5,13},{6,14},{7,15},{8,0},{9,1},... | collective-permute-start | bytes 36872 | tf_op jit(solution)/shard_map/ppermute | solution.py:372
  63.4 27.0 %all-to-all-start.1 = ((bf16[32,128,128]{2,1,0:T(8,128)(2,1)}), bf16[32,128,128]{2,1,0:T(8,128)(2,1)S(1)}, u32[]{:S(2)}, u32[]{:S(2)}) async-start(bf16[32,128,128]{2,1,0:T(8,128)(2,1)} %get-tuple-element.45), calls=%async_computation.1 | async-start | bytes 2097152 | tf_op jit(solution)/shard_map/all_to_all | solution.py:329
  67.3 19.3 %collective-permute-start.5 = (bf16[224,128]{1,0:T(8,128)(2,1)S(1)}, bf16[224,128]{1,0:T(8,128)(2,1)S(1)}, u32[]{:S(2)}, u32[]{:S(2)}) collective-permute-start(bf16[224,128]{1,0:T(8,128)(2,1)S(1)} %last.1.refs_0_), channel_id=1, source_target_pairs={{0,4},{1,5},{2,6},{3,7},{4,0},{5,1},{6,2},{7,3},{8,12},{9,13},{10,... | collective-permute-start | bytes 172040 | tf_op jit(solution)/shard_map/ppermute | solution.py:372
  69.3 17.3 %collective-permute-start.6 = (bf16[224,128]{1,0:T(8,128)(2,1)S(1)}, bf16[224,128]{1,0:T(8,128)(2,1)S(1)}, u32[]{:S(2)}, u32[]{:S(2)}) collective-permute-start(bf16[224,128]{1,0:T(8,128)(2,1)S(1)} %last.1.refs_0_), channel_id=1, source_target_pairs={{0,2},{1,3},{2,0},{3,1},{4,6},{5,7},{6,4},{7,5},{8,10},{9,11},{10,... | collective-permute-start | bytes 172040 | tf_op jit(solution)/shard_map/ppermute | solution.py:372
  70.8 16.9 %collective-permute-start.7 = (bf16[224,128]{1,0:T(8,128)(2,1)S(1)}, bf16[224,128]{1,0:T(8,128)(2,1)S(1)}, u32[]{:S(2)}, u32[]{:S(2)}) collective-permute-start(bf16[224,128]{1,0:T(8,128)(2,1)S(1)} %last.1.refs_0_), channel_id=1, source_target_pairs={{0,6},{1,7},{2,4},{3,5},{4,2},{5,3},{6,0},{7,1},{8,14},{9,15},{10,... | collective-permute-start | bytes 172040 | tf_op jit(solution)/shard_map/ppermute | solution.py:372
  70.9 17.3 %collective-permute-start.8 = (bf16[224,128]{1,0:T(8,128)(2,1)S(1)}, bf16[224,128]{1,0:T(8,128)(2,1)S(1)}, u32[]{:S(2)}, u32[]{:S(2)}) collective-permute-start(bf16[224,128]{1,0:T(8,128)(2,1)S(1)} %last.1.refs_0_), channel_id=1, source_target_pairs={{0,1},{1,0},{2,3},{3,2},{4,5},{5,4},{6,7},{7,6},{8,9},{9,8},{10,11... | collective-permute-start | bytes 172040 | tf_op jit(solution)/shard_map/ppermute | solution.py:372
  87.7 1.2 %collective-permute-start.9 = (bf16[224,128]{1,0:T(8,128)(2,1)S(1)}, bf16[224,128]{1,0:T(8,128)(2,1)S(1)}, u32[]{:S(2)}, u32[]{:S(2)}) collective-permute-start(bf16[224,128]{1,0:T(8,128)(2,1)S(1)} %collective-permute-done.5.refs_1_), channel_id=1, source_target_pairs={{0,1},{1,0},{2,3},{3,2},{4,5},{5,4},{6,7},{7,6},{8,9},{9,8},{10,11... | collective-permute-start | bytes 172040 | tf_op jit(solution)/shard_map/ppermute | solution.py:372
  87.7 1.4 %collective-permute-start.10 = (bf16[224,128]{1,0:T(8,128)(2,1)S(1)}, bf16[224,128]{1,0:T(8,128)(2,1)S(1)}, u32[]{:S(2)}, u32[]{:S(2)}) collective-permute-start(bf16[224,128]{1,0:T(8,128)(2,1)S(1)} %collective-permute-done.6.refs_2_), channel_id=1, source_target_pairs={{0,1},{1,0},{2,3},{3,2},{4,5},{5,4},{6,7},{7,6},{8,9},{9,8},{10,11... | collective-permute-start | bytes 172040 | tf_op jit(solution)/shard_map/ppermute | solution.py:372
  88.2 1.2 %collective-permute-start.11 = (bf16[224,128]{1,0:T(8,128)(2,1)S(1)}, bf16[224,128]{1,0:T(8,128)(2,1)S(1)}, u32[]{:S(2)}, u32[]{:S(2)}) collective-permute-start(bf16[224,128]{1,0:T(8,128)(2,1)S(1)} %collective-permute-done.7.refs_3_), channel_id=1, source_target_pairs={{0,1},{1,0},{2,3},{3,2},{4,5},{5,4},{6,7},{7,6},{8,9},{9,8},{10,11... | collective-permute-start | bytes 172040 | tf_op jit(solution)/shard_map/ppermute | solution.py:372

commit v12 on v10

--- a/solution.py
+++ b/solution.py
@@ -293,7 +293,13 @@
             at = group + k
             src = got.at[source * first + at] if at < first else got_rest.at[source * rest + at - first]
             put(src, table[offset * group + k], heads, out, sem)
-    pltpu.make_async_copy(out, out, sem).wait()
+
+
+def end_kernel(devices, group, first, pairs, per, levels, table, got, got_rest, stats_ref, *refs):
+    ins, (values, out, mass_ref, mass_vm, sem, place_sem) = refs[:2 * levels], refs[2 * levels:]
+    place_values_kernel(devices, group, first, table, got, got_rest, values, place_sem)
+    finish_kernel(pairs, per, values.shape[1], levels, stats_ref, *ins, out, mass_ref, mass_vm, sem)
+    pltpu.make_async_copy(values, values, place_sem).wait()
 
 
 def put(src, pair, heads, out, sem):
@@ -422,24 +428,28 @@
         )(table, *got)
 
     moved_keys = place(place_keys_kernel, "place_keys", tiles_in)
-    moved_values = place(place_values_kernel, "place_values", tiles_in, rest_in)
     *forward, moved_keys = lax.optimization_barrier((*near[1:], moved_keys))
     near = [message, *forward]
     arrived = near + [flip(x, 1) for x in near]
 
-    attn_out, mass = pl.pallas_call(
-        functools.partial(finish_kernel, pairs, per, heads, levels),
+    moved_values, attn_out, mass = pl.pallas_call(
+        functools.partial(end_kernel, devices, group, first, pairs, per, levels),
         out_shape=[
+            jax.ShapeDtypeStruct(value_cache.shape, BF16),
             jax.ShapeDtypeStruct((steps, 2, share * per, width), BF16),
             jax.ShapeDtypeStruct((rows, 1, heads), F32),
         ],
-        in_specs=[VMEM] * (1 + 2 * levels),
-        out_specs=[HBM, HBM],
-        scratch_shapes=[pltpu.VMEM((rows, 1, heads), F32), pltpu.SemaphoreType.DMA((2 * levels + 1,))],
+        in_specs=[SMEM, ANY, ANY] + [VMEM] * (1 + 2 * levels),
+        out_specs=[HBM, HBM, HBM],
+        scratch_shapes=[
+            pltpu.VMEM((rows, 1, heads), F32),
+            pltpu.SemaphoreType.DMA((2 * levels + 1,)),
+            pltpu.SemaphoreType.DMA,
+        ],
         compiler_params=PARAMS,
         cost_estimate=COST,
-        name="finish",
-    )(stats, *arrived)
+        name="end",
+    )(table, tiles_in, rest_in, stats, *arrived)
     return attn_out.reshape(queries.shape), jnp.transpose(mass, (0, 2, 1)), moved_keys, moved_values
 
 

time: 95 us -> 93.8 us (0.987)
  Pallas kernels: 13.1 us -> 12 us
    pallas_call x2 -> x1, Pallas kernels: 3.34 us -> 1.67 us  [place(): pl.pallas_call(functools.partial(kernel, devices, group, first), out_shap...]
  transfers between devices with their start and end apart: 14 -> 14, of which waited for: 8 -> 8; matrix products, arithmetic and copies ran while one was open for 0% -> 0% of each run, Pallas kernels for 8% -> 7%
where the time goes in v12:
time: 93.8 us; the launch traced here: 92.7 us
  waiting for transfers between devices  54.6 us (58%)
  starting transfers between devices  22.4 us (24%)
  Pallas kernels  12 us (13%)
  local copies, waits for them, and re-layouts  2.84 us (3%)
    ppermute x12, waiting for transfers between devices, flip(): return lax.ppermute(x, 'ctx', [(i, i ^ bit) for i in range(devices)])  52.3 us
    all_to_all x2, starting transfers between devices, exchange(): return lax.all_to_all(x, 'ctx', split_axis=0, concat_axis=0, tiled=True)  11.2 us
    ppermute x12, starting transfers between devices, flip(): return lax.ppermute(x, 'ctx', [(i, i ^ bit) for i in range(devices)])  11.2 us
    pallas_call x1, Pallas kernels, local(): pl.pallas_call(functools.partial(stage_kernel, devices, group, first), ou...  3.48 us
    pallas_call x1, Pallas kernels, local(): pl.pallas_call(functools.partial(attend_kernel, levels), out_shape=[jax.S...  3.46 us
    unnamed x12, local copies, waits for them, and re-layouts  2.84 us
    all_to_all x2, waiting for transfers between devices, exchange(): return lax.all_to_all(x, 'ctx', split_axis=0, concat_axis=0, tiled=True)  2.25 us
    pallas_call x1, Pallas kernels, local(): pl.pallas_call(functools.partial(end_kernel, devices, group, first, pairs...  2.22 us
  transfers between devices with their start and end apart: 14, of which 8 were waited for; matrix products, arithmetic and copies ran while one was open for 0% of the time, Pallas kernels for 7%

profile of v12, /device:TPU:0, one launch (start us, length us, event | category | flops | bytes accessed | tf_op | source)
XLA Modules:
  0.0 92.7 jit_solution(16700325557649733604)
XLA Ops:
  0.6 3.5 %stage.1 = (bf16[64,128,128]{2,1,0:T(8,128)(2,1)}, bf16[32,128,128]{2,1,0:T(8,128)(2,1)}, s32[48]{0:T(128)}) custom-call(s32[6,8,16]{2,1,0:T(8,128)} %dest_hbm.1, bf16[6,8,128,128]{3,2,1,0:T(8,128)(2,1)} %k_ref.3, bf16[6,8,128,128]{3,2,1,0:T(8,128)(2,1)} %v_ref.3), custom_call_target="tpu_custom_call" | custom-call | flops 1000 | bytes 1000 | tf_op jit(solution)/shard_map/stage/pallas_call | solution.py:338
  4.1 0.0 copy-start.2
  4.1 0.0 copy-start.3
  4.1 0.0 copy-start.4
  4.2 0.0 copy-start.5
  4.2 7.5 %all-to-all-start = ((bf16[64,128,128]{2,1,0:T(8,128)(2,1)}), bf16[64,128,128]{2,1,0:T(8,128)(2,1)S(1)}, u32[]{:S(2)}, u32[]{:S(2)}) async-start(bf16[64,128,128]{2,1,0:T(8,128)(2,1)} %get-tuple-element.27), calls=%async_computation | async-start | bytes 4194304 | tf_op jit(solution)/shard_map/all_to_all | solution.py:335
  11.7 0.0 copy-done.2
  11.7 0.0 copy-done.3
  11.7 0.0 copy-done.4
  11.7 0.0 copy-start
  11.8 1.4 %copy-done = bf16[6,8,128,128]{3,2,1,0:T(8,128)(2,1)S(1)} copy-done((bf16[6,8,128,128]{3,2,1,0:T(8,128)(2,1)S(1)}, bf16[6,8,128,128]{3,2,1,0:T(8,128)(2,1)}, u32[]{:S(2)}) %copy-start) | copy-done | bytes 1572888
  13.2 1.4 %copy-done.1 = bf16[6,8,128,128]{3,2,1,0:T(8,128)(2,1)S(1)} copy-done((bf16[6,8,128,128]{3,2,1,0:T(8,128)(2,1)S(1)}, bf16[6,8,128,128]{3,2,1,0:T(8,128)(2,1)}, u32[]{:S(2)}) %copy-start.1) | copy-done | bytes 1572888
  14.6 3.5 %attend.1 = (f32[2,32,128]{2,1,0:T(8,128)S(1)}, f32[2,400,128]{2,1,0:T(8,128)S(1)}, f32[2,400,128]{2,1,0:T(8,128)S(1)}) custom-call(s32[48]{0:T(128)S(1)} %copy-done.4, s32[6]{0:T(128)S(1)} %copy-done.5, s32[6,4,16]{2,1,0:T(4,128)S(1)} %bitcast.3, bf16[4,6,64,128]{3,2,1,0:T(8,128)(2,1)S(1)} %copy-done.2, bf16[6,8,128,128]{3,2,1,0:T(8,128)(2,1)S(1)} %copy-done, ...), custom_call_target="tpu_custom_call" | custom-call | flops 1000 | bytes 1000 | tf_op jit(solution)/shard_map/attend/pallas_call | solution.py:360
  18.0 0.5 collective-permute-start
  18.5 1.4 %collective-permute-done.got = f32[2,400,128]{2,1,0:T(8,128)S(1)} collective-permute-done((f32[2,400,128]{2,1,0:T(8,128)S(1)}, f32[2,400,128]{2,1,0:T(8,128)S(1)}, u32[]{:S(2)}, u32[]{:S(2)}) %collective-permute-start) | collective-permute-done | bytes 409632 | tf_op jit(solution)/shard_map/ppermute | solution.py:378
  19.9 0.4 core.1
  20.3 2.0 %collective-permute-start.1 = (f32[400,128]{1,0:T(8,128)S(1)}, f32[400,128]{1,0:T(8,128)S(1)}, u32[]{:S(2)}, u32[]{:S(2)}) collective-permute-start(f32[400,128]{1,0:T(8,128)S(1)} %get-tuple-element.31), channel_id=1, source_target_pairs={{0,2},{1,3},{2,0},{3,1},{4,6},{5,7},{6,4},{7,5},{8,10},{9,11},{10,... | collective-permute-start | bytes 614408 | tf_op jit(solution)/shard_map/ppermute | solution.py:378
  22.2 13.0 %collective-permute-done.1.got = f32[400,128]{1,0:T(8,128)S(1)} collective-permute-done((f32[400,128]{1,0:T(8,128)S(1)}, f32[400,128]{1,0:T(8,128)S(1)}, u32[]{:S(2)}, u32[]{:S(2)}) %collective-permute-start.1) | collective-permute-done | bytes 204832 | tf_op jit(solution)/shard_map/ppermute | solution.py:378
  35.3 0.3 near.1
  35.5 0.1 collective-permute-start.2
  35.6 13.3 %collective-permute-done.2.got = f32[208,128]{1,0:T(8,128)S(1)} collective-permute-done((f32[208,128]{1,0:T(8,128)S(1)}, f32[208,128]{1,0:T(8,128)S(1)}, u32[]{:S(2)}, u32[]{:S(2)}) %collective-permute-start.2) | collective-permute-done | bytes 106528 | tf_op jit(solution)/shard_map/ppermute | solution.py:378
  48.9 0.2 far.1.block
  49.0 0.1 scale.1
  49.1 0.1 fusion
  49.2 4.6 %collective-permute-start.3 = (f16[192,128]{1,0:T(8,128)(2,1)S(1)}, f16[192,128]{1,0:T(8,128)(2,1)S(1)}, u32[]{:S(2)}, u32[]{:S(2)}) collective-permute-start(f16[192,128]{1,0:T(8,128)(2,1)S(1)} %get-tuple-element.49), channel_id=1, source_target_pairs={{0,8},{1,9},{2,10},{3,11},{4,12},{5,13},{6,14},{7,15},{8,0},{9,1},... | collective-permute-start | bytes 147464 | tf_op jit(solution)/shard_map/ppermute | solution.py:378
  53.8 0.1 collective-permute-start.4
  53.9 9.4 %collective-permute-done.3 = f16[192,128]{1,0:T(8,128)(2,1)S(1)} collective-permute-done((f16[192,128]{1,0:T(8,128)(2,1)S(1)}, f16[192,128]{1,0:T(8,128)(2,1)S(1)}, u32[]{:S(2)}, u32[]{:S(2)}) %collective-permute-start.3) | collective-permute-done | bytes 49184 | tf_op jit(solution)/shard_map/ppermute | solution.py:378
  63.3 0.1 collective-permute-done.4.got_stats
  63.4 0.0 all-to-all-done.got
  63.4 3.7 %all-to-all-start.1 = ((bf16[32,128,128]{2,1,0:T(8,128)(2,1)}), bf16[32,128,128]{2,1,0:T(8,128)(2,1)S(1)}, u32[]{:S(2)}, u32[]{:S(2)}) async-start(bf16[32,128,128]{2,1,0:T(8,128)(2,1)} %get-tuple-element.37), calls=%async_computation.1 | async-start | bytes 2097152 | tf_op jit(solution)/shard_map/all_to_all | solution.py:335
  67.1 0.2 last.1.refs_0_
  67.3 2.9 %collective-permute-start.7 = (bf16[224,128]{1,0:T(8,128)(2,1)S(1)}, bf16[224,128]{1,0:T(8,128)(2,1)S(1)}, u32[]{:S(2)}, u32[]{:S(2)}) collective-permute-start(bf16[224,128]{1,0:T(8,128)(2,1)S(1)} %last.1.refs_0_), channel_id=1, source_target_pairs={{0,6},{1,7},{2,4},{3,5},{4,2},{5,3},{6,0},{7,1},{8,14},{9,15},{10,... | collective-permute-start | bytes 172040 | tf_op jit(solution)/shard_map/ppermute | solution.py:378
  70.2 0.6 collective-permute-start.6
  70.8 0.1 collective-permute-start.5
  70.9 0.0 collective-permute-start.8
  70.9 1.7 %place_keys.1 = bf16[6,8,128,128]{3,2,1,0:T(8,128)(2,1)} custom-call(s32[48]{0:T(128)S(1)} %copy-done.4, bf16[64,128,128]{2,1,0:T(8,128)(2,1)S(1)} %all-to-all-done.got), custom_call_target="tpu_custom_call" | custom-call | flops 1000 | bytes 1000 | tf_op jit(solution)/shard_map/place_keys/pallas_call | solution.py:419
  72.6 14.0 %collective-permute-done.7.refs_3_ = bf16[224,128]{1,0:T(8,128)(2,1)S(1)} collective-permute-done((bf16[224,128]{1,0:T(8,128)(2,1)S(1)}, bf16[224,128]{1,0:T(8,128)(2,1)S(1)}, u32[]{:S(2)}, u32[]{:S(2)}) %collective-permute-start.7) | collective-permute-done | bytes 57376 | tf_op jit(solution)/shard_map/ppermute | solution.py:378
  86.6 0.0 collective-permute-done.6.refs_2_
  86.6 1.0 %collective-permute-done.5.refs_1_ = bf16[224,128]{1,0:T(8,128)(2,1)S(1)} collective-permute-done((bf16[224,128]{1,0:T(8,128)(2,1)S(1)}, bf16[224,128]{1,0:T(8,128)(2,1)S(1)}, u32[]{:S(2)}, u32[]{:S(2)}) %collective-permute-start.5) | collective-permute-done | bytes 57376 | tf_op jit(solution)/shard_map/ppermute | solution.py:378
  87.7 0.0 collective-permute-start.9
  87.7 0.5 collective-permute-start.10
  88.2 0.0 collective-permute-start.11
  88.2 0.0 collective-permute-done.8.refs_4_
  88.2 2.2 %all-to-all-done.1.got_rest = bf16[32,128,128]{2,1,0:T(8,128)(2,1)S(1)} async-done(((bf16[32,128,128]{2,1,0:T(8,128)(2,1)}), bf16[32,128,128]{2,1,0:T(8,128)(2,1)S(1)}, u32[]{:S(2)}, u32[]{:S(2)}) %all-to-all-start.1) | async-done | bytes 1048608 | tf_op jit(solution)/shard_map/all_to_all | solution.py:335
  90.4 0.0 collective-permute-done.9.refs_5_
  90.4 0.0 collective-permute-done.10.refs_6_
  90.4 0.0 collective-permute-done.11.refs_7_
  90.4 2.2 %end.1 = (bf16[6,8,128,128]{3,2,1,0:T(8,128)(2,1)}, bf16[4,2,192,128]{3,2,1,0:T(8,128)(2,1)}, f32[6,1,8]{2,1,0:T(1,128)}) custom-call(s32[48]{0:T(128)S(1)} %copy-done.4, bf16[64,128,128]{2,1,0:T(8,128)(2,1)S(1)} %all-to-all-done.got, bf16[32,128,128]{2,1,0:T(8,128)(2,1)S(1)} %all-to-all-done.1.got_rest, f32[2,32,128]{2,1,0:T(8,128)S(1)} %get-tuple-element.38.stats_ref, ...), custom_call_target="tpu_custom_call" | custom-call | flops 1000 | bytes 1000 | tf_op jit(solution)/shard_map/end/pallas_call | solution.py:435
  (3 shorter events, 0.0 us)
Async XLA Ops:
  4.1 7.6 %copy-start.2 = (bf16[4,6,64,128]{3,2,1,0:T(8,128)(2,1)S(1)}, bf16[4,6,64,128]{3,2,1,0:T(8,128)(2,1)}, u32[]{:S(2)}) copy-start(bf16[4,6,64,128]{3,2,1,0:T(8,128)(2,1)} %q_ref.1) | copy-start | bytes 1179652
  4.1 7.6 %copy-start.3 = (s32[4,6,16]{2,0,1:T(4,128)S(1)}, s32[4,6,16]{2,0,1:T(4,128)}, u32[]{:S(2)}) copy-start(s32[4,6,16]{2,0,1:T(4,128)} %param.10) | copy-start | bytes 4612
  4.1 7.6 %copy-start.4 = (s32[48]{0:T(128)S(1)}, s32[48]{0:T(128)}, u32[]{:S(2)}) copy-start(s32[48]{0:T(128)} %get-tuple-element.26.table) | copy-start | bytes 580
  4.2 7.6 %copy-start.5 = (s32[6]{0:T(128)S(1)}, s32[6]{0:T(128)}, u32[]{:S(2)}) copy-start(s32[6]{0:T(128)} %len_hbm.1) | copy-start | bytes 76
  4.2 59.2 %all-to-all-start = ((bf16[64,128,128]{2,1,0:T(8,128)(2,1)}), bf16[64,128,128]{2,1,0:T(8,128)(2,1)S(1)}, u32[]{:S(2)}, u32[]{:S(2)}) async-start(bf16[64,128,128]{2,1,0:T(8,128)(2,1)} %get-tuple-element.27), calls=%async_computation | async-start | bytes 4194304 | tf_op jit(solution)/shard_map/all_to_all | solution.py:335
  11.7 1.4 %copy-start = (bf16[6,8,128,128]{3,2,1,0:T(8,128)(2,1)S(1)}, bf16[6,8,128,128]{3,2,1,0:T(8,128)(2,1)}, u32[]{:S(2)}) copy-start(bf16[6,8,128,128]{3,2,1,0:T(8,128)(2,1)} %k_ref.3) | copy-start | bytes 4718596
  13.2 1.4 %copy-start.1 = (bf16[6,8,128,128]{3,2,1,0:T(8,128)(2,1)S(1)}, bf16[6,8,128,128]{3,2,1,0:T(8,128)(2,1)}, u32[]{:S(2)}) copy-start(bf16[6,8,128,128]{3,2,1,0:T(8,128)(2,1)} %v_ref.3) | copy-start | bytes 4718596
  18.0 1.8 %collective-permute-start = (f32[2,400,128]{2,1,0:T(8,128)S(1)}, f32[2,400,128]{2,1,0:T(8,128)S(1)}, u32[]{:S(2)}, u32[]{:S(2)}) collective-permute-start(f32[2,400,128]{2,1,0:T(8,128)S(1)} %get-tuple-element.29), channel_id=1, source_target_pairs={{0,1},{1,0},{2,3},{3,2},{4,5},{5,4},{6,7},{7,6},{8,9},{9,8},{10,11... | collective-permute-start | bytes 1228808 | tf_op jit(solution)/shard_map/ppermute | solution.py:378
  20.3 15.0 %collective-permute-start.1 = (f32[400,128]{1,0:T(8,128)S(1)}, f32[400,128]{1,0:T(8,128)S(1)}, u32[]{:S(2)}, u32[]{:S(2)}) collective-permute-start(f32[400,128]{1,0:T(8,128)S(1)} %get-tuple-element.31), channel_id=1, source_target_pairs={{0,2},{1,3},{2,0},{3,1},{4,6},{5,7},{6,4},{7,5},{8,10},{9,11},{10,... | collective-permute-start | bytes 614408 | tf_op jit(solution)/shard_map/ppermute | solution.py:378
  35.5 13.4 %collective-permute-start.2 = (f32[208,128]{1,0:T(8,128)S(1)}, f32[208,128]{1,0:T(8,128)S(1)}, u32[]{:S(2)}, u32[]{:S(2)}) collective-permute-start(f32[208,128]{1,0:T(8,128)S(1)} %get-tuple-element.33), channel_id=1, source_target_pairs={{0,4},{1,5},{2,6},{3,7},{4,0},{5,1},{6,2},{7,3},{8,12},{9,13},{10,... | collective-permute-start | bytes 319496 | tf_op jit(solution)/shard_map/ppermute | solution.py:378
  49.2 14.1 %collective-permute-start.3 = (f16[192,128]{1,0:T(8,128)(2,1)S(1)}, f16[192,128]{1,0:T(8,128)(2,1)S(1)}, u32[]{:S(2)}, u32[]{:S(2)}) collective-permute-start(f16[192,128]{1,0:T(8,128)(2,1)S(1)} %get-tuple-element.49), channel_id=1, source_target_pairs={{0,8},{1,9},{2,10},{3,11},{4,12},{5,13},{6,14},{7,15},{8,0},{9,1},... | collective-permute-start | bytes 147464 | tf_op jit(solution)/shard_map/ppermute | solution.py:378
  53.8 9.6 %collective-permute-start.4 = (f32[24,128]{1,0:T(8,128)S(1)}, f32[24,128]{1,0:T(8,128)S(1)}, u32[]{:S(2)}, u32[]{:S(2)}) collective-permute-start(f32[24,128]{1,0:T(8,128)S(1)} %get-tuple-element.35.own_stats), channel_id=1, source_target_pairs={{0,8},{1,9},{2,10},{3,11},{4,12},{5,13},{6,14},{7,15},{8,0},{9,1},... | collective-permute-start | bytes 36872 | tf_op jit(solution)/shard_map/ppermute | solution.py:378
  63.4 27.0 %all-to-all-start.1 = ((bf16[32,128,128]{2,1,0:T(8,128)(2,1)}), bf16[32,128,128]{2,1,0:T(8,128)(2,1)S(1)}, u32[]{:S(2)}, u32[]{:S(2)}) async-start(bf16[32,128,128]{2,1,0:T(8,128)(2,1)} %get-tuple-element.37), calls=%async_computation.1 | async-start | bytes 2097152 | tf_op jit(solution)/shard_map/all_to_all | solution.py:335
  67.3 19.3 %collective-permute-start.7 = (bf16[224,128]{1,0:T(8,128)(2,1)S(1)}, bf16[224,128]{1,0:T(8,128)(2,1)S(1)}, u32[]{:S(2)}, u32[]{:S(2)}) collective-permute-start(bf16[224,128]{1,0:T(8,128)(2,1)S(1)} %last.1.refs_0_), channel_id=1, source_target_pairs={{0,6},{1,7},{2,4},{3,5},{4,2},{5,3},{6,0},{7,1},{8,14},{9,15},{10,... | collective-permute-start | bytes 172040 | tf_op jit(solution)/shard_map/ppermute | solution.py:378
  70.2 16.4 %collective-permute-start.6 = (bf16[224,128]{1,0:T(8,128)(2,1)S(1)}, bf16[224,128]{1,0:T(8,128)(2,1)S(1)}, u32[]{:S(2)}, u32[]{:S(2)}) collective-permute-start(bf16[224,128]{1,0:T(8,128)(2,1)S(1)} %last.1.refs_0_), channel_id=1, source_target_pairs={{0,2},{1,3},{2,0},{3,1},{4,6},{5,7},{6,4},{7,5},{8,10},{9,11},{10,... | collective-permute-start | bytes 172040 | tf_op jit(solution)/shard_map/ppermute | solution.py:378
  70.8 16.9 %collective-permute-start.5 = (bf16[224,128]{1,0:T(8,128)(2,1)S(1)}, bf16[224,128]{1,0:T(8,128)(2,1)S(1)}, u32[]{:S(2)}, u32[]{:S(2)}) collective-permute-start(bf16[224,128]{1,0:T(8,128)(2,1)S(1)} %last.1.refs_0_), channel_id=1, source_target_pairs={{0,4},{1,5},{2,6},{3,7},{4,0},{5,1},{6,2},{7,3},{8,12},{9,13},{10,... | collective-permute-start | bytes 172040 | tf_op jit(solution)/shard_map/ppermute | solution.py:378
  70.9 17.3 %collective-permute-start.8 = (bf16[224,128]{1,0:T(8,128)(2,1)S(1)}, bf16[224,128]{1,0:T(8,128)(2,1)S(1)}, u32[]{:S(2)}, u32[]{:S(2)}) collective-permute-start(bf16[224,128]{1,0:T(8,128)(2,1)S(1)} %last.1.refs_0_), channel_id=1, source_target_pairs={{0,1},{1,0},{2,3},{3,2},{4,5},{5,4},{6,7},{7,6},{8,9},{9,8},{10,11... | collective-permute-start | bytes 172040 | tf_op jit(solution)/shard_map/ppermute | solution.py:378
  87.7 2.8 %collective-permute-start.9 = (bf16[224,128]{1,0:T(8,128)(2,1)S(1)}, bf16[224,128]{1,0:T(8,128)(2,1)S(1)}, u32[]{:S(2)}, u32[]{:S(2)}) collective-permute-start(bf16[224,128]{1,0:T(8,128)(2,1)S(1)} %collective-permute-done.5.refs_1_), channel_id=1, source_target_pairs={{0,1},{1,0},{2,3},{3,2},{4,5},{5,4},{6,7},{7,6},{8,9},{9,8},{10,11... | collective-permute-start | bytes 172040 | tf_op jit(solution)/shard_map/ppermute | solution.py:378
  87.7 2.8 %collective-permute-start.10 = (bf16[224,128]{1,0:T(8,128)(2,1)S(1)}, bf16[224,128]{1,0:T(8,128)(2,1)}, u32[]{:S(2)}, u32[]{:S(2)}) collective-permute-start(bf16[224,128]{1,0:T(8,128)(2,1)S(1)} %collective-permute-done.6.refs_2_), channel_id=1, source_target_pairs={{0,1},{1,0},{2,3},{3,2},{4,5},{5,4},{6,7},{7,6},{8,9},{9,8},{10,11... | collective-permute-start | bytes 172040 | tf_op jit(solution)/shard_map/ppermute | solution.py:378
  88.2 2.3 %collective-permute-start.11 = (bf16[224,128]{1,0:T(8,128)(2,1)S(1)}, bf16[224,128]{1,0:T(8,128)(2,1)}, u32[]{:S(2)}, u32[]{:S(2)}) collective-permute-start(bf16[224,128]{1,0:T(8,128)(2,1)S(1)} %collective-permute-done.7.refs_3_), channel_id=1, source_target_pairs={{0,1},{1,0},{2,3},{3,2},{4,5},{5,4},{6,7},{7,6},{8,9},{9,8},{10,11... | collective-permute-start | bytes 172040 | tf_op jit(solution)/shard_map/ppermute | solution.py:378

commit v13 on v12

--- a/solution.py
+++ b/solution.py
@@ -67,7 +67,7 @@
                 pltpu.make_async_copy(v_vm.at[row, head], buf_rest.at[at], sem.at[2]).start()
             return carry
 
-        lax.fori_loop(0, heads, send, 0)
+        lax.fori_loop(0, heads, send, 0, unroll=True)
     pltpu.make_async_copy(k_ref, k_vm, sem.at[1]).wait()
     pltpu.make_async_copy(v_ref, v_vm, sem.at[2]).wait()
 

time: 93.8 us -> 93.8 us (level)
  no operation moved by 1% of the time
where the time goes in v13:
time: 93.8 us; the launch traced here: 92.7 us
  waiting for transfers between devices  54.6 us (58%)
  starting transfers between devices  22.4 us (24%)
  Pallas kernels  12 us (13%)
  local copies, waits for them, and re-layouts  2.84 us (3%)
    ppermute x12, waiting for transfers between devices, flip(): return lax.ppermute(x, 'ctx', [(i, i ^ bit) for i in range(devices)])  52.3 us
    all_to_all x2, starting transfers between devices, exchange(): return lax.all_to_all(x, 'ctx', split_axis=0, concat_axis=0, tiled=True)  11.2 us
    ppermute x12, starting transfers between devices, flip(): return lax.ppermute(x, 'ctx', [(i, i ^ bit) for i in range(devices)])  11.2 us
    pallas_call x1, Pallas kernels, local(): pl.pallas_call(functools.partial(stage_kernel, devices, group, first), ou...  3.48 us
    pallas_call x1, Pallas kernels, local(): pl.pallas_call(functools.partial(attend_kernel, levels), out_shape=[jax.S...  3.46 us
    unnamed x12, local copies, waits for them, and re-layouts  2.84 us
    all_to_all x2, waiting for transfers between devices, exchange(): return lax.all_to_all(x, 'ctx', split_axis=0, concat_axis=0, tiled=True)  2.25 us
    pallas_call x1, Pallas kernels, local(): pl.pallas_call(functools.partial(end_kernel, devices, group, first, pairs...  2.22 us
  transfers between devices with their start and end apart: 14, of which 8 were waited for; matrix products, arithmetic and copies ran while one was open for 0% of the time, Pallas kernels for 7%

profile of v13, /device:TPU:0, one launch (start us, length us, event | category | flops | bytes accessed | tf_op | source)
XLA Modules:
  0.0 92.7 jit_solution(3276804335657776286)
XLA Ops:
  0.6 3.5 %stage.1 = (bf16[64,128,128]{2,1,0:T(8,128)(2,1)}, bf16[32,128,128]{2,1,0:T(8,128)(2,1)}, s32[48]{0:T(128)}) custom-call(s32[6,8,16]{2,1,0:T(8,128)} %dest_hbm.1, bf16[6,8,128,128]{3,2,1,0:T(8,128)(2,1)} %k_ref.3, bf16[6,8,128,128]{3,2,1,0:T(8,128)(2,1)} %v_ref.3), custom_call_target="tpu_custom_call" | custom-call | flops 1000 | bytes 1000 | tf_op jit(solution)/shard_map/stage/pallas_call | solution.py:338
  4.1 0.0 copy-start.2
  4.1 0.0 copy-start.3
  4.1 0.0 copy-start.4
  4.2 0.0 copy-start.5
  4.2 7.5 %all-to-all-start = ((bf16[64,128,128]{2,1,0:T(8,128)(2,1)}), bf16[64,128,128]{2,1,0:T(8,128)(2,1)S(1)}, u32[]{:S(2)}, u32[]{:S(2)}) async-start(bf16[64,128,128]{2,1,0:T(8,128)(2,1)} %get-tuple-element.27), calls=%async_computation | async-start | bytes 4194304 | tf_op jit(solution)/shard_map/all_to_all | solution.py:335
  11.7 0.0 copy-done.2
  11.7 0.0 copy-done.3
  11.7 0.0 copy-done.4
  11.7 0.0 copy-start
  11.8 1.4 %copy-done = bf16[6,8,128,128]{3,2,1,0:T(8,128)(2,1)S(1)} copy-done((bf16[6,8,128,128]{3,2,1,0:T(8,128)(2,1)S(1)}, bf16[6,8,128,128]{3,2,1,0:T(8,128)(2,1)}, u32[]{:S(2)}) %copy-start) | copy-done | bytes 1572888
  13.2 1.4 %copy-done.1 = bf16[6,8,128,128]{3,2,1,0:T(8,128)(2,1)S(1)} copy-done((bf16[6,8,128,128]{3,2,1,0:T(8,128)(2,1)S(1)}, bf16[6,8,128,128]{3,2,1,0:T(8,128)(2,1)}, u32[]{:S(2)}) %copy-start.1) | copy-done | bytes 1572888
  14.6 3.5 %attend.1 = (f32[2,32,128]{2,1,0:T(8,128)S(1)}, f32[2,400,128]{2,1,0:T(8,128)S(1)}, f32[2,400,128]{2,1,0:T(8,128)S(1)}) custom-call(s32[48]{0:T(128)S(1)} %copy-done.4, s32[6]{0:T(128)S(1)} %copy-done.5, s32[6,4,16]{2,1,0:T(4,128)S(1)} %bitcast.3, bf16[4,6,64,128]{3,2,1,0:T(8,128)(2,1)S(1)} %copy-done.2, bf16[6,8,128,128]{3,2,1,0:T(8,128)(2,1)S(1)} %copy-done, ...), custom_call_target="tpu_custom_call" | custom-call | flops 1000 | bytes 1000 | tf_op jit(solution)/shard_map/attend/pallas_call | solution.py:360
  18.0 0.5 collective-permute-start
  18.5 1.4 %collective-permute-done.got = f32[2,400,128]{2,1,0:T(8,128)S(1)} collective-permute-done((f32[2,400,128]{2,1,0:T(8,128)S(1)}, f32[2,400,128]{2,1,0:T(8,128)S(1)}, u32[]{:S(2)}, u32[]{:S(2)}) %collective-permute-start) | collective-permute-done | bytes 409632 | tf_op jit(solution)/shard_map/ppermute | solution.py:378
  19.9 0.4 core.1
  20.3 2.0 %collective-permute-start.1 = (f32[400,128]{1,0:T(8,128)S(1)}, f32[400,128]{1,0:T(8,128)S(1)}, u32[]{:S(2)}, u32[]{:S(2)}) collective-permute-start(f32[400,128]{1,0:T(8,128)S(1)} %get-tuple-element.31), channel_id=1, source_target_pairs={{0,2},{1,3},{2,0},{3,1},{4,6},{5,7},{6,4},{7,5},{8,10},{9,11},{10,... | collective-permute-start | bytes 614408 | tf_op jit(solution)/shard_map/ppermute | solution.py:378
  22.2 13.0 %collective-permute-done.1.got = f32[400,128]{1,0:T(8,128)S(1)} collective-permute-done((f32[400,128]{1,0:T(8,128)S(1)}, f32[400,128]{1,0:T(8,128)S(1)}, u32[]{:S(2)}, u32[]{:S(2)}) %collective-permute-start.1) | collective-permute-done | bytes 204832 | tf_op jit(solution)/shard_map/ppermute | solution.py:378
  35.3 0.3 near.1
  35.5 0.1 collective-permute-start.2
  35.6 13.3 %collective-permute-done.2.got = f32[208,128]{1,0:T(8,128)S(1)} collective-permute-done((f32[208,128]{1,0:T(8,128)S(1)}, f32[208,128]{1,0:T(8,128)S(1)}, u32[]{:S(2)}, u32[]{:S(2)}) %collective-permute-start.2) | collective-permute-done | bytes 106528 | tf_op jit(solution)/shard_map/ppermute | solution.py:378
  48.9 0.2 far.1.block
  49.0 0.1 scale.1
  49.1 0.1 fusion
  49.2 4.6 %collective-permute-start.3 = (f16[192,128]{1,0:T(8,128)(2,1)S(1)}, f16[192,128]{1,0:T(8,128)(2,1)S(1)}, u32[]{:S(2)}, u32[]{:S(2)}) collective-permute-start(f16[192,128]{1,0:T(8,128)(2,1)S(1)} %get-tuple-element.49), channel_id=1, source_target_pairs={{0,8},{1,9},{2,10},{3,11},{4,12},{5,13},{6,14},{7,15},{8,0},{9,1},... | collective-permute-start | bytes 147464 | tf_op jit(solution)/shard_map/ppermute | solution.py:378
  53.8 0.1 collective-permute-start.4
  53.9 9.4 %collective-permute-done.3 = f16[192,128]{1,0:T(8,128)(2,1)S(1)} collective-permute-done((f16[192,128]{1,0:T(8,128)(2,1)S(1)}, f16[192,128]{1,0:T(8,128)(2,1)S(1)}, u32[]{:S(2)}, u32[]{:S(2)}) %collective-permute-start.3) | collective-permute-done | bytes 49184 | tf_op jit(solution)/shard_map/ppermute | solution.py:378
  63.3 0.1 collective-permute-done.4.got_stats
  63.4 0.0 all-to-all-done.got
  63.4 3.7 %all-to-all-start.1 = ((bf16[32,128,128]{2,1,0:T(8,128)(2,1)}), bf16[32,128,128]{2,1,0:T(8,128)(2,1)S(1)}, u32[]{:S(2)}, u32[]{:S(2)}) async-start(bf16[32,128,128]{2,1,0:T(8,128)(2,1)} %get-tuple-element.37), calls=%async_computation.1 | async-start | bytes 2097152 | tf_op jit(solution)/shard_map/all_to_all | solution.py:335
  67.1 0.2 last.1.refs_0_
  67.3 2.9 %collective-permute-start.7 = (bf16[224,128]{1,0:T(8,128)(2,1)S(1)}, bf16[224,128]{1,0:T(8,128)(2,1)S(1)}, u32[]{:S(2)}, u32[]{:S(2)}) collective-permute-start(bf16[224,128]{1,0:T(8,128)(2,1)S(1)} %last.1.refs_0_), channel_id=1, source_target_pairs={{0,6},{1,7},{2,4},{3,5},{4,2},{5,3},{6,0},{7,1},{8,14},{9,15},{10,... | collective-permute-start | bytes 172040 | tf_op jit(solution)/shard_map/ppermute | solution.py:378
  70.2 0.6 collective-permute-start.6
  70.8 0.1 collective-permute-start.5
  70.9 0.0 collective-permute-start.8
  70.9 1.7 %place_keys.1 = bf16[6,8,128,128]{3,2,1,0:T(8,128)(2,1)} custom-call(s32[48]{0:T(128)S(1)} %copy-done.4, bf16[64,128,128]{2,1,0:T(8,128)(2,1)S(1)} %all-to-all-done.got), custom_call_target="tpu_custom_call" | custom-call | flops 1000 | bytes 1000 | tf_op jit(solution)/shard_map/place_keys/pallas_call | solution.py:419
  72.6 14.0 %collective-permute-done.7.refs_3_ = bf16[224,128]{1,0:T(8,128)(2,1)S(1)} collective-permute-done((bf16[224,128]{1,0:T(8,128)(2,1)S(1)}, bf16[224,128]{1,0:T(8,128)(2,1)S(1)}, u32[]{:S(2)}, u32[]{:S(2)}) %collective-permute-start.7) | collective-permute-done | bytes 57376 | tf_op jit(solution)/shard_map/ppermute | solution.py:378
  86.6 0.0 collective-permute-done.6.refs_2_
  86.6 1.0 %collective-permute-done.5.refs_1_ = bf16[224,128]{1,0:T(8,128)(2,1)S(1)} collective-permute-done((bf16[224,128]{1,0:T(8,128)(2,1)S(1)}, bf16[224,128]{1,0:T(8,128)(2,1)S(1)}, u32[]{:S(2)}, u32[]{:S(2)}) %collective-permute-start.5) | collective-permute-done | bytes 57376 | tf_op jit(solution)/shard_map/ppermute | solution.py:378
  87.7 0.0 collective-permute-start.9
  87.7 0.5 collective-permute-start.10
  88.2 0.0 collective-permute-start.11
  88.2 0.0 collective-permute-done.8.refs_4_
  88.2 2.2 %all-to-all-done.1.got_rest = bf16[32,128,128]{2,1,0:T(8,128)(2,1)S(1)} async-done(((bf16[32,128,128]{2,1,0:T(8,128)(2,1)}), bf16[32,128,128]{2,1,0:T(8,128)(2,1)S(1)}, u32[]{:S(2)}, u32[]{:S(2)}) %all-to-all-start.1) | async-done | bytes 1048608 | tf_op jit(solution)/shard_map/all_to_all | solution.py:335
  90.4 0.0 collective-permute-done.9.refs_5_
  90.4 0.0 collective-permute-done.10.refs_6_
  90.4 0.0 collective-permute-done.11.refs_7_
  90.4 2.2 %end.1 = (bf16[6,8,128,128]{3,2,1,0:T(8,128)(2,1)}, bf16[4,2,192,128]{3,2,1,0:T(8,128)(2,1)}, f32[6,1,8]{2,1,0:T(1,128)}) custom-call(s32[48]{0:T(128)S(1)} %copy-done.4, bf16[64,128,128]{2,1,0:T(8,128)(2,1)S(1)} %all-to-all-done.got, bf16[32,128,128]{2,1,0:T(8,128)(2,1)S(1)} %all-to-all-done.1.got_rest, f32[2,32,128]{2,1,0:T(8,128)S(1)} %get-tuple-element.38.stats_ref, ...), custom_call_target="tpu_custom_call" | custom-call | flops 1000 | bytes 1000 | tf_op jit(solution)/shard_map/end/pallas_call | solution.py:435
  (3 shorter events, 0.0 us)
Async XLA Ops:
  4.1 7.6 %copy-start.2 = (bf16[4,6,64,128]{3,2,1,0:T(8,128)(2,1)S(1)}, bf16[4,6,64,128]{3,2,1,0:T(8,128)(2,1)}, u32[]{:S(2)}) copy-start(bf16[4,6,64,128]{3,2,1,0:T(8,128)(2,1)} %q_ref.1) | copy-start | bytes 1179652
  4.1 7.6 %copy-start.3 = (s32[4,6,16]{2,0,1:T(4,128)S(1)}, s32[4,6,16]{2,0,1:T(4,128)}, u32[]{:S(2)}) copy-start(s32[4,6,16]{2,0,1:T(4,128)} %param.10) | copy-start | bytes 4612
  4.1 7.6 %copy-start.4 = (s32[48]{0:T(128)S(1)}, s32[48]{0:T(128)}, u32[]{:S(2)}) copy-start(s32[48]{0:T(128)} %get-tuple-element.26.table) | copy-start | bytes 580
  4.2 7.6 %copy-start.5 = (s32[6]{0:T(128)S(1)}, s32[6]{0:T(128)}, u32[]{:S(2)}) copy-start(s32[6]{0:T(128)} %len_hbm.1) | copy-start | bytes 76
  4.2 59.2 %all-to-all-start = ((bf16[64,128,128]{2,1,0:T(8,128)(2,1)}), bf16[64,128,128]{2,1,0:T(8,128)(2,1)S(1)}, u32[]{:S(2)}, u32[]{:S(2)}) async-start(bf16[64,128,128]{2,1,0:T(8,128)(2,1)} %get-tuple-element.27), calls=%async_computation | async-start | bytes 4194304 | tf_op jit(solution)/shard_map/all_to_all | solution.py:335
  11.7 1.4 %copy-start = (bf16[6,8,128,128]{3,2,1,0:T(8,128)(2,1)S(1)}, bf16[6,8,128,128]{3,2,1,0:T(8,128)(2,1)}, u32[]{:S(2)}) copy-start(bf16[6,8,128,128]{3,2,1,0:T(8,128)(2,1)} %k_ref.3) | copy-start | bytes 4718596
  13.2 1.4 %copy-start.1 = (bf16[6,8,128,128]{3,2,1,0:T(8,128)(2,1)S(1)}, bf16[6,8,128,128]{3,2,1,0:T(8,128)(2,1)}, u32[]{:S(2)}) copy-start(bf16[6,8,128,128]{3,2,1,0:T(8,128)(2,1)} %v_ref.3) | copy-start | bytes 4718596
  18.0 1.8 %collective-permute-start = (f32[2,400,128]{2,1,0:T(8,128)S(1)}, f32[2,400,128]{2,1,0:T(8,128)S(1)}, u32[]{:S(2)}, u32[]{:S(2)}) collective-permute-start(f32[2,400,128]{2,1,0:T(8,128)S(1)} %get-tuple-element.29), channel_id=1, source_target_pairs={{0,1},{1,0},{2,3},{3,2},{4,5},{5,4},{6,7},{7,6},{8,9},{9,8},{10,11... | collective-permute-start | bytes 1228808 | tf_op jit(solution)/shard_map/ppermute | solution.py:378
  20.3 15.0 %collective-permute-start.1 = (f32[400,128]{1,0:T(8,128)S(1)}, f32[400,128]{1,0:T(8,128)S(1)}, u32[]{:S(2)}, u32[]{:S(2)}) collective-permute-start(f32[400,128]{1,0:T(8,128)S(1)} %get-tuple-element.31), channel_id=1, source_target_pairs={{0,2},{1,3},{2,0},{3,1},{4,6},{5,7},{6,4},{7,5},{8,10},{9,11},{10,... | collective-permute-start | bytes 614408 | tf_op jit(solution)/shard_map/ppermute | solution.py:378
  35.5 13.4 %collective-permute-start.2 = (f32[208,128]{1,0:T(8,128)S(1)}, f32[208,128]{1,0:T(8,128)S(1)}, u32[]{:S(2)}, u32[]{:S(2)}) collective-permute-start(f32[208,128]{1,0:T(8,128)S(1)} %get-tuple-element.33), channel_id=1, source_target_pairs={{0,4},{1,5},{2,6},{3,7},{4,0},{5,1},{6,2},{7,3},{8,12},{9,13},{10,... | collective-permute-start | bytes 319496 | tf_op jit(solution)/shard_map/ppermute | solution.py:378
  49.2 14.1 %collective-permute-start.3 = (f16[192,128]{1,0:T(8,128)(2,1)S(1)}, f16[192,128]{1,0:T(8,128)(2,1)S(1)}, u32[]{:S(2)}, u32[]{:S(2)}) collective-permute-start(f16[192,128]{1,0:T(8,128)(2,1)S(1)} %get-tuple-element.49), channel_id=1, source_target_pairs={{0,8},{1,9},{2,10},{3,11},{4,12},{5,13},{6,14},{7,15},{8,0},{9,1},... | collective-permute-start | bytes 147464 | tf_op jit(solution)/shard_map/ppermute | solution.py:378
  53.8 9.6 %collective-permute-start.4 = (f32[24,128]{1,0:T(8,128)S(1)}, f32[24,128]{1,0:T(8,128)S(1)}, u32[]{:S(2)}, u32[]{:S(2)}) collective-permute-start(f32[24,128]{1,0:T(8,128)S(1)} %get-tuple-element.35.own_stats), channel_id=1, source_target_pairs={{0,8},{1,9},{2,10},{3,11},{4,12},{5,13},{6,14},{7,15},{8,0},{9,1},... | collective-permute-start | bytes 36872 | tf_op jit(solution)/shard_map/ppermute | solution.py:378
  63.4 27.0 %all-to-all-start.1 = ((bf16[32,128,128]{2,1,0:T(8,128)(2,1)}), bf16[32,128,128]{2,1,0:T(8,128)(2,1)S(1)}, u32[]{:S(2)}, u32[]{:S(2)}) async-start(bf16[32,128,128]{2,1,0:T(8,128)(2,1)} %get-tuple-element.37), calls=%async_computation.1 | async-start | bytes 2097152 | tf_op jit(solution)/shard_map/all_to_all | solution.py:335
  67.3 19.3 %collective-permute-start.7 = (bf16[224,128]{1,0:T(8,128)(2,1)S(1)}, bf16[224,128]{1,0:T(8,128)(2,1)S(1)}, u32[]{:S(2)}, u32[]{:S(2)}) collective-permute-start(bf16[224,128]{1,0:T(8,128)(2,1)S(1)} %last.1.refs_0_), channel_id=1, source_target_pairs={{0,6},{1,7},{2,4},{3,5},{4,2},{5,3},{6,0},{7,1},{8,14},{9,15},{10,... | collective-permute-start | bytes 172040 | tf_op jit(solution)/shard_map/ppermute | solution.py:378
  70.2 16.4 %collective-permute-start.6 = (bf16[224,128]{1,0:T(8,128)(2,1)S(1)}, bf16[224,128]{1,0:T(8,128)(2,1)S(1)}, u32[]{:S(2)}, u32[]{:S(2)}) collective-permute-start(bf16[224,128]{1,0:T(8,128)(2,1)S(1)} %last.1.refs_0_), channel_id=1, source_target_pairs={{0,2},{1,3},{2,0},{3,1},{4,6},{5,7},{6,4},{7,5},{8,10},{9,11},{10,... | collective-permute-start | bytes 172040 | tf_op jit(solution)/shard_map/ppermute | solution.py:378
  70.8 16.9 %collective-permute-start.5 = (bf16[224,128]{1,0:T(8,128)(2,1)S(1)}, bf16[224,128]{1,0:T(8,128)(2,1)S(1)}, u32[]{:S(2)}, u32[]{:S(2)}) collective-permute-start(bf16[224,128]{1,0:T(8,128)(2,1)S(1)} %last.1.refs_0_), channel_id=1, source_target_pairs={{0,4},{1,5},{2,6},{3,7},{4,0},{5,1},{6,2},{7,3},{8,12},{9,13},{10,... | collective-permute-start | bytes 172040 | tf_op jit(solution)/shard_map/ppermute | solution.py:378
  70.9 17.3 %collective-permute-start.8 = (bf16[224,128]{1,0:T(8,128)(2,1)S(1)}, bf16[224,128]{1,0:T(8,128)(2,1)S(1)}, u32[]{:S(2)}, u32[]{:S(2)}) collective-permute-start(bf16[224,128]{1,0:T(8,128)(2,1)S(1)} %last.1.refs_0_), channel_id=1, source_target_pairs={{0,1},{1,0},{2,3},{3,2},{4,5},{5,4},{6,7},{7,6},{8,9},{9,8},{10,11... | collective-permute-start | bytes 172040 | tf_op jit(solution)/shard_map/ppermute | solution.py:378
  87.7 2.8 %collective-permute-start.9 = (bf16[224,128]{1,0:T(8,128)(2,1)S(1)}, bf16[224,128]{1,0:T(8,128)(2,1)S(1)}, u32[]{:S(2)}, u32[]{:S(2)}) collective-permute-start(bf16[224,128]{1,0:T(8,128)(2,1)S(1)} %collective-permute-done.5.refs_1_), channel_id=1, source_target_pairs={{0,1},{1,0},{2,3},{3,2},{4,5},{5,4},{6,7},{7,6},{8,9},{9,8},{10,11... | collective-permute-start | bytes 172040 | tf_op jit(solution)/shard_map/ppermute | solution.py:378
  87.7 2.8 %collective-permute-start.10 = (bf16[224,128]{1,0:T(8,128)(2,1)S(1)}, bf16[224,128]{1,0:T(8,128)(2,1)}, u32[]{:S(2)}, u32[]{:S(2)}) collective-permute-start(bf16[224,128]{1,0:T(8,128)(2,1)S(1)} %collective-permute-done.6.refs_2_), channel_id=1, source_target_pairs={{0,1},{1,0},{2,3},{3,2},{4,5},{5,4},{6,7},{7,6},{8,9},{9,8},{10,11... | collective-permute-start | bytes 172040 | tf_op jit(solution)/shard_map/ppermute | solution.py:378
  88.2 2.3 %collective-permute-start.11 = (bf16[224,128]{1,0:T(8,128)(2,1)S(1)}, bf16[224,128]{1,0:T(8,128)(2,1)}, u32[]{:S(2)}, u32[]{:S(2)}) collective-permute-start(bf16[224,128]{1,0:T(8,128)(2,1)S(1)} %collective-permute-done.7.refs_3_), channel_id=1, source_target_pairs={{0,1},{1,0},{2,3},{3,2},{4,5},{5,4},{6,7},{7,6},{8,9},{9,8},{10,11... | collective-permute-start | bytes 172040 | tf_op jit(solution)/shard_map/ppermute | solution.py:378
